TPU v7x, 128 devices: a whole 4x4x4 slice. The times are simulated.
128 devices in a mesh: dp: 32 (over y, x, core), mp: 4 (over z).
Axes of the slice: x: 4, y: 4, z: 4, core: 2. Of those that a mesh axis runs over, the one named last changes fastest.
Arguments:
- sparse_ids: int32 [65536, 26], P(('dp', 'mp')), may hold values from 0 to 524287, as said below
- dense_feats: float32 [65536, 13], P(('dp', 'mp')), may hold values from -6 to 6
- labels: int32 [65536, 2], P(('dp', 'mp')), may hold values 0 or 1
- tables: float32 [26, 524288, 16], P(None, ('dp', 'mp')), may hold values from -6 to 6
- dense_w: float32 [13, 96], replicated, may hold values from -1.75 to 1.75
- dense_b: float32 [96], replicated, may hold values from -3 to 3
- w_in: bfloat16 [8, 512, 256], P(None, None, 'mp'), may hold values from -0.25 to 0.25
- b_in: bfloat16 [8, 256], P(None, 'mp'), may hold values from -3 to 3
- w_out: bfloat16 [8, 256, 128], P(None, 'mp'), may hold values from -0.375 to 0.375
- b_out: float32 [8, 128], replicated, may hold values from -3 to 3
- gate_w: float32 [2, 512, 8], replicated, may hold values from -0.125 to 0.125
- gate_b: float32 [2, 8], replicated, may hold values from -0.6 to 0.6
- tower_w1: float32 [2, 128, 64], replicated, may hold values from -0.5 to 0.5
- tower_b1: float32 [2, 64], replicated, may hold values from -3 to 3
- tower_w2: float32 [2, 64], replicated, may hold values from -0.75 to 0.75
- tower_b2: float32 [2], replicated, may hold values from -3 to 3
Outputs:
- grad_tables: float32 [26, 524288, 16], P(None, ('dp', 'mp'))
- grad_dense_w: float32 [13, 96], replicated
- grad_dense_b: float32 [96], replicated
- grad_w_in: float32 [8, 512, 256], P(None, None, 'mp')
- grad_b_in: float32 [8, 256], P(None, 'mp')
- grad_w_out: float32 [8, 256, 128], P(None, 'mp')
- grad_b_out: float32 [8, 128], replicated
- grad_gate_w: float32 [2, 512, 8], replicated
- grad_gate_b: float32 [2, 8], replicated
- grad_tower_w1: float32 [2, 128, 64], replicated
- grad_tower_b1: float32 [2, 64], replicated
- grad_tower_w2: float32 [2, 64], replicated
- grad_tower_b2: float32 [2], replicated
- grad_dense: float32 [65536, 13], P(('dp', 'mp'))
Inputs may be any that keep to these rules, and one draw needn't show every extreme that they name: `sparse_ids`: consider the 512 examples of one device (blocks of rows in the order of dp, then mp) and the table rows of one device (ids in [j * 4096, (j + 1) * 4096)). At most 208 of a device's 13312 ids, over all features, fall in one device's rows; each device sends exactly 208 ids to each of 16 devices and splits the rest as evenly as possible over the others.
All inputs are finite; a program needn't handle non-finite values. No bound on the sum of `labels` on one device may be relied on, other than what follows from the above.
Results may differ from a plain program's by a relative error of at most 0.02.
Values may be sent and summed in bfloat16 or wider, within the bound.
A program may use at most 192 MiB of HBM per device.

v0:
```python
import jax
import jax.numpy as jnp
from jax import lax
from jax.sharding import PartitionSpec as P

exact_prec = lax.Precision.HIGHEST


def smooth(value):
    return jax.nn.gelu(value, approximate=True)


def head_loss(
    inputs, expert_raw, gate_w, gate_b, b_out, tower_w1, tower_b1, tower_w2, tower_b2, label_block
):
    row_count = inputs.shape[0]
    num_experts = gate_w.shape[2]
    logits = jnp.einsum("rd,tdk->rtk", inputs, gate_w, precision=exact_prec) + gate_b[None]
    gate_probs = jax.nn.softmax(logits, axis=-1)
    outputs = expert_raw.reshape(row_count, num_experts, -1) + b_out[None]
    mixture = jnp.einsum("rtk,rko->rto", gate_probs, outputs, precision=exact_prec)
    return tower_loss(mixture, tower_w1, tower_b1, tower_w2, tower_b2, label_block)


def tower_loss(mixture, tower_w1, tower_b1, tower_w2, tower_b2, label_block):
    tower_mid = smooth(
        jnp.einsum("rto,toh->rth", mixture, tower_w1, precision=exact_prec) + tower_b1[None]
    )
    task_logit = (
        jnp.einsum("rth,th->rt", tower_mid, tower_w2, precision=exact_prec) + tower_b2[None]
    )
    return jnp.sum(jax.nn.softplus(task_logit) - label_block.astype(jnp.float32) * task_logit)


def contract_first(left, right):
    return lax.dot_general(
        left, right, (((0,), (0,)), ((), ())), preferred_element_type=jnp.float32
    )


def contract_last(left, right):
    return lax.dot_general(
        left, right, (((1,), (1,)), ((), ())), preferred_element_type=jnp.float32
    )


def packed_pick(packed, index, width):
    per_row = packed.shape[1] // width
    whole = packed[index // per_row].reshape(index.shape[0], per_row, width)
    select = (index % per_row)[:, None] == jnp.arange(per_row, dtype=jnp.int32)[None, :]
    return jnp.sum(jnp.where(select[:, :, None], whole, 0.0), axis=1)


def packed_add(row_total, index, values, per_row):
    width = values.shape[1]
    select = (index % per_row)[:, None] == jnp.arange(per_row, dtype=jnp.int32)[None, :]
    spread = jnp.where(select[:, :, None], values[:, None, :], 0.0).reshape(
        index.shape[0], per_row * width
    )
    return jnp.zeros((row_total, per_row * width), jnp.float32).at[index // per_row].add(spread)


def expert_backward(grouped, hidden, pre_act, d_three, out_weights):
    grp_rows, num_experts, out_width = d_three.shape
    hid_part = out_weights.shape[1]
    in_width = grouped.shape[1]
    grad_w_out = jnp.einsum(
        "rkh,rko->kho",
        hidden.reshape(grp_rows, num_experts, hid_part),
        d_three,
        preferred_element_type=jnp.float32,
    )
    d_hidden = jnp.einsum(
        "rko,kho->rkh", d_three, out_weights, preferred_element_type=jnp.float32
    ).reshape(grp_rows, -1)
    unused, smooth_pull = jax.vjp(smooth, pre_act)
    d_pre = smooth_pull(d_hidden)[0].astype(jnp.bfloat16)
    grad_b_in = jnp.sum(d_pre, axis=0, dtype=jnp.float32).reshape(num_experts, hid_part)
    grad_w_in = (
        contract_first(grouped, d_pre).reshape(in_width, num_experts, hid_part).transpose(1, 0, 2)
    )
    return (grad_w_out, d_pre, grad_b_in, grad_w_in)


def body(
    sparse_ids,
    dense_feats,
    labels,
    tables,
    dense_w,
    dense_b,
    w_in,
    b_in,
    w_out,
    b_out,
    gate_w,
    gate_b,
    tower_w1,
    tower_b1,
    tower_w2,
    tower_b2,
):
    owners = lax.axis_size(("dp", "mp"))
    rows_loc, fields = sparse_ids.shape
    rows_dev = tables.shape[1]
    emb_width = tables.shape[2]
    per_row = max(1, 128 // emb_width)
    lookups = rows_loc * fields
    slots_per = 2 * (lookups // owners)
    num_experts = w_in.shape[0]
    in_width = w_in.shape[1]
    out_width = w_out.shape[2]
    flat_ids = sparse_ids.reshape(-1)
    owner_of = flat_ids // rows_dev
    sort_order = jnp.argsort(owner_of, stable=True)
    sorted_owner = owner_of[sort_order]
    counts = jnp.sum(
        (owner_of[:, None] == jnp.arange(owners, dtype=jnp.int32)[None, :]).astype(jnp.int32),
        axis=0,
    )
    starts = jnp.cumsum(counts) - counts
    rank_in = jnp.arange(lookups, dtype=jnp.int32) - starts[sorted_owner]
    position = (
        jnp.zeros((lookups,), jnp.int32).at[sort_order].set(sorted_owner * slots_per + rank_in)
    )
    field_of = jnp.arange(lookups, dtype=jnp.int32) % fields
    packed = field_of * rows_dev + flat_ids - owner_of * rows_dev
    requests = (
        jnp.full((owners * slots_per,), -1, jnp.int32)
        .at[position]
        .set(packed)
        .reshape(owners, slots_per)
    )
    packed_tables = tables.reshape(-1, per_row * emb_width)
    received = lax.all_to_all(requests, ("dp", "mp"), split_axis=0, concat_axis=0, tiled=True)
    flat_received = received.reshape(-1)
    is_live = flat_received >= 0
    safe_ids = jnp.maximum(flat_received, 0)
    found_rows = packed_pick(packed_tables, safe_ids, emb_width)
    found_rows = jnp.where(is_live[:, None], found_rows, 0.0)
    answer = lax.all_to_all(
        found_rows.reshape(owners, -1).astype(jnp.bfloat16),
        ("dp", "mp"),
        split_axis=0,
        concat_axis=0,
        tiled=True,
    ).astype(jnp.float32)
    embedded = packed_pick(answer.reshape(-1, per_row * emb_width), position, emb_width).reshape(
        rows_loc, fields * emb_width
    )
    projected = jnp.dot(dense_feats, dense_w, precision=exact_prec) + dense_b[None]
    inputs_low = jnp.concatenate([embedded, projected], axis=1).astype(jnp.bfloat16)
    inputs_wide = inputs_low.astype(jnp.float32)

    def head_grads_of(raw_value):

        def local_head(
            inputs32,
            raw_in,
            gate_weight,
            gate_bias,
            bias_out,
            tower_in,
            tower_bias,
            tower_last,
            tower_shift,
        ):
            return head_loss(
                inputs32,
                raw_in,
                gate_weight,
                gate_bias,
                bias_out,
                tower_in,
                tower_bias,
                tower_last,
                tower_shift,
                labels,
            )

        loss_value, pullback = jax.vjp(
            local_head,
            inputs_wide,
            raw_value,
            gate_w,
            gate_b,
            b_out,
            tower_w1,
            tower_b1,
            tower_w2,
            tower_b2,
        )
        return pullback(jnp.ones_like(loss_value))

    grouped = lax.all_gather(inputs_low, "mp", axis=0, tiled=True)
    grp_rows = grouped.shape[0]
    hid_part = w_in.shape[2]
    weight_in = w_in.transpose(1, 0, 2).reshape(in_width, -1)
    pre_act = (
        jnp.dot(grouped, weight_in, preferred_element_type=jnp.float32)
        + b_in.reshape(-1).astype(jnp.float32)[None]
    )
    hidden = smooth(pre_act).astype(jnp.bfloat16)
    row_count = lax.axis_size("mp") * rows_loc
    row_piece = hidden.reshape(row_count, num_experts, hid_part)
    expert_raw = lax.psum_scatter(
        jnp.einsum("rkh,kho->rko", row_piece, w_out, preferred_element_type=jnp.float32).reshape(
            row_count, -1
        ),
        "mp",
        scatter_dimension=0,
        tiled=True,
    )
    (
        d_gate_in,
        d_raw,
        grad_gate_w,
        grad_gate_b,
        grad_b_out,
        grad_tower_w1,
        grad_tower_b1,
        grad_tower_w2,
        grad_tower_b2,
    ) = head_grads_of(expert_raw)
    d_grouped = lax.all_gather(d_raw.astype(jnp.bfloat16), "mp", axis=0, tiled=True)
    d_three = d_grouped.reshape(grp_rows, num_experts, out_width)
    grad_w_out, d_pre, grad_b_in, grad_w_in = expert_backward(
        grouped, hidden, pre_act, d_three, w_out
    )
    row_piece = d_pre
    d_inputs_exp = lax.psum_scatter(
        contract_last(row_piece, weight_in), "mp", scatter_dimension=0, tiled=True
    )
    grad_w_in, grad_b_in, grad_w_out = (
        lax.psum(grad_w_in.astype(jnp.bfloat16), "dp").astype(jnp.float32),
        lax.psum(grad_b_in.astype(jnp.bfloat16), "dp").astype(jnp.float32),
        lax.psum(grad_w_out.astype(jnp.bfloat16), "dp").astype(jnp.float32),
    )
    d_inputs = d_inputs_exp + d_gate_in
    emb_cols = fields * emb_width
    d_embedded = d_inputs[:, :emb_cols]
    d_projected = d_inputs[:, emb_cols:]
    grad_dense_w = jnp.dot(dense_feats.T, d_projected, precision=exact_prec)
    grad_dense_b = jnp.sum(d_projected, axis=0)
    grad_dense = jnp.dot(d_projected, dense_w.T, precision=exact_prec)
    summed = lax.psum(
        (
            grad_gate_w,
            grad_gate_b,
            grad_b_out,
            grad_tower_w1,
            grad_tower_b1,
            grad_tower_w2,
            grad_tower_b2,
            grad_dense_w,
            grad_dense_b,
        ),
        ("dp", "mp"),
    )
    (
        grad_gate_w,
        grad_gate_b,
        grad_b_out,
        grad_tower_w1,
        grad_tower_b1,
        grad_tower_w2,
        grad_tower_b2,
        grad_dense_w,
        grad_dense_b,
    ) = summed
    outgoing = packed_add(
        owners * slots_per // per_row, position, d_embedded.reshape(lookups, emb_width), per_row
    ).reshape(owners, -1)
    incoming = lax.all_to_all(
        outgoing, ("dp", "mp"), split_axis=0, concat_axis=0, tiled=True
    ).reshape(-1, emb_width)
    served_flat = received.reshape(-1)
    is_served = served_flat >= 0
    safe_served = jnp.maximum(served_flat, 0)
    table_total = fields * rows_dev // per_row
    grad_tables = packed_add(
        table_total, safe_served, jnp.where(is_served[:, None], incoming, 0.0), per_row
    ).reshape(tables.shape)
    return (
        grad_tables,
        grad_dense_w,
        grad_dense_b,
        grad_w_in,
        grad_b_in,
        grad_w_out,
        grad_b_out,
        grad_gate_w,
        grad_gate_b,
        grad_tower_w1,
        grad_tower_b1,
        grad_tower_w2,
        grad_tower_b2,
        grad_dense,
    )


def solution(mesh):
    return jax.shard_map(
        body,
        mesh=mesh,
        in_specs=(
            P(("dp", "mp"), None),
            P(("dp", "mp"), None),
            P(("dp", "mp"), None),
            P(None, ("dp", "mp"), None),
            P(),
            P(),
            P(None, None, "mp"),
            P(None, "mp"),
            P(None, "mp", None),
            P(),
            P(),
            P(),
            P(),
            P(),
            P(),
            P(),
        ),
        out_specs=(
            P(None, ("dp", "mp"), None),
            P(),
            P(),
            P(None, None, "mp"),
            P(None, "mp"),
            P(None, "mp", None),
            P(),
            P(),
            P(),
            P(),
            P(),
            P(),
            P(),
            P(("dp", "mp"), None),
        ),
        check_vma=False,
    )
```

profile of v0, /device:TPU:1, one launch (start us, length us, event | category | flops | bytes accessed | tf_op | source)
XLA Modules:
  0.0 1388.4 jit_solution(994499971661913823)
XLA Ops:
  14.5 9.2 sort.17
  23.7 73.7 %gather_fusion = s32[13312]{0:T(1024)S(1)} fusion(s32[13312]{0:T(1024)S(1)} %get-tuple-element.115, s32[13312]{0:T(1024)S(1)} %get-tuple-element.116), kind=kCustom, calls=%fused_computation | custom fusion | bytes 159744 | tf_op jit(solution)/shard_map/gather | solution.py:116
  97.8 79.1 %gather_fusion.1 = s32[13312]{0:T(1024)S(1)} fusion(s32[128]{0:T(128)S(1)} %sub.51, s32[13312]{0:T(1024)S(1)} %broadcast_clamp_fusion.2), kind=kCustom, calls=%fused_computation.1 | custom fusion | bytes 159744 | tf_op jit(solution)/shard_map/gather | solution.py:122
  176.9 49.2 %scatter_custom_fusion = s32[13312]{0:T(1024)S(1)} fusion(s32[13312]{0:T(1024)S(1)} %get-tuple-element.117, s32[13312]{0:T(1024)S(1)} %subtract_add_fusion, s32[]{:T(128)} %constant.109.clone.1), kind=kCustom, calls=%fused_computation.145 | custom fusion | bytes 53252 | tf_op jit(solution)/shard_map/scatter | solution.py:124
  226.8 49.2 %scatter_custom_fusion.1 = s32[26624]{0:T(1024)S(1)} fusion(s32[13312]{0:T(1024)S(1)} %get-tuple-element.111, s32[13312]{0:T(1024)S(1)} %get-tuple-element.114, s32[]{:T(128)} %constant.108.clone.1), kind=kCustom, calls=%fused_computation.132 | custom fusion | bytes 106500 | tf_op jit(solution)/shard_map/scatter | solution.py:131
  276.9 11.8 all-to-all-start
  288.7 26.6 %copy.171 = f32[26,4096,16]{2,1,0:T(8,128)} copy(f32[26,4096,16]{1,2,0:T(8,128)} %param.19) | data formatting | bytes 13631488 | tf_op args[3]
  315.4 34.0 %reshape.373 = f32[13312,128]{1,0:T(8,128)} reshape(f32[26,4096,16]{2,1,0:T(8,128)} %copy.171) | data formatting | bytes 13631488 | tf_op jit(solution)/shard_map/reshape | solution.py:134
  350.9 91.0 %gather_fusion.2 = f32[26624,128]{1,0:T(8,128)} fusion(f32[13312,128]{1,0:T(8,128)} %reshape.373, s32[26624]{0:T(1024)S(1)} %broadcast_clamp_fusion), kind=kCustom, calls=%fused_computation.2 | custom fusion | bytes 27369472 | tf_op jit(solution)/shard_map/gather | solution.py:49
  442.0 14.4 %copy.172 = f32[26624,128]{0,1:T(8,128)} copy(f32[26624,128]{1,0:T(8,128)} %gather_fusion.2) | data formatting | bytes 27262976 | tf_op jit(solution)/shard_map/gather | solution.py:49
  467.8 7.9 reduce_sum.107
  480.2 9.8 all-to-all-start.1
  491.1 16.3 %all-to-all-done.1 = bf16[128,2,1664]{2,1,0:T(2,128)(2,1)S(1)} async-done(((bf16[128,2,1664]{2,1,0:T(2,128)(2,1)}), bf16[128,2,1664]{2,1,0:T(2,128)(2,1)S(1)}, u32[]{:S(2)}, u32[]{:S(2)}) %all-to-all-start.1) | async-done | bytes 852000 | tf_op jit(solution)/shard_map/all_to_all | solution.py:141
  512.6 44.7 %gather_fusion.3 = f32[13312,128]{1,0:T(8,128)} fusion(f32[3328,128]{1,0:T(8,128)S(1)} %bitcast.192, s32[13312]{0:T(1024)S(1)} %get-tuple-element.112), kind=kCustom, calls=%fused_computation.3 | custom fusion | bytes 13684736 | tf_op jit(solution)/shard_map/gather | solution.py:49
  557.2 8.4 copy.176
  577.6 26.9 %all-gather.3.cloned.1.call-done = bf16[2048,512]{1,0:T(8,128)(2,1)} async-done(((bf16[512,512]{1,0:T(8,128)(2,1)}), bf16[2048,512]{1,0:T(8,128)(2,1)}) %all-gather.3.cloned.1.call-update) | async-done | bytes 2097168 | tf_op jit(solution)/shard_map/all_gather | solution.py:195
  617.2 78.2 %reduce-scatter.3.cloned.1.call-done = f32[512,1024]{0,1:T(8,128)} async-done(((f32[2048,1024]{0,1:T(8,128)}), f32[512,1024]{0,1:T(8,128)}) %reduce-scatter.3.cloned.1.call-update) | async-done | bytes 2097168 | tf_op jit(solution)/shard_map/reduce_scatter | solution.py:206
  713.9 48.1 %all-gather.5.cloned.1.call-done = bf16[2048,1024]{0,1:T(8,128)(2,1)} async-done(((bf16[512,1024]{0,1:T(8,128)(2,1)}), bf16[2048,1024]{0,1:T(8,128)(2,1)}) %all-gather.5.cloned.1.call-update) | async-done | bytes 4194320 | tf_op jit(solution)/shard_map/all_gather | solution.py:225
  788.2 34.3 %reduce-scatter.5.cloned.1.call-done = f32[512,512]{1,0:T(8,128)} async-done(((f32[2048,512]{1,0:T(8,128)}), f32[512,512]{1,0:T(8,128)}) %reduce-scatter.5.cloned.1.call-update) | async-done | bytes 1048592 | tf_op jit(solution)/shard_map/reduce_scatter | solution.py:231
  837.8 8.4 copy.191
  846.1 72.9 %scatter_custom_fusion.2 = f32[3328,128]{1,0:T(8,128)} fusion(s32[13312]{0:T(1024)} %get-tuple-element.113, f32[13312,128]{1,0:T(8,128)} %copy.191, f32[]{:T(128)} %constant.107.clone.1), kind=kCustom, calls=%fused_computation.51 | custom fusion | flops 1703936 | bytes 1704448 | tf_op jit(solution)/shard_map/scatter-add | solution.py:60
  919.0 8.2 all-to-all-start.2
  936.7 68.2 %psum.87 = bf16[8,64]{1,0:T(8,128)(2,1)S(1)} all-reduce(bf16[8,64]{1,0:T(8,128)(2,1)S(1)} %convert_element_type.88), channel_id=1, replica_groups=mesh['dp'=32,'mp'=4] {'dp'}, use_global_device_ids=true, to_apply=%region_19.20 | all-reduce | flops 512 | bytes 2048 | tf_op jit(solution)/shard_map/psum | solution.py:236
  1005.5 32.3 %all-reduce.7.cloned.1.call-done = (bf16[8,512,64]{1,2,0:T(8,128)(2,1)}, bf16[8,64,128]{2,1,0:T(8,128)(2,1)}) async-done(((bf16[8,512,64]{1,2,0:T(8,128)(2,1)}, bf16[8,64,128]{2,1,0:T(8,128)(2,1)}), (bf16[8,512,64]{1,2,0:T(8,128)(2,1)}, bf16[8,64,128]{2,1,0:T(8,128)(2,1)})) %all-reduce.7.cloned.1.call-update) | async-done | bytes 655376 | tf_op jit(solution)/shard_map/psum | solution.py:235
  1042.1 66.3 %all-reduce = (f32[13,96]{1,0:T(8,128)}, f32[96]{0:T(128)}, f32[8,128]{1,0:T(8,128)}, f32[2,512,8]{1,2,0:T(8,128)}, f32[2,8]{1,0:T(2,128)}, /*index=5*/f32[2,64]{1,0:T(2,128)}, f32[2,64]{1,0:T(2,128)}, f32[2]{0:T(128)}) all-reduce(f32[13,96]{1,0:T(8,128)S(1)} %convolution_bitcast_fusion.4, ...), channel_id=1, replica_groups=mesh['dp'=32,'mp'=4] {'dp','mp'}, use_global_device_ids=true, to_apply=%region_14.15 | all-reduce | flops 10834 | bytes 86672 | tf_op jit(solution)/shard_map/psum | solution.py:246
  1114.9 7.0 reshape.383
  1122.0 16.0 %broadcast_select_fusion.1 = f32[26624,16]{1,0:T(8,128)} fusion(f32[26624,16]{1,0:T(8,128)} %reshape.383, pred[26624]{0:T(1024)(128)(4,1)S(1)} %ge.16), kind=kLoop, calls=%fused_computation.10 | loop fusion | flops 425984 | bytes 3434496 | tf_op jit(solution)/shard_map/jit(_where)/select_n | solution.py:282
  1138.0 7.9 copy.193
  1152.4 14.5 %copy.194 = f32[26624,128]{1,0:T(8,128)} copy(f32[26624,128]{0,1:T(8,128)} %bitcast.193) | data formatting | bytes 27262976 | tf_op jit(solution)/shard_map/jit(_where)/select_n | solution.py:57
  1166.8 151.5 %scatter_custom_fusion.3 = f32[13312,128]{1,0:T(8,128)} fusion(s32[26624]{0:T(1024)} %bitcast.210, f32[26624,128]{1,0:T(8,128)} %copy.194, f32[]{:T(128)} %constant.107.clone.1), kind=kCustom, calls=%fused_computation.30 | custom fusion | flops 3407872 | bytes 6816256 | tf_op jit(solution)/shard_map/scatter-add | solution.py:60
  1318.3 30.9 %reshape.384 = f32[26,4096,16]{2,1,0:T(8,128)} reshape(f32[13312,128]{1,0:T(8,128)} %scatter_custom_fusion.3) | data formatting | bytes 13631488 | tf_op jit(solution)/shard_map/reshape | solution.py:283
  1349.2 30.8 %copy.197 = f32[26,4096,16]{1,2,0:T(8,128)} copy(f32[26,4096,16]{2,1,0:T(8,128)} %reshape.384) | data formatting | bytes 13631488
  (175 shorter events, 146.0 us)
Async XLA Ops:
  7.2 597.2 %copy-start = (bf16[8,512,64]{1,2,0:T(8,128)(2,1)S(1)}, bf16[8,512,64]{1,2,0:T(8,128)(2,1)}, u32[]{:S(2)}) copy-start(bf16[8,512,64]{1,2,0:T(8,128)(2,1)} %param.22) | copy-start | bytes 1572868
  276.9 72.5 %all-to-all-start = ((s32[128,1,208]{2,1,0:T(1,128)}), s32[128,1,208]{2,1,0:T(1,128)S(1)}, u32[]{:S(2)}, u32[]{:S(2)}) async-start(s32[128,1,208]{2,1,0:T(1,128)} %all_to_all.21), calls=%async_computation | async-start | bytes 262144 | tf_op jit(solution)/shard_map/all_to_all | solution.py:135
  349.6 126.7 %copy-start.14 = (pred[128,1,208]{0,2,1:T(8,128)(4,1)}, pred[128,1,208]{0,2,1:T(8,128)(4,1)S(1)}, u32[]{:S(2)}) copy-start(pred[128,1,208]{0,2,1:T(8,128)(4,1)S(1)} %get-tuple-element.106) | copy-start | bytes 79876
  350.9 91.1 %copy-start.13 = (s32[26624,1]{0,1:T(1,128)}, s32[26624,1]{0,1:T(1,128)S(1)}, u32[]{:S(2)}) copy-start(s32[26624,1]{0,1:T(1,128)S(1)} %compare_select_fusion) | copy-start | bytes 319492
  476.4 14.1 %copy-start.18 = (f32[512,13]{0,1:T(8,128)S(1)}, f32[512,13]{0,1:T(8,128)}, u32[]{:S(2)}) copy-start(f32[512,13]{0,1:T(8,128)} %param.17) | copy-start | bytes 79876
  476.4 14.1 %copy-start.21 = (f32[13,96]{1,0:T(8,128)S(1)}, f32[13,96]{1,0:T(8,128)}, u32[]{:S(2)}) copy-start(f32[13,96]{1,0:T(8,128)} %param.20) | copy-start | bytes 14980
  476.4 14.1 %copy-start.32 = (f32[96]{0:T(128)S(1)}, f32[96]{0:T(128)}, u32[]{:S(2)}) copy-start(f32[96]{0:T(128)} %param.21) | copy-start | bytes 1156
  480.2 27.1 %all-to-all-start.1 = ((bf16[128,2,1664]{2,1,0:T(2,128)(2,1)}), bf16[128,2,1664]{2,1,0:T(2,128)(2,1)S(1)}, u32[]{:S(2)}, u32[]{:S(2)}) async-start(bf16[128,2,1664]{2,1,0:T(2,128)(2,1)} %reshape.474), calls=%async_computation.1 | async-start | bytes 1703936 | tf_op jit(solution)/shard_map/all_to_all | solution.py:141
  490.0 114.4 %all-gather.3.cloned.1.call-start = ((), (), s32[]{:S(2)}) async-start(), calls=%async_computation.5 | async-start | bytes 2621440 | tf_op jit(solution)/shard_map/all_gather | solution.py:195
  569.3 8.1 copy-start.27
  577.4 118.0 %reduce-scatter.3.cloned.1.call-start = ((), (), s32[]{:S(2)}) async-start(), calls=%async_computation.6 | async-start | bytes 10485760 | tf_op jit(solution)/shard_map/reduce_scatter | solution.py:206
  614.6 82.9 %copy-start.22 = (f32[8,128]{1,0:T(8,128)S(1)}, f32[8,128]{1,0:T(8,128)}, u32[]{:S(2)}) copy-start(f32[8,128]{1,0:T(8,128)} %param.25) | copy-start | bytes 12292
  614.6 87.6 %copy-start.29 = (f32[2,64]{1,0:T(2,128)S(1)}, f32[2,64]{1,0:T(2,128)}, u32[]{:S(2)}) copy-start(f32[2,64]{1,0:T(2,128)} %param.29) | copy-start | bytes 1540
  614.6 147.4 %all-gather.5.cloned.1.call-start = ((), (), s32[]{:S(2)}) async-start(), calls=%async_computation.7 | async-start | bytes 5242880 | tf_op jit(solution)/shard_map/all_gather | solution.py:225
  617.2 86.6 %copy-start.30 = (f32[2,64]{1,0:T(2,128)S(1)}, f32[2,64]{1,0:T(2,128)}, u32[]{:S(2)}) copy-start(f32[2,64]{1,0:T(2,128)} %param.30) | copy-start | bytes 1540
  695.4 8.8 copy-start.25
  695.4 8.8 copy-start.33
  697.5 7.4 copy-start.20
  697.5 8.5 copy-start.7
  702.2 9.3 copy-start.9
  713.9 108.7 %reduce-scatter.5.cloned.1.call-start = ((), (), s32[]{:S(2)}) async-start(), calls=%async_computation.8 | async-start | bytes 5242880 | tf_op jit(solution)/shard_map/reduce_scatter | solution.py:231
  780.5 42.0 %copy-start.17 = (f32[2,512,8]{1,2,0:T(8,128)S(1)}, f32[2,512,8]{1,2,0:T(8,128)}, u32[]{:S(2)}) copy-start(f32[2,512,8]{1,2,0:T(8,128)} %param.26) | copy-start | bytes 98308
  824.8 9.3 copy-start.5
  846.1 81.2 %copy-start.2 = (bf16[2048,512]{0,1:T(8,128)(2,1)S(1)}, bf16[2048,512]{0,1:T(8,128)(2,1)}, u32[]{:S(2)}) copy-start(bf16[2048,512]{0,1:T(8,128)(2,1)} %copy-done.1) | copy-start | bytes 6291460
  919.0 190.4 %all-to-all-start.2 = ((f32[128,1,3328]{2,1,0:T(1,128)}), f32[128,1,3328]{2,1,0:T(1,128)}, u32[]{:S(2)}, u32[]{:S(2)}) async-start(f32[128,1,3328]{2,1,0:T(1,128)} %bitcast.203), calls=%async_computation.4 | async-start | bytes 3407872 | tf_op jit(solution)/shard_map/all_to_all | solution.py:274
  927.3 9.4 copy-start.24
  927.3 110.5 %all-reduce.7.cloned.1.call-start = ((), (), s32[]{:S(2)}) async-start(), calls=%async_computation.10 | async-start | bytes 1310720 | tf_op jit(solution)/shard_map/psum | solution.py:235
  931.0 110.6 %copy-start.6 = (f32[512,512]{1,0:T(8,128)S(1)}, f32[512,512]{1,0:T(8,128)}, u32[]{:S(2)}) copy-start(f32[512,512]{1,0:T(8,128)} %copy-done.5) | copy-start | bytes 3145732
  931.0 110.7 %copy-start.19 = (f32[512,13]{0,1:T(8,128)S(1)}, f32[512,13]{0,1:T(8,128)}, u32[]{:S(2)}) copy-start(f32[512,13]{0,1:T(8,128)} %param.17) | copy-start | bytes 79876
  931.0 111.1 %copy-start.23 = (f32[2,8]{1,0:T(2,128)S(1)}, f32[2,8]{1,0:T(2,128)}, u32[]{:S(2)}) copy-start(f32[2,8]{1,0:T(2,128)} %get-tuple-element.100) | copy-start | bytes 196
  931.0 111.1 %copy-start.26 = (f32[2]{0:T(128)S(1)}, f32[2]{0:T(128)}, u32[]{:S(2)}) copy-start(f32[2]{0:T(128)} %get-tuple-element.98) | copy-start | bytes 28
  931.0 448.9 %all-reduce.5.cloned.1.call-start = ((), (), s32[]{:S(2)}) async-start(), calls=%async_computation.9 | async-start | bytes 131072 | tf_op jit(solution)/shard_map/psum | solution.py:246
  (11 other events, 32.6 us)
Sparse Core Ops, SparseCore 0:
  577.5 26.8 all-gather.2
  614.7 80.6 reduce-scatter.2
  714.0 47.9 all-gather.4
  775.2 47.2 reduce-scatter.4
  932.1 105.6 all-reduce.6
  1043.7 137.4 all-reduce.4
where the time goes:
time: 1410 us; the launch traced here: 1390 us
  local copies, waits for them, and re-layouts  618 us (44%)
  other arithmetic  301 us (21%)
  waiting for transfers between devices  236 us (17%)
  blocking collectives  134 us (10%)
  matrix products  53 us (4%)
  starting transfers between devices  30.6 us (2%)
  between operations  15 us (1%)
    scatter-add x2, other arithmetic, packed_add(): jnp.zeros((row_total, per_row * width), jnp.float32).at[index // per_row]  224 us
    gather x4, local copies, waits for them, and re-layouts, packed_pick(): whole = packed[index // per_row].reshape(index.shape[0], per_row, width)  158 us
    gather x1, local copies, waits for them, and re-layouts, body(): rank_in = jnp.arange(lookups, dtype=jnp.int32) - starts[sorted_owner]  79.1 us
    reduce_scatter x1, waiting for transfers between devices, body(): lax.psum_scatter(jnp.einsum('rkh,kho->rko', row_piece, w_out, preferred_e...  78.2 us
    gather x1, local copies, waits for them, and re-layouts, body(): sorted_owner = owner_of[sort_order]  73.7 us
    psum x1, blocking collectives, body(): lax.psum(grad_b_in.astype(jnp.bfloat16), 'dp').astype(jnp.float32)  68.2 us
    unnamed x75, local copies, waits for them, and re-layouts  66.3 us
    psum x1, blocking collectives, body(): lax.psum((grad_gate_w, grad_gate_b, grad_b_out, grad_tower_w1, grad_tower...  66.3 us
  transfers between devices with their start and end apart: 9, of which 6 were waited for; matrix products, arithmetic and copies ran while one was open for 26% of the time, Pallas kernels for 0%

commit v1 on v0

v1 whole, which is shorter than its diff:
```python
import functools

import jax
import jax.numpy as jnp
from jax import lax
from jax.experimental import pallas as pl
from jax.experimental.pallas import tpu as pltpu
from jax.sharding import PartitionSpec as P

ALL = ("dp", "mp")
EXACT = lax.Precision.HIGHEST
F32 = jnp.float32
BF16 = jnp.bfloat16

OWNERS = 128
FIELDS = 26
EMB = 16
ROWS_LOC = 512
ROWS_DEV = 4096
LOOKUPS = ROWS_LOC * FIELDS
PACKED = FIELDS * ROWS_DEV // 8
CAP = 208
COLD = 96
HOT = 16
SLOTS = 256
GROUPS = SLOTS // 8
EXPERTS = 8
HID = 256
EOUT = 128
TASKS = 2
THID = 64
DIN = 512
DENSE = 13
DPROJ = 96
SMALL = 256
CHUNK = 80

VM = pl.BlockSpec(memory_space=pltpu.VMEM)
SM = pl.BlockSpec(memory_space=pltpu.SMEM)


def params(mib):
    return pltpu.CompilerParams(vmem_limit_bytes=mib * 1024 * 1024)


def shape(dims, dtype):
    return jax.ShapeDtypeStruct(dims, dtype)


def lane_group(rows):
    return lax.broadcasted_iota(jnp.int32, (rows, 128), 1) // EMB


def dot_nt(a, b, precision=None):
    return lax.dot_general(
        a, b, (((1,), (1,)), ((), ())), precision=precision, preferred_element_type=F32
    )


def dot_tn(a, b, precision=None):
    return lax.dot_general(
        a, b, (((0,), (0,)), ((), ())), precision=precision, preferred_element_type=F32
    )


def dot_nn(a, b, precision=None):
    return lax.dot_general(
        a, b, (((1,), (0,)), ((), ())), precision=precision, preferred_element_type=F32
    )


def split3(value):
    high = value.astype(BF16)
    rest = value - high.astype(F32)
    mid = rest.astype(BF16)
    low = (rest - mid.astype(F32)).astype(BF16)
    return high, mid, low


def route_kernel(key_ref, pay_ref, req_ref, src_ref, hot_ref, keys, pays, starts_v, starts, sem):
    keys[pl.ds(0, 104), :] = key_ref[...]
    keys[pl.ds(104, 8), :] = jnp.full((8, 128), 1 << 30, jnp.int32)
    pays[pl.ds(0, 104), :] = pay_ref[...]
    pays[pl.ds(104, 8), :] = jnp.zeros((8, 128), jnp.int32)
    owner_at = lax.broadcasted_iota(jnp.int32, (128, 128), 0)

    def count(step, total):
        rows = keys[pl.ds(pl.multiple_of(step * 8, 8), 8), :] >> 14
        for at in range(8):
            total = total + (rows[at : at + 1, :] < owner_at).astype(jnp.int32)
        return total

    below = lax.fori_loop(0, 13, count, jnp.zeros((128, 128), jnp.int32))
    first = jnp.sum(below.astype(F32).T, axis=0, keepdims=True).astype(jnp.int32)
    starts_v[...] = jnp.broadcast_to(first, (8, 128))
    copy = pltpu.make_async_copy(starts_v, starts, sem)
    copy.start()
    copy.wait()
    for at in range(HOT):
        hot_ref[at] = 0
    lane = lax.broadcasted_iota(jnp.int32, (1, 128), 1)
    turn = (lane % 8) * EMB

    def per_owner(owner, hot_count):
        start = starts[0, owner]
        end = jnp.where(owner == OWNERS - 1, LOOKUPS, starts[0, jnp.minimum(owner + 1, 127)])
        row = start >> 7
        off = start & 127
        back = (128 - off) & 127
        key = [pltpu.roll(keys[pl.ds(row + at, 1), :], back, 1) for at in range(3)]
        pay = [pltpu.roll(pays[pl.ds(row + at, 1), :], back, 1) for at in range(3)]
        for half in range(2):
            here = lane < 128 - off
            seg = jnp.where(here, key[half], key[half + 1])
            load = jnp.where(here, pay[half], pay[half + 1])
            valid = (seg >> 14) == owner
            if half:
                valid = valid & (lane < CAP - 128)
            source = jnp.where(valid, seg & 16383, LOOKUPS)
            wanted = jnp.where(valid, load >> 7, PACKED) * 128 + ((turn - load) & 127)
            src_ref[pl.ds(2 * owner + half, 1), :] = source
            req_ref[pl.ds(2 * owner + half, 1), :] = wanted
        is_hot = (end - start > COLD) & (hot_count < HOT)

        @pl.when(is_hot)
        def _():
            hot_ref[hot_count] = owner

        return hot_count + is_hot.astype(jnp.int32)

    lax.fori_loop(0, OWNERS, per_owner, 0)


def route(keys, pays):
    return pl.pallas_call(
        route_kernel,
        in_specs=[VM, VM],
        out_specs=[VM, VM, SM],
        out_shape=[
            shape((2 * OWNERS, 128), jnp.int32),
            shape((2 * OWNERS, 128), jnp.int32),
            shape((HOT,), jnp.int32),
        ],
        scratch_shapes=[
            pltpu.VMEM((112, 128), jnp.int32),
            pltpu.VMEM((112, 128), jnp.int32),
            pltpu.VMEM((8, 128), jnp.int32),
            pltpu.SMEM((8, 128), jnp.int32),
            pltpu.SemaphoreType.DMA,
        ],
        compiler_params=params(32),
        name="route",
    )(keys, pays)


def pack_kernel(table_ref, out_ref):
    for part in range(4):
        block = jnp.concatenate(
            [table_ref[0, :, pl.ds(part * 1024 + k * 128, 128)] for k in range(8)], axis=0
        )
        out_ref[pl.ds(part * 128, 128), :] = block.T


def pack_tables(tables_t):
    return pl.pallas_call(
        pack_kernel,
        grid=(FIELDS,),
        in_specs=[pl.BlockSpec((1, EMB, ROWS_DEV), lambda f: (f, 0, 0))],
        out_specs=pl.BlockSpec((512, 128), lambda f: (f, 0)),
        out_shape=shape((PACKED + 8, 128), F32),
        compiler_params=params(32),
        name="pack_tables",
    )(tables_t)


def look_up_kernel(ids_ref, table_ref, out_ref, found):
    group = lane_group(1)

    def per_source(source, carry):
        for q in range(CAP // 8):
            total = None
            for g in range(8):
                wanted = ids_ref[source * SLOTS + q * 8 + g]
                row = table_ref[pl.ds(lax.shift_right_logical(wanted, 7), 1), :]
                row = pltpu.roll(row, wanted & 127, 1)
                total = jnp.where(group == g, row, total) if g else row
            found[pl.ds(source * GROUPS + q, 1), :] = total
        return carry

    lax.fori_loop(0, OWNERS, per_source, 0)

    def narrow(step, carry):
        at = pl.ds(pl.multiple_of(step * 512, 512), 512)
        out_ref[at, :] = found[at, :].astype(BF16)
        return carry

    lax.fori_loop(0, OWNERS * GROUPS // 512, narrow, 0)


def look_up(ids, table):
    return pl.pallas_call(
        look_up_kernel,
        in_specs=[SM, VM],
        out_specs=VM,
        out_shape=shape((OWNERS * GROUPS, 128), BF16),
        scratch_shapes=[pltpu.VMEM((OWNERS * GROUPS, 128), F32)],
        compiler_params=params(48),
        name="look_up",
    )(ids, table)


def embed_kernel(src_ref, hot_ref, answer_ref, feats_ref, dw_ref, db_ref, out_ref, wide, rows):
    def widen(step, carry):
        at = pl.ds(pl.multiple_of(step * 512, 512), 512)
        wide[at, :] = answer_ref[at, :].astype(F32)
        return carry

    lax.fori_loop(0, OWNERS * GROUPS // 512, widen, 0)

    def place(owner, first, last):
        for q in range(first, last):
            row = wide[pl.ds(owner * GROUPS + q, 1), :]
            for g in range(8):
                at = src_ref[owner * SLOTS + q * 8 + g]
                rows[pl.ds(at, 1), :] = pltpu.roll(row, 128 - EMB * g, 1) if g else row

    def per_owner(owner, carry):
        place(owner, 0, COLD // 8)
        return carry

    def per_hot(at, carry):
        place(hot_ref[at], COLD // 8, CAP // 8)
        return carry

    lax.fori_loop(0, OWNERS, per_owner, 0)
    lax.fori_loop(0, HOT, per_hot, 0)
    group = lane_group(ROWS_LOC)
    for tile in range(4):
        total = None
        for u in range(min(8, FIELDS - tile * 8)):
            block = rows[pl.ds((tile * 8 + u) * ROWS_LOC, ROWS_LOC), :]
            if u:
                block = pltpu.roll(block, EMB * u, 1)
            total = jnp.where(group == u, block, total) if u else block
        if tile == 3:
            projected = dot_tn(feats_ref[...], dw_ref[...], EXACT) + db_ref[...]
            total = jnp.where(group < 2, total, projected)
        out_ref[:, pl.ds(tile * 128, 128)] = total.astype(BF16)


def embed(src, hot, answer, feats_t, dense_w, dense_b):
    return pl.pallas_call(
        embed_kernel,
        in_specs=[SM, SM, VM, VM, VM, VM],
        out_specs=VM,
        out_shape=shape((ROWS_LOC, DIN), BF16),
        scratch_shapes=[
            pltpu.VMEM((OWNERS * GROUPS, 128), F32),
            pltpu.VMEM((LOOKUPS + 8, 128), F32),
        ],
        compiler_params=params(48),
        name="embed",
    )(src, hot, answer, feats_t, dense_w, dense_b)


C0 = 0.7978845608
C1 = 0.7978845608 * 0.044715


def gelu_both(value):
    square = value * value
    bend = jnp.tanh(value * (C0 + C1 * square))
    half = 0.5 * (1.0 + bend)
    slope = half + 0.5 * value * (1.0 - bend * bend) * (C0 + 3.0 * C1 * square)
    return value * half, slope


def model_kernel(
    x_ref,
    labels_ref,
    feats_ref,
    dw_ref,
    w_in_ref,
    b_in_ref,
    w_out_ref,
    b_out_ref,
    gate_w_ref,
    gate_b_ref,
    w1_ref,
    b1_ref,
    w2_ref,
    b2_ref,
    grads_ref,
    small_ref,
    d_in_ref,
    grad_dense_ref,
    hidden,
    slope,
    outs,
    probs,
    d_raw,
    prod_hi,
    prod_lo,
    mix,
    stage,
):
    x = x_ref[...]
    phase = pl.program_id(0)

    def forward(k, carry):
        pre = dot_nt(x, w_in_ref[k]) + b_in_ref[k].astype(F32)
        act, grad = gelu_both(pre)
        act = act.astype(BF16)
        hidden[k] = act
        slope[k] = grad
        outs[k] = dot_nn(act, w_out_ref[k]) + b_out_ref[k]
        return carry

    def head():
        gate_parts = jnp.concatenate(split3(gate_w_ref[...]), axis=0)
        stage[...] = dot_nt(gate_parts, x)
        logits = stage[0:16] + stage[16:32] + stage[32:48] + gate_b_ref[...]
        logits = logits.reshape(TASKS, EXPERTS, ROWS_LOC)
        gates = jnp.exp(logits - jnp.max(logits, axis=1, keepdims=True))
        gates = gates / jnp.sum(gates, axis=1, keepdims=True)
        gates_t = gates.reshape(TASKS * EXPERTS, ROWS_LOC)
        gate_stack = jnp.concatenate(split3(gates_t), axis=0)
        row_at = lax.broadcasted_iota(jnp.int32, (48, 128), 0) % 16

        def spread(k, carry):
            ones = (row_at == k).astype(F32).astype(BF16)
            probs[k] = dot_tn(gate_stack, ones)
            return carry

        lax.fori_loop(0, TASKS * EXPERTS, spread, 0)

        for t in range(TASKS):
            def add(k, total):
                return total + probs[t * EXPERTS + k] * outs[k]

            mix[:, pl.ds(t * EOUT, EOUT)] = lax.fori_loop(
                1, EXPERTS, add, probs[t * EXPERTS] * outs[0]
            )
        mixture = mix[...]
        zero = jnp.zeros((THID, EOUT), F32)
        w1_bd = jnp.concatenate(
            [
                jnp.concatenate([w1_ref[0], zero], axis=1),
                jnp.concatenate([zero, w1_ref[1]], axis=1),
            ],
            axis=0,
        )
        upper, upper_slope = gelu_both(dot_nt(mixture, w1_bd, EXACT) + b1_ref[...])
        w2_bd = w2_ref[...]
        logit = dot_nt(w2_bd, upper, EXACT) + b2_ref[...]
        d_logit = jax.nn.sigmoid(logit) - labels_ref[...].astype(F32)
        d_pre1 = dot_tn(d_logit, w2_bd, EXACT) * upper_slope
        grad_w2 = dot_nn(d_logit, upper, EXACT)
        grad_b1 = jnp.sum(d_pre1, axis=0, keepdims=True)
        grad_w1 = dot_tn(d_pre1, mixture, EXACT)
        d_mix = dot_nn(d_pre1, w1_bd, EXACT)
        mix[...] = d_mix

        def back_raw(k, carry):
            d_one = mix[:, pl.ds(0, EOUT)]
            d_two = mix[:, pl.ds(EOUT, EOUT)]
            grad = probs[k] * d_one + probs[EXPERTS + k] * d_two
            small_ref[pl.ds(128 + k, 1), :] = jnp.sum(grad, axis=0, keepdims=True)
            d_raw[k] = grad.astype(BF16)
            value = outs[k]
            for t, d_task in enumerate((d_one, d_two)):
                product = value * d_task
                high = product.astype(BF16)
                at = pl.ds(pl.multiple_of((t * EXPERTS + k) * EOUT, EOUT), EOUT)
                prod_hi[:, at] = high
                prod_lo[:, at] = (product - high.astype(F32)).astype(BF16)
            return carry

        lax.fori_loop(0, EXPERTS, back_raw, 0)

        wide = TASKS * EXPERTS * EOUT
        column_gate = lax.broadcasted_iota(jnp.int32, (16, wide), 1) // EOUT
        own_gate = lax.broadcasted_iota(jnp.int32, (16, wide), 0)
        ones = (column_gate == own_gate).astype(F32).astype(BF16)
        stage[0:16] = dot_nt(ones, prod_hi[...])
        stage[16:32] = dot_nt(ones, prod_lo[...])
        d_gates = stage[0:16] + stage[16:32]
        d_gates = d_gates.reshape(TASKS, EXPERTS, ROWS_LOC)
        mean = jnp.sum(d_gates * gates, axis=1, keepdims=True)
        d_logits = (gates * (d_gates - mean)).reshape(16, ROWS_LOC)
        d_parts = jnp.concatenate(split3(d_logits), axis=0)
        stage[...] = dot_nn(d_parts, x)
        grad_gate = stage[0:16] + stage[16:32] + stage[32:48]
        d_in_ref[...] = dot_tn(d_logits, gate_w_ref[...], EXACT)
        small_ref[pl.ds(0, THID), :] = grad_w1[0:THID, 0:EOUT]
        small_ref[pl.ds(THID, THID), :] = grad_w1[THID : 2 * THID, EOUT : 2 * EOUT]
        for tile in range(4):
            small_ref[pl.ds(136 + 16 * tile, 16), :] = grad_gate[:, tile * 128 : tile * 128 + 128]
        small_ref[pl.ds(217, 1), :] = grad_b1
        lane = lax.broadcasted_iota(jnp.int32, (1, 128), 1)
        small_ref[pl.ds(218, 1), :] = jnp.where(lane < THID, grad_w2[0:1], grad_w2[1:2])
        small_ref[pl.ds(219, 1), :] = jnp.zeros((1, 128), F32)
        small_ref[pl.ds(220, 2), :] = jnp.broadcast_to(
            jnp.sum(d_logit, axis=1, keepdims=True), (2, 128)
        )
        small_ref[pl.ds(222, 2), :] = jnp.zeros((2, 128), F32)
        small_ref[pl.ds(224, 16), :] = jnp.broadcast_to(
            jnp.sum(d_logits, axis=1, keepdims=True), (16, 128)
        )

    def backward(k, carry):
        d_out = d_raw[k]
        grad_out = dot_tn(hidden[k], d_out).astype(BF16)
        d_pre = (dot_nt(d_out, w_out_ref[k]) * slope[k]).astype(BF16)
        bias = jnp.sum(d_pre.astype(F32), axis=0, keepdims=True)
        small_ref[pl.ds(240 + 2 * k, 1), :] = bias[:, 0:128]
        small_ref[pl.ds(241 + 2 * k, 1), :] = bias[:, 128:256]
        grad_in = dot_tn(d_pre, x).astype(BF16)
        for part in range(4):
            for block in range(5):
                for piece in range(4):
                    at = block * 64 + piece * 16
                    rows = slice(part * 64 + piece * 16, part * 64 + piece * 16 + 16)
                    if block < 4:
                        value = grad_in[rows, block * 128 : block * 128 + 128]
                    else:
                        value = grad_out[rows, :]
                    grads_ref[4 * k + at // CHUNK, part, pl.ds(at % CHUNK, 16), :] = value
        d_in_ref[...] += dot_nn(d_pre, w_in_ref[k])
        return carry

    def tail():
        d_last = d_in_ref[:, pl.ds(384, 128)]
        small_ref[pl.ds(200, 16), :] = jnp.zeros((16, 128), F32)
        small_ref[pl.ds(200, DENSE), :] = dot_nn(feats_ref[...], d_last, EXACT)
        small_ref[pl.ds(216, 1), :] = jnp.sum(d_last, axis=0, keepdims=True)
        grad_dense_ref[...] = dot_nt(dw_ref[...], d_last, EXACT)

    @pl.when(phase == 0)
    def _():
        lax.fori_loop(0, EXPERTS, forward, 0)

    @pl.when(phase == 1)
    def _():
        head()

    @pl.when(phase == 2)
    def _():
        lax.fori_loop(0, EXPERTS, backward, 0)
        tail()


def model(*operands):
    return pl.pallas_call(
        model_kernel,
        grid=(3,),
        in_specs=[VM] * 14,
        out_specs=[VM] * 4,
        out_shape=[
            shape((32, 4, CHUNK, 128), BF16),
            shape((SMALL, 128), F32),
            shape((ROWS_LOC, DIN), F32),
            shape((DENSE, ROWS_LOC), F32),
        ],
        scratch_shapes=[
            pltpu.VMEM((EXPERTS, ROWS_LOC, HID), BF16),
            pltpu.VMEM((EXPERTS, ROWS_LOC, HID), F32),
            pltpu.VMEM((EXPERTS, ROWS_LOC, EOUT), F32),
            pltpu.VMEM((TASKS * EXPERTS, ROWS_LOC, EOUT), F32),
            pltpu.VMEM((EXPERTS, ROWS_LOC, EOUT), BF16),
            pltpu.VMEM((ROWS_LOC, TASKS * EXPERTS * EOUT), BF16),
            pltpu.VMEM((ROWS_LOC, TASKS * EXPERTS * EOUT), BF16),
            pltpu.VMEM((ROWS_LOC, TASKS * EOUT), F32),
            pltpu.VMEM((48, DIN), F32),
        ],
        compiler_params=params(56),
        name="model",
    )(*operands)


def spread_kernel(src_ref, hot_ref, d_ref, out_ref, wide, rows):
    for field in range(FIELDS):
        block = d_ref[:, pl.ds((field // 8) * 128, 128)]
        if field % 8:
            block = pltpu.roll(block, 128 - EMB * (field % 8), 1)
        rows[pl.ds(field * ROWS_LOC, ROWS_LOC), :] = block
    rows[pl.ds(LOOKUPS, 8), :] = jnp.zeros((8, 128), F32)
    group = lane_group(1)

    def collect(owner, first, last):
        for q in range(first, last):
            total = None
            for g in range(8):
                at = src_ref[owner * SLOTS + q * 8 + g]
                row = rows[pl.ds(at, 1), :]
                total = jnp.where(group == g, pltpu.roll(row, EMB * g, 1), total) if g else row
            wide[pl.ds(owner * GROUPS + q, 1), :] = total

    def per_owner(owner, carry):
        collect(owner, 0, COLD // 8)
        return carry

    def per_hot(at, carry):
        collect(hot_ref[at], COLD // 8, CAP // 8)
        return carry

    lax.fori_loop(0, OWNERS, per_owner, 0)
    lax.fori_loop(0, HOT, per_hot, 0)

    def narrow(step, carry):
        at = pl.ds(pl.multiple_of(step * 512, 512), 512)
        out_ref[at, :] = wide[at, :].astype(BF16)
        return carry

    lax.fori_loop(0, OWNERS * GROUPS // 512, narrow, 0)


def spread_grads(src, hot, d_inputs):
    return pl.pallas_call(
        spread_kernel,
        in_specs=[SM, SM, VM],
        out_specs=VM,
        out_shape=shape((OWNERS * GROUPS, 128), BF16),
        scratch_shapes=[
            pltpu.VMEM((OWNERS * GROUPS, 128), F32),
            pltpu.VMEM((LOOKUPS + 8, 128), F32),
        ],
        compiler_params=params(48),
        name="spread_grads",
    )(src, hot, d_inputs)


PARTS = 4


def scatter_kernel(ids_ref, grads_ref, out_ref, wide, *sums):
    def widen(step, carry):
        at = pl.ds(pl.multiple_of(step * 512, 512), 512)
        wide[at, :] = grads_ref[at, :].astype(F32)
        return carry

    lax.fori_loop(0, OWNERS * GROUPS // 512, widen, 0)

    def clear(step, carry):
        at = pl.ds(pl.multiple_of(step * 512, 512), 512)
        for total in sums:
            total[at, :] = jnp.zeros((512, 128), F32)
        return carry

    lax.fori_loop(0, PACKED // 512, clear, 0)
    group = lane_group(1)

    def per_source(source, carry):
        for q in range(CAP // 8):
            row = wide[pl.ds(source * GROUPS + q, 1), :]
            for g in range(8):
                wanted = ids_ref[source * SLOTS + q * 8 + g]
                part = jnp.where(group == g, row, 0.0)
                part = pltpu.roll(part, (128 - wanted) & 127, 1)
                at = pl.ds(lax.shift_right_logical(wanted, 7), 1)
                total = sums[g % PARTS]
                total[at, :] = total[at, :] + part
        return carry

    lax.fori_loop(0, OWNERS, per_source, 0)

    def write(field, carry):
        for part in range(4):
            at = pl.ds(pl.multiple_of(field * 512 + part * 128, 128), 128)
            block = sums[0][at, :]
            for total in sums[1:]:
                block = block + total[at, :]
            block = block.T
            for k in range(8):
                out_ref[field, :, pl.ds(part * 1024 + k * 128, 128)] = block[16 * k : 16 * k + 16]
        return carry

    lax.fori_loop(0, FIELDS, write, 0)


def scatter_add(ids, grads):
    return pl.pallas_call(
        scatter_kernel,
        in_specs=[SM, VM],
        out_specs=VM,
        out_shape=shape((FIELDS, EMB, ROWS_DEV), F32),
        scratch_shapes=[pltpu.VMEM((OWNERS * GROUPS, 128), F32)]
        + [pltpu.VMEM((PACKED + 8, 128), F32)] * PARTS,
        compiler_params=params(56),
        name="scatter_add",
    )(ids, grads)


def sum_kernel(parts_ref, out_ref):
    total = parts_ref[0].astype(F32)

    def add(at, total):
        return total + parts_ref[at].astype(F32)

    total = lax.fori_loop(1, OWNERS, add, total)
    for at in range(out_ref.shape[0]):
        out_ref[at] = total.astype(out_ref.dtype)


def sum_parts(parts, copies, name):
    return pl.pallas_call(
        sum_kernel,
        in_specs=[VM],
        out_specs=VM,
        out_shape=shape((copies,) + parts.shape[1:], parts.dtype),
        compiler_params=params(32),
        name=name,
    )(parts)


def exchange(value, axes):
    return lax.all_to_all(value, axes, split_axis=0, concat_axis=0, tiled=True)


def body(
    sparse_ids,
    dense_feats,
    labels,
    tables,
    dense_w,
    dense_b,
    w_in,
    b_in,
    w_out,
    b_out,
    gate_w,
    gate_b,
    tower_w1,
    tower_b1,
    tower_w2,
    tower_b2,
):
    part = lax.axis_index("mp")
    w_in_all = lax.all_gather(w_in.transpose(0, 2, 1), "mp", axis=1, tiled=True)
    w_out_all = lax.all_gather(w_out, "mp", axis=1, tiled=True)
    b_in_all = lax.all_gather(b_in, "mp", axis=1, tiled=True)

    ids = sparse_ids.T
    field = lax.broadcasted_iota(jnp.int32, (FIELDS, ROWS_LOC), 0)
    example = lax.broadcasted_iota(jnp.int32, (FIELDS, ROWS_LOC), 1)
    row = ids & (ROWS_DEV - 1)
    packed = field * 512 + (row >> 10) * 128 + (row & 127)
    key = ((ids >> 12) << 14) | (field * ROWS_LOC + example)
    load = (packed << 7) | (((row >> 7) & 7) * EMB)
    keys, loads = lax.sort((key.reshape(-1), load.reshape(-1)), num_keys=1, is_stable=False)
    requests, sources, hot = route(keys.reshape(-1, 128), loads.reshape(-1, 128))
    asked = exchange(requests, ALL).reshape(-1)
    sources = sources.reshape(-1)
    table = pack_tables(tables.transpose(0, 2, 1))
    answer = exchange(look_up(asked, table), ALL)
    feats_t = dense_feats.T
    dense_pad = jnp.pad(dense_w, ((0, 0), (128 - DPROJ, 0)))
    bias_pad = jnp.pad(dense_b, (128 - DPROJ, 0)).reshape(1, 128)
    inputs = embed(sources, hot, answer, feats_t, dense_pad, bias_pad)
    task_at = lax.broadcasted_iota(jnp.int32, (TASKS, TASKS * THID), 1) // THID
    task_row = lax.broadcasted_iota(jnp.int32, (TASKS, TASKS * THID), 0)
    w2_bd = jnp.where(task_at == task_row, tower_w2.reshape(1, -1), 0.0)
    grads, small, d_inputs, grad_dense = model(
        inputs,
        labels.T,
        feats_t,
        dense_pad,
        w_in_all,
        b_in_all.reshape(EXPERTS, 1, HID),
        w_out_all,
        b_out.reshape(EXPERTS, 1, EOUT),
        gate_w.transpose(0, 2, 1).reshape(TASKS * EXPERTS, DIN),
        gate_b.reshape(TASKS * EXPERTS, 1),
        tower_w1.transpose(0, 2, 1),
        tower_b1.reshape(1, TASKS * THID),
        w2_bd,
        tower_b2.reshape(TASKS, 1),
    )
    grads = exchange(grads.reshape(OWNERS, CHUNK, 128), ALL)
    small = exchange(small.reshape(OWNERS, 2, 128), ALL)
    incoming = exchange(spread_grads(sources, hot, d_inputs), ALL)
    grads = exchange(sum_parts(grads, 32, "sum_grads"), "dp")
    small = exchange(sum_parts(small, OWNERS, "sum_small"), ALL).reshape(SMALL, 128)
    grad_tables = scatter_add(asked, incoming).transpose(0, 2, 1)

    grads = grads.reshape(EXPERTS, 5, 64, 128).astype(F32)
    grad_w_in = grads[:, :4].transpose(0, 1, 3, 2).reshape(EXPERTS, DIN, 64)
    grad_w_out = grads[:, 4]
    grad_w1 = small[0:128].reshape(TASKS, THID, EOUT).transpose(0, 2, 1)
    grad_b_out = small[128:136]
    grad_gate_w = small[136:200].reshape(4, TASKS, EXPERTS, 128)
    grad_gate_w = grad_gate_w.transpose(1, 0, 3, 2).reshape(TASKS, DIN, EXPERTS)
    grad_dense_w = small[200 : 200 + DENSE, 128 - DPROJ :]
    grad_dense_b = small[216, 128 - DPROJ :]
    grad_b1 = small[217].reshape(TASKS, THID)
    grad_w2 = small[218].reshape(TASKS, THID)
    grad_b2 = small[220:222, 0]
    grad_gate_b = small[224:240, 0].reshape(TASKS, EXPERTS)
    grad_b_in = small[240:256].reshape(EXPERTS, HID)
    grad_b_in = lax.dynamic_slice(grad_b_in, (0, part * 64), (EXPERTS, 64))
    return (
        grad_tables,
        grad_dense_w,
        grad_dense_b,
        grad_w_in,
        grad_b_in,
        grad_w_out,
        grad_b_out,
        grad_gate_w,
        grad_gate_b,
        grad_w1,
        grad_b1,
        grad_w2,
        grad_b2,
        grad_dense.T,
    )


def solution(mesh):
    return jax.shard_map(
        body,
        mesh=mesh,
        in_specs=(
            P(ALL, None),
            P(ALL, None),
            P(ALL, None),
            P(None, ALL, None),
            P(),
            P(),
            P(None, None, "mp"),
            P(None, "mp"),
            P(None, "mp", None),
            P(),
            P(),
            P(),
            P(),
            P(),
            P(),
            P(),
        ),
        out_specs=(
            P(None, ALL, None),
            P(),
            P(),
            P(None, None, "mp"),
            P(None, "mp"),
            P(None, "mp", None),
            P(),
            P(),
            P(),
            P(),
            P(),
            P(),
            P(),
            P(ALL, None),
        ),
        check_vma=False,
    )
```

time: 1410 us -> 387 us (0.27); the launches traced: 1390 us -> 384 us
  local copies, waits for them, and re-layouts: 618 us -> 20 us
  other arithmetic: 301 us -> 9.96 us
  Pallas kernels: 0 us -> 220 us
  waiting for transfers between devices: 236 us -> 22.1 us
  blocking collectives: 134 us -> 63.3 us
  matrix products: 53 us -> 0 us
    gather x6 -> x0, local copies, waits for them, and re-layouts: 311 us -> none  [the longest x4 158 us: packed_pick(): whole = packed[index // per_row].reshape(index.shape[0], per_row, width)]
    scatter-add x2 -> x0, other arithmetic: 224 us -> none  [packed_add(): jnp.zeros((row_total, per_row * width), jnp.float32).at[index // per_row]]
    pallas_call x0 -> x9, Pallas kernels: none -> 220 us  [the longest x1 72.2 us: scatter_add(): pl.pallas_call(scatter_kernel, in_specs=[SM, VM], out_specs=VM, out_shape...]
    psum x2 -> x0, blocking collectives: 134 us -> none  [the longest x1 68.2 us: body(): lax.psum(grad_b_in.astype(jnp.bfloat16), 'dp').astype(jnp.float32)]
    reduce_scatter x2 -> x0, waiting for transfers between devices: 112 us -> none  [the longest x1 78.2 us: body(): lax.psum_scatter(jnp.einsum('rkh,kho->rko', row_piece, w_out, preferred_e...]
    scatter x2 -> x0, local copies, waits for them, and re-layouts: 98.3 us -> none  [the longest x1 49.2 us: body(): jnp.zeros((lookups,), jnp.int32).at[sort_order]]
    all_gather x2 -> x1, waiting for transfers between devices: 75 us -> 0.01 us  [body(): w_in_all = lax.all_gather(w_in.transpose(0, 2, 1), 'mp', axis=1, tiled=True)]
    reshape x6 -> x8, local copies, waits for them, and re-layouts: 78.4 us -> 3.72 us  [the longest x1 1.11 us: body(): grad_w_in = grads[:, :4].transpose(0, 1, 3, 2).reshape(EXPERTS, DIN, 64)]
  transfers between devices with their start and end apart: 9 -> 6, of which waited for: 6 -> 2; matrix products, arithmetic and copies ran while one was open for 26% -> 5% of each run, Pallas kernels for 0% -> 50%
where the time goes in v1:
time: 387 us; the launch traced here: 384 us
  Pallas kernels  220 us (57%)
  blocking collectives  63.3 us (16%)
  starting transfers between devices  34.2 us (9%)
  waiting for transfers between devices  22.1 us (6%)
  local copies, waits for them, and re-layouts  20 us (5%)
  between operations  14.3 us (4%)
  other arithmetic  9.96 us (3%)
    pallas_call x1, Pallas kernels, scatter_add(): pl.pallas_call(scatter_kernel, in_specs=[SM, VM], out_specs=VM, out_shape...  72.2 us
    pallas_call x1, Pallas kernels, look_up(): pl.pallas_call(look_up_kernel, in_specs=[SM, VM], out_specs=VM, out_shape...  47.9 us
    all_to_all x2, blocking collectives, exchange(): return lax.all_to_all(value, axes, split_axis=0, concat_axis=0, tiled=True)  39.4 us
    all_to_all x5, starting transfers between devices, exchange(): return lax.all_to_all(value, axes, split_axis=0, concat_axis=0, tiled=True)  34.2 us
    pallas_call x1, Pallas kernels, model(): pl.pallas_call(model_kernel, grid=(3,), in_specs=[VM] * 14, out_specs=[VM...  27.7 us
    pallas_call x1, Pallas kernels, spread_grads(): pl.pallas_call(spread_kernel, in_specs=[SM, SM, VM], out_specs=VM, out_sh...  27.2 us
    pallas_call x1, Pallas kernels, embed(): pl.pallas_call(embed_kernel, in_specs=[SM, SM, VM, VM, VM, VM], out_specs...  26.4 us
    all_to_all x5, waiting for transfers between devices, exchange(): return lax.all_to_all(value, axes, split_axis=0, concat_axis=0, tiled=True)  21.4 us
  transfers between devices with their start and end apart: 6, of which 2 were waited for; matrix products, arithmetic and copies ran while one was open for 5% of the time, Pallas kernels for 50%

profile of v1, /device:TPU:1, one launch (start us, length us, event | category | flops | bytes accessed | tf_op | source)
XLA Modules:
  0.0 384.2 jit_solution(4368510382883717649)
XLA Ops:
  7.2 0.7 all-gather.3.cloned.1.call-update
  7.9 0.9 or_bitcast_fusion
  8.9 0.9 bitcast_or_fusion
  9.8 7.4 %sort.15 = (s32[13312]{0:T(1024)S(1)}, s32[13312]{0:T(1024)S(1)}) sort(s32[13312]{0:T(1024)S(1)} %reshape.110, s32[13312]{0:T(1024)S(1)} %reshape.111), dimensions={0}, to_apply=%region_0.0 | sort | flops 186368 | bytes 212992 | tf_op jit(solution)/shard_map/sort | solution.py:650
  17.2 12.1 %route.1 = (s32[256,128]{1,0:T(8,128)}, s32[256,128]{1,0:T(8,128)S(1)}, s32[16]{0:T(128)S(1)}) custom-call(s32[104,128]{1,0:T(8,128)S(1)} %bitcast.76, s32[104,128]{1,0:T(8,128)S(1)} %bitcast.77), custom_call_target="tpu_custom_call" | custom-call | tf_op jit(solution)/shard_map/route/pallas_call | solution.py:135
  29.3 11.5 %all-to-all-start = ((s32[128,2,128]{2,1,0:T(2,128)}), s32[128,2,128]{2,1,0:T(2,128)S(1)}, u32[]{:S(2)}, u32[]{:S(2)}) async-start(s32[128,2,128]{2,1,0:T(2,128)} %bitcast.4), calls=%async_computation | async-start | bytes 262144 | tf_op jit(solution)/shard_map/all_to_all | solution.py:617
  40.9 2.9 copy-done.1
  43.8 4.4 %pack_tables.1.table_ref = f32[13320,128]{1,0:T(8,128)S(1)} custom-call(f32[26,16,4096]{2,1,0:T(8,128)S(1)} %bitcast.67), custom_call_target="tpu_custom_call" | custom-call | tf_op jit(solution)/shard_map/pack_tables/pallas_call | solution.py:165
  48.2 2.8 copy-done
  51.1 47.9 %look_up.1 = bf16[4096,128]{1,0:T(8,128)(2,1)} custom-call(s32[32768]{0:T(1024)S(1)} %bitcast.70, f32[13320,128]{1,0:T(8,128)} %copy-done), custom_call_target="tpu_custom_call" | custom-call | tf_op jit(solution)/shard_map/look_up/pallas_call | solution.py:201
  99.0 9.8 %all-to-all-start.1 = ((bf16[128,32,128]{2,1,0:T(8,128)(2,1)}), bf16[128,32,128]{2,1,0:T(8,128)(2,1)S(1)}, u32[]{:S(2)}, u32[]{:S(2)}) async-start(bf16[128,32,128]{2,1,0:T(8,128)(2,1)} %bitcast.8), calls=%async_computation.1 | async-start | bytes 2097152 | tf_op jit(solution)/shard_map/all_to_all | solution.py:617
  110.1 11.7 %all-gather = bf16[4,64,8]{1,2,0:T(8,128)(2,1)S(1)} all-gather(bf16[1,64,8]{1,2,0:T(8,128)(2,1)S(1)} %bitcast.98), channel_id=1, replica_groups=mesh['dp'=32,'mp'=4] {'mp'}, dimensions={0}, use_global_device_ids=true | all-gather | bytes 5120 | tf_op jit(solution)/shard_map/all_gather | solution.py:641
  122.5 0.7 reshape.134.gate_b_ref
  123.4 12.3 %all_gather.11.w_out_ref = bf16[8,256,128]{2,1,0:T(8,128)(2,1)} all-gather(bf16[8,64,128]{2,1,0:T(8,128)(2,1)S(1)} %copy-done.8), channel_id=1, replica_groups=mesh['dp'=32,'mp'=4] {'mp'}, dimensions={1}, use_global_device_ids=true | all-gather | bytes 655360 | tf_op jit(solution)/shard_map/all_gather | solution.py:640
  136.2 26.4 %embed.1.x_ref = bf16[512,512]{1,0:T(8,128)(2,1)S(1)} custom-call(s32[32768]{0:T(1024)S(1)} %bitcast.72, s32[16]{0:T(128)S(1)} %get-tuple-element.27.hot_ref, bf16[4096,128]{1,0:T(8,128)(2,1)S(1)} %bitcast.69, f32[13,512]{1,0:T(8,128)S(1)} %bitcast.75, f32[13,128]{1,0:T(8,128)S(1)} %pad.8.dw_ref, f32[1,128]{1,0:T(1,128)S(1)} %pad_bitcast_fusion.db_ref), custom_call_target="tpu_custom_call" | custom-call | tf_op jit(solution)/shard_map/embed/pallas_call | solution.py:252
  162.7 0.8 copy-done.3
  163.5 27.7 %model.1 = (bf16[32,4,80,128]{3,2,1,0:T(8,128)(2,1)}, f32[256,128]{1,0:T(8,128)}, f32[512,512]{1,0:T(8,128)}, f32[13,512]{1,0:T(8,128)}) custom-call(bf16[512,512]{1,0:T(8,128)(2,1)} %copy-done.3, s32[2,512]{1,0:T(2,128)} %bitcast.95, f32[13,512]{1,0:T(8,128)} %bitcast.74, f32[13,128]{1,0:T(8,128)} %copy-done.7, ...), custom_call_target="tpu_custom_call" | custom-call | tf_op jit(solution)/shard_map/model/pallas_call | solution.py:454
  191.2 25.4 %all_to_all.51.parts_ref = f32[128,2,128]{2,1,0:T(2,128)S(1)} all-to-all(f32[128,2,128]{2,1,0:T(2,128)} %bitcast.87), channel_id=1, replica_groups=mesh['dp'=32,'mp'=4] {'dp','mp'}, dimensions={0} | all-to-all | bytes 262144 | tf_op jit(solution)/shard_map/all_to_all | solution.py:617
  216.5 0.7 sum_small.1
  217.2 14.0 %all_to_all.52 = f32[128,2,128]{2,1,0:T(2,128)S(1)} all-to-all(f32[128,2,128]{2,1,0:T(2,128)S(1)} %sum_small.1), channel_id=1, replica_groups=mesh['dp'=32,'mp'=4] {'dp','mp'}, dimensions={0} | all-to-all | bytes 262144 | tf_op jit(solution)/shard_map/all_to_all | solution.py:617
  231.2 4.2 %all-to-all-start.5 = ((bf16[128,80,128]{2,1,0:T(8,128)(2,1)}), bf16[128,80,128]{2,1,0:T(8,128)(2,1)S(1)}, u32[]{:S(2)}, u32[]{:S(2)}) async-start(bf16[128,80,128]{2,1,0:T(8,128)(2,1)} %bitcast.79), calls=%async_computation.5 | async-start | bytes 5242880 | tf_op jit(solution)/shard_map/all_to_all | solution.py:617
  235.4 1.2 copy-done.5
  236.7 27.2 %spread_grads.1 = bf16[4096,128]{1,0:T(8,128)(2,1)S(1)} custom-call(s32[32768]{0:T(1024)S(1)} %bitcast.73, s32[16]{0:T(128)S(1)} %get-tuple-element.27.hot_ref, f32[512,512]{1,0:T(8,128)S(1)} %copy-done.5), custom_call_target="tpu_custom_call" | custom-call | tf_op jit(solution)/shard_map/spread_grads/pallas_call | solution.py:519
  263.9 1.0 copy-done.2
  264.8 6.7 %all-to-all-done.5.parts_ref = bf16[128,80,128]{2,1,0:T(8,128)(2,1)S(1)} async-done(((bf16[128,80,128]{2,1,0:T(8,128)(2,1)}), bf16[128,80,128]{2,1,0:T(8,128)(2,1)S(1)}, u32[]{:S(2)}, u32[]{:S(2)}) %all-to-all-start.5) | async-done | bytes 2621472 | tf_op jit(solution)/shard_map/all_to_all | solution.py:617
  271.6 4.8 %all-to-all-start.2 = ((bf16[128,32,128]{2,1,0:T(8,128)(2,1)}), bf16[128,32,128]{2,1,0:T(8,128)(2,1)}, u32[]{:S(2)}, u32[]{:S(2)}) async-start(bf16[128,32,128]{2,1,0:T(8,128)(2,1)} %bitcast.68), calls=%async_computation.2 | async-start | bytes 2097152 | tf_op jit(solution)/shard_map/all_to_all | solution.py:617
  279.1 1.8 sum_grads.1
  280.9 14.7 %all-to-all-done.2 = bf16[128,32,128]{2,1,0:T(8,128)(2,1)} async-done(((bf16[128,32,128]{2,1,0:T(8,128)(2,1)}), bf16[128,32,128]{2,1,0:T(8,128)(2,1)}, u32[]{:S(2)}, u32[]{:S(2)}) %all-to-all-start.2) | async-done | bytes 1048608 | tf_op jit(solution)/shard_map/all_to_all | solution.py:617
  295.5 3.9 %all-to-all-start.6 = ((bf16[32,80,128]{2,1,0:T(8,128)(2,1)}), bf16[32,80,128]{2,1,0:T(8,128)(2,1)S(1)}, u32[]{:S(2)}, u32[]{:S(2)}) async-start(bf16[32,80,128]{2,1,0:T(8,128)(2,1)} %sum_grads.1), calls=%async_computation.6 | async-start | bytes 1310720 | tf_op jit(solution)/shard_map/all_to_all | solution.py:617
  303.2 72.2 %scatter_add.1 = f32[26,16,4096]{2,1,0:T(8,128)} custom-call(s32[32768]{0:T(1024)} %bitcast.71, bf16[4096,128]{1,0:T(8,128)(2,1)} %bitcast.24.grads_ref), custom_call_target="tpu_custom_call" | custom-call | tf_op jit(solution)/shard_map/scatter_add/pallas_call | solution.py:582
  375.6 0.7 slice_bitcast_fusion.1
  376.3 1.1 copy_bitcast_fusion
  (62 shorter events, 9.5 us)
Async XLA Ops:
  7.2 156.3 %all-gather.3.cloned.1.call-start = ((), (), s32[]{:S(2)}) async-start(), calls=%async_computation.7 | async-start | bytes 2621440 | tf_op jit(solution)/shard_map/all_gather | solution.py:639
  29.3 21.7 %all-to-all-start = ((s32[128,2,128]{2,1,0:T(2,128)}), s32[128,2,128]{2,1,0:T(2,128)S(1)}, u32[]{:S(2)}, u32[]{:S(2)}) async-start(s32[128,2,128]{2,1,0:T(2,128)} %bitcast.4), calls=%async_computation | async-start | bytes 262144 | tf_op jit(solution)/shard_map/all_to_all | solution.py:617
  40.8 2.9 copy-start.1
  48.2 2.8 copy-start
  51.1 48.0 %copy-start.4 = (s32[128,2,128]{2,1,0:T(2,128)}, s32[128,2,128]{2,1,0:T(2,128)S(1)}, u32[]{:S(2)}) copy-start(s32[128,2,128]{2,1,0:T(2,128)S(1)} %all-to-all-done) | copy-start | bytes 393220
  51.1 57.7 %copy-start.12 = (f32[2,64]{1,0:T(2,128)S(1)}, f32[2,64]{1,0:T(2,128)}, u32[]{:S(2)}) copy-start(f32[2,64]{1,0:T(2,128)} %param.29) | copy-start | bytes 1540
  51.1 58.3 %copy-start.13 = (f32[2,64]{1,0:T(2,128)S(1)}, f32[2,64]{1,0:T(2,128)}, u32[]{:S(2)}) copy-start(f32[2,64]{1,0:T(2,128)} %param.30) | copy-start | bytes 1540
  51.1 58.4 %copy-start.14 = (f32[2]{0:T(128)S(1)}, f32[2]{0:T(128)}, u32[]{:S(2)}) copy-start(f32[2]{0:T(128)} %param.31) | copy-start | bytes 28
  51.1 59.1 %copy-start.10 = (bf16[8,64]{1,0:T(8,128)(2,1)S(1)}, bf16[8,64]{1,0:T(8,128)(2,1)}, u32[]{:S(2)}) copy-start(bf16[8,64]{1,0:T(8,128)(2,1)} %param.23) | copy-start | bytes 3076
  51.1 71.4 %copy-start.11 = (f32[2,8]{1,0:T(2,128)S(1)}, f32[2,8]{1,0:T(2,128)}, u32[]{:S(2)}) copy-start(f32[2,8]{1,0:T(2,128)} %param.27) | copy-start | bytes 196
  51.1 72.1 %copy-start.9 = (f32[13,96]{1,0:T(8,128)S(1)}, f32[13,96]{1,0:T(8,128)}, u32[]{:S(2)}) copy-start(f32[13,96]{1,0:T(8,128)} %param.20) | copy-start | bytes 14980
  51.1 72.2 %copy-start.15 = (f32[96]{0:T(128)S(1)}, f32[96]{0:T(128)}, u32[]{:S(2)}) copy-start(f32[96]{0:T(128)} %param.21) | copy-start | bytes 1156
  51.1 72.2 %copy-start.8 = (bf16[8,64,128]{2,1,0:T(8,128)(2,1)S(1)}, bf16[8,64,128]{2,1,0:T(8,128)(2,1)}, u32[]{:S(2)}) copy-start(bf16[8,64,128]{2,1,0:T(8,128)(2,1)} %param.24) | copy-start | bytes 393220
  99.0 37.2 %copy-start.6 = (f32[512,13]{0,1:T(8,128)S(1)}, f32[512,13]{0,1:T(8,128)}, u32[]{:S(2)}) copy-start(f32[512,13]{0,1:T(8,128)} %param.17) | copy-start | bytes 79876
  99.0 37.2 %all-to-all-start.1 = ((bf16[128,32,128]{2,1,0:T(8,128)(2,1)}), bf16[128,32,128]{2,1,0:T(8,128)(2,1)S(1)}, u32[]{:S(2)}, u32[]{:S(2)}) async-start(bf16[128,32,128]{2,1,0:T(8,128)(2,1)} %bitcast.8), calls=%async_computation.1 | async-start | bytes 2097152 | tf_op jit(solution)/shard_map/all_to_all | solution.py:617
  123.3 40.2 %copy-start.7 = (f32[13,128]{1,0:T(8,128)}, f32[13,128]{1,0:T(8,128)S(1)}, u32[]{:S(2)}) copy-start(f32[13,128]{1,0:T(8,128)S(1)} %pad.8.dw_ref) | copy-start | bytes 19972
  162.7 0.8 copy-start.3
  231.2 40.3 %all-to-all-start.5 = ((bf16[128,80,128]{2,1,0:T(8,128)(2,1)}), bf16[128,80,128]{2,1,0:T(8,128)(2,1)S(1)}, u32[]{:S(2)}, u32[]{:S(2)}) async-start(bf16[128,80,128]{2,1,0:T(8,128)(2,1)} %bitcast.79), calls=%async_computation.5 | async-start | bytes 5242880 | tf_op jit(solution)/shard_map/all_to_all | solution.py:617
  235.4 1.2 copy-start.5
  263.9 1.0 copy-start.2
  271.6 24.0 %all-to-all-start.2 = ((bf16[128,32,128]{2,1,0:T(8,128)(2,1)}), bf16[128,32,128]{2,1,0:T(8,128)(2,1)}, u32[]{:S(2)}, u32[]{:S(2)}) async-start(bf16[128,32,128]{2,1,0:T(8,128)(2,1)} %bitcast.68), calls=%async_computation.2 | async-start | bytes 2097152 | tf_op jit(solution)/shard_map/all_to_all | solution.py:617
  295.5 79.9 %all-to-all-start.6 = ((bf16[32,80,128]{2,1,0:T(8,128)(2,1)}), bf16[32,80,128]{2,1,0:T(8,128)(2,1)S(1)}, u32[]{:S(2)}, u32[]{:S(2)}) async-start(bf16[32,80,128]{2,1,0:T(8,128)(2,1)} %sum_grads.1), calls=%async_computation.6 | async-start | bytes 1310720 | tf_op jit(solution)/shard_map/all_to_all | solution.py:617
Sparse Core Ops, SparseCore 0:
  9.7 34.3 all-gather.2

commit v2 on v1

v2 whole, which is shorter than its diff:
```python
import functools

import jax
import jax.numpy as jnp
from jax import lax
from jax.experimental import pallas as pl
from jax.experimental.pallas import tpu as pltpu
from jax.sharding import PartitionSpec as P

ALL = ("dp", "mp")
EXACT = lax.Precision.HIGHEST
F32 = jnp.float32
BF16 = jnp.bfloat16

OWNERS = 128
FIELDS = 26
EMB = 16
ROWS_LOC = 512
ROWS_DEV = 4096
LOOKUPS = ROWS_LOC * FIELDS
PACKED = FIELDS * ROWS_DEV // 8
CAP = 208
COLD = 96
HOT = 16
SLOTS = 256
GROUPS = SLOTS // 8
EXPERTS = 8
HID = 256
EOUT = 128
TASKS = 2
THID = 64
DIN = 512
DENSE = 13
DPROJ = 96
CHUNK = 80
TILES = 32
SENT = CHUNK + 16
PART = 64
SUMS = 6

VM = pl.BlockSpec(memory_space=pltpu.VMEM)
SM = pl.BlockSpec(memory_space=pltpu.SMEM)


def params(mib):
    return pltpu.CompilerParams(vmem_limit_bytes=mib * 1024 * 1024)


def shape(dims, dtype):
    return jax.ShapeDtypeStruct(dims, dtype)


def lane_group(rows):
    return lax.broadcasted_iota(jnp.int32, (rows, 128), 1) // EMB


def sublane_group():
    return lax.broadcasted_iota(jnp.int32, (128, 128), 0) // EMB


def eight(index, unit=8):
    return pl.multiple_of(index, unit)


def dot_nt(a, b, precision=None):
    return lax.dot_general(
        a, b, (((1,), (1,)), ((), ())), precision=precision, preferred_element_type=F32
    )


def dot_tn(a, b, precision=None):
    return lax.dot_general(
        a, b, (((0,), (0,)), ((), ())), precision=precision, preferred_element_type=F32
    )


def dot_nn(a, b, precision=None):
    return lax.dot_general(
        a, b, (((1,), (0,)), ((), ())), precision=precision, preferred_element_type=F32
    )


def split3(value):
    high = value.astype(BF16)
    rest = value - high.astype(F32)
    mid = rest.astype(BF16)
    low = (rest - mid.astype(F32)).astype(BF16)
    return high, mid, low


def route_kernel(key_ref, load_ref, req_ref, src_ref, hot_ref, both, cut, starts_v, starts, sem):
    own = (key_ref[...] & 16383) << 17
    both[pl.ds(0, 104), :] = own | load_ref[...]
    both[pl.ds(104, 8), :] = jnp.zeros((8, 128), jnp.int32)
    owner_at = lax.broadcasted_iota(jnp.int32, (128, 128), 0)

    def count(step, total):
        rows = key_ref[pl.ds(eight(step * 8), 8), :] >> 14
        for at in range(8):
            total = total + (rows[at : at + 1, :] < owner_at).astype(jnp.int32)
        return total

    below = lax.fori_loop(0, 13, count, jnp.zeros((128, 128), jnp.int32))
    first = jnp.sum(below.astype(F32).T, axis=0, keepdims=True).astype(jnp.int32)
    starts_v[...] = jnp.broadcast_to(first, (8, 128))
    copy = pltpu.make_async_copy(starts_v, starts, sem)
    copy.start()
    copy.wait()
    for at in range(2 * HOT):
        hot_ref[at] = 0
    lane = lax.broadcasted_iota(jnp.int32, (1, 128), 1)
    unused = (LOOKUPS << 17) | (PACKED * 8)

    def per_owner(owner, hot_count):
        start = starts[0, owner]
        end = jnp.where(owner == OWNERS - 1, LOOKUPS, starts[0, jnp.minimum(owner + 1, 127)])
        row = start >> 7
        off = start & 127
        pieces = [both[pl.ds(row + at, 1), :] for at in range(3)]
        for half in range(2):
            piece = jnp.where(lane >= off, pieces[half], pieces[half + 1])
            piece = pltpu.roll(piece, (128 - off) & 127, 1)
            cut[pl.ds(2 * owner + half, 1), :] = jnp.where(
                lane < end - start - 128 * half, piece, unused
            )
        hot_ref[hot_count] = owner
        return jnp.minimum(hot_count + (end - start > COLD).astype(jnp.int32), 2 * HOT - 1)

    lax.fori_loop(0, OWNERS, per_owner, 0, unroll=8)
    src_ref[...] = cut[...] >> 17
    req_ref[...] = cut[...] & ((1 << 17) - 1)


def route(keys, loads):
    return pl.pallas_call(
        route_kernel,
        in_specs=[VM, VM],
        out_specs=[VM, VM, SM],
        out_shape=[
            shape((2 * OWNERS, 128), jnp.int32),
            shape((2 * OWNERS, 128), jnp.int32),
            shape((2 * HOT,), jnp.int32),
        ],
        scratch_shapes=[
            pltpu.VMEM((112, 128), jnp.int32),
            pltpu.VMEM((2 * OWNERS, 128), jnp.int32),
            pltpu.VMEM((8, 128), jnp.int32),
            pltpu.SMEM((8, 128), jnp.int32),
            pltpu.SemaphoreType.DMA,
        ],
        compiler_params=params(32),
        name="route",
    )(keys, loads)


def pack_kernel(table_ref, out_ref):
    for part in range(4):
        block = jnp.concatenate(
            [table_ref[0, :, pl.ds(part * 1024 + k * 128, 128)] for k in range(8)], axis=0
        )
        out_ref[pl.ds(part * 128, 128), :] = block.T


def pack_tables(tables_t):
    return pl.pallas_call(
        pack_kernel,
        grid=(FIELDS,),
        in_specs=[pl.BlockSpec((1, EMB, ROWS_DEV), lambda f: (f, 0, 0))],
        out_specs=pl.BlockSpec((512, 128), lambda f: (f, 0)),
        out_shape=shape((PACKED + 8, 128), F32),
        compiler_params=params(32),
        name="pack_tables",
    )(tables_t)


def split_wanted(asked_ref, rows_v, groups, rows, sem):
    rows_v[...] = asked_ref[...] >> 3
    copy = pltpu.make_async_copy(rows_v, rows, sem)
    copy.start()
    groups[...] = asked_ref[...] & 7
    copy.wait()


def split_scratch():
    return [
        pltpu.VMEM((2 * OWNERS, 128), jnp.int32),
        pltpu.VMEM((2 * OWNERS, 128), jnp.int32),
        pltpu.SMEM((2 * OWNERS, 128), jnp.int32),
        pltpu.SemaphoreType.DMA,
    ]


def look_up_kernel(asked_ref, table_ref, out_ref, rows_v, groups, rows, sem, even, odd):
    split_wanted(asked_ref, rows_v, groups, rows, sem)
    at_group = sublane_group()

    def gather(source, found):
        for n in range(CAP):
            at = rows[2 * source + n // 128, n % 128]
            found[pl.ds(n, 1), :] = table_ref[pl.ds(at, 1), :]

    def pick(source, found):
        for half in range(2):
            block = found[pl.ds(half * 128, 128), :].T
            block = jnp.where(at_group == groups[pl.ds(2 * source + half, 1), :], block, 0.0)
            block = jnp.sum(block.reshape(8, EMB, 128), axis=0)
            out_ref[pl.ds(eight(source * GROUPS + EMB * half, EMB), EMB), :] = block.astype(BF16)

    even[...] = jnp.zeros_like(even)
    odd[...] = jnp.zeros_like(odd)
    gather(0, even)

    def two_sources(step, carry):
        source = 2 * step
        gather(source + 1, odd)
        pick(source, even)
        gather(jnp.minimum(source + 2, OWNERS - 1), even)
        pick(source + 1, odd)
        return carry

    lax.fori_loop(0, OWNERS // 2, two_sources, 0)


def look_up(asked, table):
    return pl.pallas_call(
        look_up_kernel,
        in_specs=[VM, VM],
        out_specs=VM,
        out_shape=shape((OWNERS * GROUPS, 128), BF16),
        scratch_shapes=split_scratch() + [pltpu.VMEM((SLOTS, 128), F32)] * 2,
        compiler_params=params(48),
        name="look_up",
    )(asked, table)


def embed_kernel(
    src_ref, hot_ref, ids_ref, answer_ref, feats_ref, dw_ref, db_ref, out_ref, slots, rows, x_t
):
    for block in range(32):
        owner, half = block // 2 * 8, block % 2
        parts = [
            answer_ref[pl.ds((owner + u) * GROUPS + EMB * half, EMB), :] for u in range(8)
        ]
        slots[pl.ds(block * 128, 128), :] = jnp.concatenate(parts, axis=0).astype(F32).T

    def cold(step, carry):
        base = step // 6 * SLOTS + step % 6 * 16
        source = step // 6 * (8 * SLOTS) + step % 6 * 16
        for n in range(16):
            row = slots[pl.ds(base + n, 1), :]
            for u in range(8):
                rows[pl.ds(src_ref[source + u * SLOTS + n], 1), :] = row
        return carry

    def hot(at, carry):
        owner = hot_ref[at]
        base = (owner >> 3) * SLOTS
        for n in range(COLD, CAP):
            rows[pl.ds(src_ref[owner * SLOTS + n], 1), :] = slots[pl.ds(base + n, 1), :]
        return carry

    lax.fori_loop(0, OWNERS // 8 * 6, cold, 0)
    lax.fori_loop(0, HOT, hot, 0)
    at_group = sublane_group()

    def field(f, carry):
        group = (ids_ref[pl.ds(f, 1), :] >> 12) & 7
        for part in range(4):
            block = rows[pl.ds(eight(f * ROWS_LOC + part * 128, 128), 128), :].T
            block = jnp.where(at_group == group[:, part * 128 : part * 128 + 128], block, 0.0)
            block = jnp.sum(block.reshape(8, EMB, 128), axis=0)
            x_t[pl.ds(eight(f * EMB, EMB), EMB), pl.ds(part * 128, 128)] = block
        return carry

    lax.fori_loop(0, FIELDS, field, 0)
    x_t[pl.ds(FIELDS * EMB, DPROJ), :] = dot_tn(dw_ref[...], feats_ref[...], EXACT) + db_ref[...]
    out_ref[...] = x_t[...].T.astype(BF16)


def embed(src, hot, ids, answer, feats_t, dense_w, dense_b):
    return pl.pallas_call(
        embed_kernel,
        in_specs=[SM, SM, VM, VM, VM, VM, VM],
        out_specs=VM,
        out_shape=shape((ROWS_LOC, DIN), BF16),
        scratch_shapes=[
            pltpu.VMEM((OWNERS * GROUPS, 128), F32),
            pltpu.VMEM((LOOKUPS + 8, 128), F32),
            pltpu.VMEM((DIN, ROWS_LOC), F32),
        ],
        compiler_params=params(48),
        name="embed",
    )(src, hot, ids, answer, feats_t, dense_w, dense_b)


C0 = 0.7978845608
C1 = 0.7978845608 * 0.044715


def gelu_both(value):
    square = value * value
    bend = jnp.tanh(value * (C0 + C1 * square))
    half = 0.5 * (1.0 + bend)
    slope = half + 0.5 * value * (1.0 - bend * bend) * (C0 + 3.0 * C1 * square)
    return value * half, slope


def two_parts(value):
    high = value.astype(BF16).astype(F32)
    return jnp.concatenate([high, value - high], axis=0).astype(BF16)


def one_of(parts):
    wide = parts.astype(F32)
    return wide[0:8] + wide[8:16]


def model_kernel(
    x_ref,
    labels_ref,
    feats_ref,
    dw_ref,
    weights_ref,
    b_out_ref,
    gate_w_ref,
    gate_b_ref,
    w1_ref,
    b1_ref,
    w2_ref,
    b2_ref,
    grads_ref,
    d_low_ref,
    grad_dense_ref,
    small_ref,
    small_b,
    d_in_ref,
    hidden,
    slope,
    outs,
    probs,
    d_raw,
    prod_hi,
    prod_lo,
    mix,
    stage,
):
    x = x_ref[...]
    phase = pl.program_id(0)

    def weights_in(k):
        return jnp.concatenate(
            [weights_ref[p, k, pl.ds(0, PART), pl.ds(0, DIN)] for p in range(4)], axis=0
        )

    def weights_out(k):
        return jnp.concatenate(
            [weights_ref[p, k, pl.ds(0, PART), pl.ds(DIN, EOUT)] for p in range(4)], axis=0
        )

    def forward(k, carry):
        bias = [
            weights_ref[p, k, pl.ds(PART, 16), pl.ds(0, 128)].astype(F32)[0:1, 0:PART]
            for p in range(4)
        ]
        pre = dot_nt(x, weights_in(k)) + jnp.concatenate(bias, axis=1)
        act, grad = gelu_both(pre)
        act = act.astype(BF16)
        hidden[k] = act
        slope[k] = grad
        outs[k] = dot_nn(act, weights_out(k)) + b_out_ref[k]
        return carry

    def head():
        gate_parts = jnp.concatenate(split3(gate_w_ref[...]), axis=0)
        stage[...] = dot_nt(gate_parts, x)
        logits = stage[0:16] + stage[16:32] + stage[32:48] + gate_b_ref[...]
        logits = logits.reshape(TASKS, EXPERTS, ROWS_LOC)
        gates = jnp.exp(logits - jnp.max(logits, axis=1, keepdims=True))
        gates = gates / jnp.sum(gates, axis=1, keepdims=True)
        gates_t = gates.reshape(TASKS * EXPERTS, ROWS_LOC)
        gate_stack = jnp.concatenate(split3(gates_t), axis=0)
        row_at = lax.broadcasted_iota(jnp.int32, (48, 128), 0) % 16

        def spread(k, carry):
            ones = (row_at == k).astype(F32).astype(BF16)
            probs[k] = dot_tn(gate_stack, ones)
            return carry

        lax.fori_loop(0, TASKS * EXPERTS, spread, 0)

        for t in range(TASKS):
            def add(k, total):
                return total + probs[t * EXPERTS + k] * outs[k]

            mix[:, pl.ds(t * EOUT, EOUT)] = lax.fori_loop(
                1, EXPERTS, add, probs[t * EXPERTS] * outs[0]
            )
        mixture = mix[...]
        zero = jnp.zeros((THID, EOUT), F32)
        w1_bd = jnp.concatenate(
            [
                jnp.concatenate([w1_ref[0], zero], axis=1),
                jnp.concatenate([zero, w1_ref[1]], axis=1),
            ],
            axis=0,
        )
        upper, upper_slope = gelu_both(dot_nt(mixture, w1_bd, EXACT) + b1_ref[...])
        w2_bd = w2_ref[...]
        logit = dot_nt(w2_bd, upper, EXACT) + b2_ref[...]
        d_logit = jax.nn.sigmoid(logit) - labels_ref[...].astype(F32)
        d_pre1 = dot_tn(d_logit, w2_bd, EXACT) * upper_slope
        grad_w2 = dot_nn(d_logit, upper, EXACT)
        grad_b1 = jnp.sum(d_pre1, axis=0, keepdims=True)
        grad_w1 = dot_tn(d_pre1, mixture, EXACT)
        d_mix = dot_nn(d_pre1, w1_bd, EXACT)
        mix[...] = d_mix

        def back_raw(k, carry):
            d_one = mix[:, pl.ds(0, EOUT)]
            d_two = mix[:, pl.ds(EOUT, EOUT)]
            grad = probs[k] * d_one + probs[EXPERTS + k] * d_two
            small_ref[pl.ds(128 + k, 1), :] = jnp.sum(grad, axis=0, keepdims=True)
            d_raw[k] = grad.astype(BF16)
            value = outs[k]
            for t, d_task in enumerate((d_one, d_two)):
                product = value * d_task
                high = product.astype(BF16)
                at = pl.ds(pl.multiple_of((t * EXPERTS + k) * EOUT, EOUT), EOUT)
                prod_hi[:, at] = high
                prod_lo[:, at] = (product - high.astype(F32)).astype(BF16)
            return carry

        lax.fori_loop(0, EXPERTS, back_raw, 0)

        wide = TASKS * EXPERTS * EOUT
        column_gate = lax.broadcasted_iota(jnp.int32, (16, wide), 1) // EOUT
        own_gate = lax.broadcasted_iota(jnp.int32, (16, wide), 0)
        ones = (column_gate == own_gate).astype(F32).astype(BF16)
        stage[0:16] = dot_nt(ones, prod_hi[...])
        stage[16:32] = dot_nt(ones, prod_lo[...])
        d_gates = stage[0:16] + stage[16:32]
        d_gates = d_gates.reshape(TASKS, EXPERTS, ROWS_LOC)
        mean = jnp.sum(d_gates * gates, axis=1, keepdims=True)
        d_logits = (gates * (d_gates - mean)).reshape(16, ROWS_LOC)
        d_parts = jnp.concatenate(split3(d_logits), axis=0)
        stage[...] = dot_nn(d_parts, x)
        grad_gate = stage[0:16] + stage[16:32] + stage[32:48]
        d_in_ref[...] = dot_tn(d_logits, gate_w_ref[...], EXACT)
        small_ref[pl.ds(0, THID), :] = grad_w1[0:THID, 0:EOUT]
        small_ref[pl.ds(THID, THID), :] = grad_w1[THID : 2 * THID, EOUT : 2 * EOUT]
        for tile in range(4):
            small_ref[pl.ds(136 + 16 * tile, 16), :] = grad_gate[:, tile * 128 : tile * 128 + 128]
        small_ref[pl.ds(217, 1), :] = grad_b1
        lane = lax.broadcasted_iota(jnp.int32, (1, 128), 1)
        small_ref[pl.ds(218, 1), :] = jnp.where(lane < THID, grad_w2[0:1], grad_w2[1:2])
        small_ref[pl.ds(219, 1), :] = jnp.zeros((1, 128), F32)
        small_b[...] = jnp.zeros_like(small_b)
        small_ref[pl.ds(220, 2), :] = jnp.broadcast_to(
            jnp.sum(d_logit, axis=1, keepdims=True), (2, 128)
        )
        small_ref[pl.ds(222, 2), :] = jnp.zeros((2, 128), F32)
        small_ref[pl.ds(224, 16), :] = jnp.broadcast_to(
            jnp.sum(d_logits, axis=1, keepdims=True), (16, 128)
        )

    def backward(k, carry):
        d_out = d_raw[k]
        grad_out = dot_tn(hidden[k], d_out).astype(BF16)
        d_pre = (dot_nt(d_out, weights_out(k)) * slope[k]).astype(BF16)
        bias = jnp.sum(d_pre.astype(F32), axis=0, keepdims=True)
        for p in range(4):
            small_b[p, pl.ds(k, 1), pl.ds(0, PART)] = bias[:, PART * p : PART * p + PART]
        grad_in = dot_tn(d_pre, x).astype(BF16)
        for part in range(4):
            for block in range(5):
                for piece in range(4):
                    at = block * 64 + piece * 16
                    rows = slice(part * 64 + piece * 16, part * 64 + piece * 16 + 16)
                    if block < 4:
                        value = grad_in[rows, block * 128 : block * 128 + 128]
                    else:
                        value = grad_out[rows, :]
                    grads_ref[4 * k + at // CHUNK, part, pl.ds(at % CHUNK, 16), :] = value
        d_in_ref[...] += dot_nn(d_pre, weights_in(k))
        return carry

    def tail():
        d_last = d_in_ref[:, pl.ds(DIN - DPROJ, DPROJ)]
        small_ref[pl.ds(200, 16), :] = jnp.zeros((16, 128), F32)
        small_ref[pl.ds(200, DENSE), pl.ds(0, DPROJ)] = dot_nn(feats_ref[...], d_last, EXACT)
        small_ref[pl.ds(216, 1), :] = jnp.zeros((1, 128), F32)
        small_ref[pl.ds(216, 1), pl.ds(0, DPROJ)] = jnp.sum(d_last, axis=0, keepdims=True)
        grad_dense_ref[...] = dot_nt(dw_ref[...], d_last, EXACT)
        d_low_ref[...] = d_in_ref[...].astype(BF16)
        for tile in range(TILES - 2):
            value = small_ref[pl.ds(8 * tile, 8), :]
            both = two_parts(value)
            for p in range(4):
                grads_ref[tile, p, pl.ds(CHUNK, 16), :] = both
        for p in range(4):
            grads_ref[TILES - 2, p, pl.ds(CHUNK, 16), :] = two_parts(small_b[p])
            grads_ref[TILES - 1, p, pl.ds(CHUNK, 16), :] = jnp.zeros((16, 128), BF16)

    @pl.when(phase == 0)
    def _():
        lax.fori_loop(0, EXPERTS, forward, 0)

    @pl.when(phase == 1)
    def _():
        head()

    @pl.when(phase == 2)
    def _():
        lax.fori_loop(0, EXPERTS, backward, 0)
        tail()


def model(*operands):
    return pl.pallas_call(
        model_kernel,
        grid=(3,),
        in_specs=[VM] * len(operands),
        out_specs=[VM] * 3,
        out_shape=[
            shape((TILES, 4, SENT, 128), BF16),
            shape((ROWS_LOC, DIN), BF16),
            shape((DENSE, ROWS_LOC), F32),
        ],
        scratch_shapes=[
            pltpu.VMEM((8 * (TILES - 2), 128), F32),
            pltpu.VMEM((4, 8, 128), F32),
            pltpu.VMEM((ROWS_LOC, DIN), F32),
            pltpu.VMEM((EXPERTS, ROWS_LOC, HID), BF16),
            pltpu.VMEM((EXPERTS, ROWS_LOC, HID), F32),
            pltpu.VMEM((EXPERTS, ROWS_LOC, EOUT), F32),
            pltpu.VMEM((TASKS * EXPERTS, ROWS_LOC, EOUT), F32),
            pltpu.VMEM((EXPERTS, ROWS_LOC, EOUT), BF16),
            pltpu.VMEM((ROWS_LOC, TASKS * EXPERTS * EOUT), BF16),
            pltpu.VMEM((ROWS_LOC, TASKS * EXPERTS * EOUT), BF16),
            pltpu.VMEM((ROWS_LOC, TASKS * EOUT), F32),
            pltpu.VMEM((48, DIN), F32),
        ],
        compiler_params=params(56),
        name="model",
    )(*operands)


def spread_kernel(src_ref, hot_ref, d_ref, out_ref, slots, rows, hot_rows):
    lane_from = lax.broadcasted_iota(jnp.int32, (128, 128), 0)
    lane_to = lax.broadcasted_iota(jnp.int32, (128, 128), 1)
    for field in range(FIELDS):
        take = lane_from == EMB * (field % 8) + lane_to % EMB
        copies = dot_nn(d_ref[:, pl.ds(field // 8 * 128, 128)], take.astype(F32).astype(BF16))
        rows[pl.ds(field * ROWS_LOC, ROWS_LOC), :] = copies
    rows[pl.ds(LOOKUPS, 8), :] = jnp.zeros((8, 128), F32)
    group = lane_group(1)

    def clear(step, carry):
        slots[pl.ds(eight(step * SLOTS + COLD), SLOTS - COLD), :] = jnp.zeros(
            (SLOTS - COLD, 128), F32
        )
        return carry

    lax.fori_loop(0, OWNERS // 8, clear, 0)

    def cold(step, carry):
        base = step // 6 * SLOTS + step % 6 * 16
        source = step // 6 * (8 * SLOTS) + step % 6 * 16
        for n in range(16):
            total = rows[pl.ds(src_ref[source + n], 1), :]
            for u in range(1, 8):
                row = rows[pl.ds(src_ref[source + u * SLOTS + n], 1), :]
                total = jnp.where(group == u, row, total)
            slots[pl.ds(base + n, 1), :] = total
        return carry

    def hot(at, carry):
        owner = hot_ref[at]
        for n in range(COLD, CAP):
            row = rows[pl.ds(src_ref[owner * SLOTS + n], 1), :]
            hot_rows[pl.ds(at * (CAP - COLD) + n - COLD, 1), :] = row
        return carry

    lax.fori_loop(0, OWNERS // 8 * 6, cold, 0)
    lax.fori_loop(0, HOT, hot, 0)
    wide_group = lane_group(CAP - COLD)

    def merge(at, carry):
        owner = hot_ref[at]
        place = pl.ds(eight((owner >> 3) * SLOTS + COLD), CAP - COLD)
        new = hot_rows[pl.ds(eight(at * (CAP - COLD)), CAP - COLD), :]
        slots[place, :] = jnp.where(wide_group == (owner & 7), new, slots[place, :])
        return carry

    lax.fori_loop(0, HOT, merge, 0)
    for block in range(32):
        owner, half = block // 2 * 8, block % 2
        turned = slots[pl.ds(block * 128, 128), :].T.astype(BF16)
        for u in range(8):
            out_ref[pl.ds((owner + u) * GROUPS + EMB * half, EMB), :] = turned[
                EMB * u : EMB * u + EMB
            ]


def spread_grads(src, hot, d_inputs):
    return pl.pallas_call(
        spread_kernel,
        in_specs=[SM, SM, VM],
        out_specs=VM,
        out_shape=shape((OWNERS * GROUPS, 128), BF16),
        scratch_shapes=[
            pltpu.VMEM((OWNERS * GROUPS, 128), F32),
            pltpu.VMEM((LOOKUPS + 8, 128), F32),
            pltpu.VMEM((HOT * (CAP - COLD), 128), F32),
        ],
        compiler_params=params(48),
        name="spread_grads",
    )(src, hot, d_inputs)


def scatter_kernel(
    asked_ref, grads_ref, out_ref, rows_v, groups, rows, sem, even, odd, *sums
):
    split_wanted(asked_ref, rows_v, groups, rows, sem)
    at_group = sublane_group()

    def clear(step, carry):
        for total in sums:
            total[pl.ds(eight(step * 512), 512), :] = jnp.zeros((512, 128), F32)
        return carry

    lax.fori_loop(0, PACKED // 512, clear, 0)

    def place(source, found):
        for half in range(2):
            block = grads_ref[pl.ds(eight(source * GROUPS + EMB * half, EMB), EMB), :].astype(F32)
            block = jnp.broadcast_to(block[None], (8, EMB, 128)).reshape(128, 128)
            block = jnp.where(at_group == groups[pl.ds(2 * source + half, 1), :], block, 0.0)
            found[pl.ds(half * 128, 128), :] = block.T

    def add(source, found):
        for n in range(CAP):
            at = pl.ds(rows[2 * source + n // 128, n % 128], 1)
            total = sums[n % SUMS]
            total[at, :] = total[at, :] + found[pl.ds(n, 1), :]

    place(0, even)

    def two_sources(step, carry):
        source = 2 * step
        place(source + 1, odd)
        add(source, even)
        place(jnp.minimum(source + 2, OWNERS - 1), even)
        add(source + 1, odd)
        return carry

    lax.fori_loop(0, OWNERS // 2, two_sources, 0)

    def write(field, carry):
        for part in range(4):
            at = pl.ds(eight(field * 512 + part * 128, 128), 128)
            block = sums[0][at, :]
            for total in sums[1:]:
                block = block + total[at, :]
            block = block.T
            for k in range(8):
                out_ref[field, :, pl.ds(part * 1024 + k * 128, 128)] = block[16 * k : 16 * k + 16]
        return carry

    lax.fori_loop(0, FIELDS, write, 0)


def scatter_add(asked, grads):
    return pl.pallas_call(
        scatter_kernel,
        in_specs=[VM, VM],
        out_specs=VM,
        out_shape=shape((FIELDS, EMB, ROWS_DEV), F32),
        scratch_shapes=split_scratch()
        + [pltpu.VMEM((SLOTS, 128), F32)] * 2
        + [pltpu.VMEM((PACKED + 8, 128), F32)] * SUMS,
        compiler_params=params(58),
        name="scatter_add",
    )(asked, grads)


def sum_kernel(parts_ref, out_ref):
    def add(at, total):
        return total + parts_ref[at].astype(F32)

    total = lax.fori_loop(1, OWNERS, add, parts_ref[0].astype(F32))
    small = two_parts(total[CHUNK : CHUNK + 8] + total[CHUNK + 8 : SENT])
    low = total[0:CHUNK].astype(BF16)
    for at in range(TILES):
        out_ref[at, pl.ds(0, CHUNK), :] = low
        out_ref[at, pl.ds(CHUNK, 16), :] = small


def sum_parts(parts):
    return pl.pallas_call(
        sum_kernel,
        in_specs=[VM],
        out_specs=VM,
        out_shape=shape((TILES, SENT, 128), BF16),
        compiler_params=params(32),
        name="sum_parts",
    )(parts)


def unpack_kernel(
    sums_ref,
    w_in_ref,
    w_out_ref,
    w1_ref,
    b_out_ref,
    gate_ref,
    dense_w_ref,
    dense_b_ref,
    b1_ref,
    w2_ref,
    b2_ref,
    gate_b_ref,
    b_in_ref,
):
    def expert(k, carry):
        rows = [sums_ref[4 * k + at, pl.ds(0, CHUNK), :] for at in range(4)]
        rows = jnp.concatenate(rows, axis=0).astype(F32)
        for block in range(4):
            w_in_ref[k, :, pl.ds(block * 128, 128)] = rows[PART * block : PART * block + PART]
        w_out_ref[k] = rows[4 * PART : 5 * PART]
        return carry

    lax.fori_loop(0, EXPERTS, expert, 0)

    def tile(at):
        return one_of(sums_ref[at, pl.ds(CHUNK, 16), :])

    for at in range(16):
        w1_ref[at // 8, pl.ds(at % 8 * 8, 8), :] = tile(at)
    b_out_ref[...] = tile(16)
    for at in range(8):
        gate_ref[pl.ds(at % 2 * 8, 8), pl.ds(at // 2 * 128, 128)] = tile(17 + at)
    dense_w_ref[pl.ds(0, 8), :] = tile(25)[:, 0:DPROJ]
    dense_w_ref[pl.ds(8, DENSE - 8), :] = tile(26)[0 : DENSE - 8, 0:DPROJ]
    rest = tile(27)
    dense_b_ref[...] = rest[0:1, 0:DPROJ]
    for t in range(TASKS):
        b1_ref[pl.ds(t, 1), :] = rest[1:2, t * THID : t * THID + THID]
        w2_ref[pl.ds(t, 1), :] = rest[2:3, t * THID : t * THID + THID]
    lane = lax.broadcasted_iota(jnp.int32, (1, 128), 1)
    b2_ref[...] = jnp.where(lane == 0, rest[4:5], rest[5:6])[:, 0:TASKS]
    own = lax.broadcasted_iota(jnp.int32, (8, 128), 0) == lax.broadcasted_iota(
        jnp.int32, (8, 128), 1
    )
    for t in range(TASKS):
        value = jnp.sum(jnp.where(own, tile(28 + t), 0.0), axis=0, keepdims=True)
        gate_b_ref[pl.ds(t, 1), :] = value[:, 0:EXPERTS]
    b_in_ref[...] = tile(30)[:, 0:PART]


def unpack(sums):
    return pl.pallas_call(
        unpack_kernel,
        in_specs=[VM],
        out_specs=[VM] * 12,
        out_shape=[
            shape((EXPERTS, PART, DIN), F32),
            shape((EXPERTS, PART, EOUT), F32),
            shape((TASKS, THID, EOUT), F32),
            shape((EXPERTS, EOUT), F32),
            shape((TASKS * EXPERTS, DIN), F32),
            shape((DENSE, DPROJ), F32),
            shape((1, DPROJ), F32),
            shape((TASKS, THID), F32),
            shape((TASKS, THID), F32),
            shape((1, TASKS), F32),
            shape((TASKS, EXPERTS), F32),
            shape((EXPERTS, PART), F32),
        ],
        compiler_params=params(32),
        name="unpack",
    )(sums)


def exchange(value, axes):
    return lax.all_to_all(value, axes, split_axis=0, concat_axis=0, tiled=True)


def body(
    sparse_ids,
    dense_feats,
    labels,
    tables,
    dense_w,
    dense_b,
    w_in,
    b_in,
    w_out,
    b_out,
    gate_w,
    gate_b,
    tower_w1,
    tower_b1,
    tower_w2,
    tower_b2,
):
    weights = jnp.concatenate([w_in.transpose(0, 2, 1), w_out], axis=2)
    bias = jnp.pad(b_in[:, None, :], ((0, 0), (0, 15), (0, DIN + EOUT - PART)))
    weights = lax.all_gather(jnp.concatenate([weights, bias], axis=1), "mp", axis=0)

    ids = sparse_ids.T
    field = lax.broadcasted_iota(jnp.int32, (FIELDS, ROWS_LOC), 0)
    example = lax.broadcasted_iota(jnp.int32, (FIELDS, ROWS_LOC), 1)
    row = ids & (ROWS_DEV - 1)
    packed = field * 512 + (row >> 10) * 128 + (row & 127)
    key = ((ids >> 12) << 14) | (field * ROWS_LOC + example)
    load = (packed << 3) | ((row >> 7) & 7)
    keys, loads = lax.sort((key.reshape(-1), load.reshape(-1)), num_keys=1, is_stable=False)
    requests, sources, hot = route(keys.reshape(-1, 128), loads.reshape(-1, 128))
    asked = exchange(requests, ALL)
    sources = sources.reshape(-1)
    table = pack_tables(tables.transpose(0, 2, 1))
    answer = exchange(look_up(asked, table), ALL)
    feats_t = dense_feats.T
    inputs = embed(sources, hot, ids, answer, feats_t, dense_w, dense_b.reshape(DPROJ, 1))
    task_at = lax.broadcasted_iota(jnp.int32, (TASKS, TASKS * THID), 1) // THID
    task_row = lax.broadcasted_iota(jnp.int32, (TASKS, TASKS * THID), 0)
    w2_bd = jnp.where(task_at == task_row, tower_w2.reshape(1, -1), 0.0)
    grads, d_inputs, grad_dense = model(
        inputs,
        labels.T,
        feats_t,
        dense_w,
        weights,
        b_out.reshape(EXPERTS, 1, EOUT),
        gate_w.transpose(0, 2, 1).reshape(TASKS * EXPERTS, DIN),
        gate_b.reshape(TASKS * EXPERTS, 1),
        tower_w1.transpose(0, 2, 1),
        tower_b1.reshape(1, TASKS * THID),
        w2_bd,
        tower_b2.reshape(TASKS, 1),
    )
    grads = exchange(grads.reshape(OWNERS, SENT, 128), ALL)
    incoming = exchange(spread_grads(sources, hot, d_inputs), ALL)
    sums = exchange(sum_parts(grads), "dp")
    grad_tables = scatter_add(asked, incoming).transpose(0, 2, 1)
    (
        grad_w_in,
        grad_w_out,
        grad_w1,
        grad_b_out,
        grad_gate_w,
        grad_dense_w,
        grad_dense_b,
        grad_b1,
        grad_w2,
        grad_b2,
        grad_gate_b,
        grad_b_in,
    ) = unpack(sums)
    return (
        grad_tables,
        grad_dense_w,
        grad_dense_b.reshape(DPROJ),
        grad_w_in.transpose(0, 2, 1),
        grad_b_in,
        grad_w_out,
        grad_b_out,
        grad_gate_w.reshape(TASKS, EXPERTS, DIN).transpose(0, 2, 1),
        grad_gate_b,
        grad_w1.transpose(0, 2, 1),
        grad_b1,
        grad_w2,
        grad_b2.reshape(TASKS),
        grad_dense.T,
    )


def solution(mesh):
    return jax.shard_map(
        body,
        mesh=mesh,
        in_specs=(
            P(ALL, None),
            P(ALL, None),
            P(ALL, None),
            P(None, ALL, None),
            P(),
            P(),
            P(None, None, "mp"),
            P(None, "mp"),
            P(None, "mp", None),
            P(),
            P(),
            P(),
            P(),
            P(),
            P(),
            P(),
        ),
        out_specs=(
            P(None, ALL, None),
            P(),
            P(),
            P(None, None, "mp"),
            P(None, "mp"),
            P(None, "mp", None),
            P(),
            P(),
            P(),
            P(),
            P(),
            P(),
            P(),
            P(ALL, None),
        ),
        check_vma=False,
    )
```

time: 387 us -> 281 us (0.73)
  Pallas kernels: 220 us -> 153 us
  blocking collectives: 63.3 us -> 0 us
  waiting for transfers between devices: 22.1 us -> 56.8 us
  local copies, waits for them, and re-layouts: 20 us -> 12.3 us
    pallas_call x4 -> x5, Pallas kernels: 174 us -> 127 us  [the longest x1 42.3 us: scatter_add(): pl.pallas_call(scatter_kernel, in_specs=[VM, VM], out_specs=VM, out_shape...]
    all_to_all x2 -> x0, blocking collectives: 39.4 us -> none  [exchange(): return lax.all_to_all(value, axes, split_axis=0, concat_axis=0, tiled=True)]
    all_to_all x5, waiting for transfers between devices: 21.4 us -> 56.8 us  [exchange(): return lax.all_to_all(value, axes, split_axis=0, concat_axis=0, tiled=True)]
    all_gather x2 -> x0, blocking collectives: 24 us -> none  [the longest x1 12.3 us: body(): w_out_all = lax.all_gather(w_out, 'mp', axis=1, tiled=True)]
    pallas_call x1, Pallas kernels: 27.2 us -> 17 us  [spread_grads(): pl.pallas_call(spread_kernel, in_specs=[SM, SM, VM], out_specs=VM, out_sh...]
    pallas_call x1, Pallas kernels: 12.1 us -> 3.62 us  [route(): pl.pallas_call(route_kernel, in_specs=[VM, VM], out_specs=[VM, VM, SM], o...]
    unnamed x35 -> x31, local copies, waits for them, and re-layouts: 8.9 us -> 10.2 us
  transfers between devices with their start and end apart: 6 -> 6, of which waited for: 2 -> 3; matrix products, arithmetic and copies ran while one was open for 5% -> 4% of each run, Pallas kernels for 50% -> 44%
where the time goes in v2:
time: 281 us
  Pallas kernels  153 us (54%)
  waiting for transfers between devices  56.8 us (20%)
  starting transfers between devices  34 us (12%)
  between operations  14.3 us (5%)
  local copies, waits for them, and re-layouts  12.3 us (4%)
  other arithmetic  10.1 us (4%)
    all_to_all x5, waiting for transfers between devices, exchange(): return lax.all_to_all(value, axes, split_axis=0, concat_axis=0, tiled=True)  56.8 us
    pallas_call x1, Pallas kernels, scatter_add(): pl.pallas_call(scatter_kernel, in_specs=[VM, VM], out_specs=VM, out_shape...  42.3 us
    pallas_call x1, Pallas kernels, look_up(): pl.pallas_call(look_up_kernel, in_specs=[VM, VM], out_specs=VM, out_shape...  35.8 us
    all_to_all x5, starting transfers between devices, exchange(): return lax.all_to_all(value, axes, split_axis=0, concat_axis=0, tiled=True)  34 us
    pallas_call x1, Pallas kernels, model(): pl.pallas_call(model_kernel, grid=(3,), in_specs=[VM] * len(operands), ou...  28.2 us
    pallas_call x1, Pallas kernels, embed(): pl.pallas_call(embed_kernel, in_specs=[SM, SM, VM, VM, VM, VM, VM], out_s...  19.6 us
    pallas_call x1, Pallas kernels, spread_grads(): pl.pallas_call(spread_kernel, in_specs=[SM, SM, VM], out_specs=VM, out_sh...  17 us
    unnamed x31, local copies, waits for them, and re-layouts  10.2 us
  transfers between devices with their start and end apart: 6, of which 3 were waited for; matrix products, arithmetic and copies ran while one was open for 4% of the time, Pallas kernels for 44%

profile of v2, /device:TPU:1, one launch (start us, length us, event | category | flops | bytes accessed | tf_op | source)
XLA Modules:
  0.0 280.7 jit_solution(2047468823131222375)
XLA Ops:
  7.2 0.7 copy.41
  7.9 2.1 fusion.1
  10.0 0.1 and_or_fusion
  10.2 7.4 %sort.15 = (s32[13312]{0:T(1024)S(1)}, s32[13312]{0:T(1024)S(1)}) sort(s32[13312]{0:T(1024)S(1)} %reshape.81, s32[13312]{0:T(1024)S(1)} %reshape.82), dimensions={0}, to_apply=%region_0.1 | sort | flops 186368 | bytes 212992 | tf_op jit(solution)/shard_map/sort | solution.py:818
  17.6 3.6 %route.1 = (s32[256,128]{1,0:T(8,128)}, s32[256,128]{1,0:T(8,128)S(1)}, s32[32]{0:T(128)S(1)}) custom-call(s32[104,128]{1,0:T(8,128)S(1)} %bitcast.45, s32[104,128]{1,0:T(8,128)S(1)} %bitcast.46), custom_call_target="tpu_custom_call" | custom-call | tf_op jit(solution)/shard_map/route/pallas_call | solution.py:135
  21.2 11.5 %all-to-all-start = ((s32[128,2,128]{2,1,0:T(2,128)}), s32[128,2,128]{2,1,0:T(2,128)S(1)}, u32[]{:S(2)}, u32[]{:S(2)}) async-start(s32[128,2,128]{2,1,0:T(2,128)} %bitcast.3), calls=%async_computation | async-start | bytes 262144 | tf_op jit(solution)/shard_map/all_to_all | solution.py:786
  32.7 3.0 %copy-done.1 = f32[26,4096,16]{1,2,0:T(8,128)S(1)} copy-done((f32[26,4096,16]{1,2,0:T(8,128)S(1)}, f32[26,4096,16]{1,2,0:T(8,128)}, u32[]{:S(2)}) %copy-start.1) | copy-done | bytes 6815768
  35.7 4.4 %pack_tables.1.table_ref = f32[13320,128]{1,0:T(8,128)S(1)} custom-call(f32[26,16,4096]{2,1,0:T(8,128)S(1)} %bitcast.35), custom_call_target="tpu_custom_call" | custom-call | tf_op jit(solution)/shard_map/pack_tables/pallas_call | solution.py:165
  40.1 2.8 copy-done
  43.0 35.8 %look_up.1 = bf16[4096,128]{1,0:T(8,128)(2,1)} custom-call(s32[256,128]{1,0:T(8,128)S(1)} %bitcast.38, f32[13320,128]{1,0:T(8,128)} %copy-done), custom_call_target="tpu_custom_call" | custom-call | tf_op jit(solution)/shard_map/look_up/pallas_call | solution.py:225
  78.9 9.8 %all-to-all-start.1 = ((bf16[128,32,128]{2,1,0:T(8,128)(2,1)}), bf16[128,32,128]{2,1,0:T(8,128)(2,1)S(1)}, u32[]{:S(2)}, u32[]{:S(2)}) async-start(bf16[128,32,128]{2,1,0:T(8,128)(2,1)} %bitcast.7), calls=%async_computation.1 | async-start | bytes 2097152 | tf_op jit(solution)/shard_map/all_to_all | solution.py:786
  88.7 0.6 reshape.90.b1_ref
  89.3 0.6 copy.40.b2_ref
  90.0 0.7 reshape.97.gate_b_ref
  90.7 0.1 copy.37.db_ref
  90.8 0.6 compare_select_fusion.w2_ref
  91.4 16.7 %all-to-all-done.1 = bf16[128,32,128]{2,1,0:T(8,128)(2,1)S(1)} async-done(((bf16[128,32,128]{2,1,0:T(8,128)(2,1)}), bf16[128,32,128]{2,1,0:T(8,128)(2,1)S(1)}, u32[]{:S(2)}, u32[]{:S(2)}) %all-to-all-start.1) | async-done | bytes 1048608 | tf_op jit(solution)/shard_map/all_to_all | solution.py:786
  108.1 19.6 %embed.1.x_ref = bf16[512,512]{1,0:T(8,128)(2,1)S(1)} custom-call(s32[32768]{0:T(1024)S(1)} %bitcast.40, s32[32]{0:T(128)S(1)} %get-tuple-element.38.hot_ref, s32[26,512]{1,0:T(8,128)S(1)} %bitcast.42, bf16[4096,128]{1,0:T(8,128)(2,1)S(1)} %bitcast.37, f32[13,512]{1,0:T(8,128)S(1)} %bitcast.44, f32[13,96]{1,0:T(8,128)S(1)} %copy-done.9, f32[96,1]{1,0:T(8,128)S(1)} %copy.37.db_ref), custom_call_target="tpu_custom_call" | custom-call | tf_op jit(solution)/shard_map/embed/pallas_call | solution.py:281
  127.7 0.8 copy-done.4
  128.4 28.2 %model.1 = (bf16[32,4,96,128]{3,2,1,0:T(8,128)(2,1)}, bf16[512,512]{1,0:T(8,128)(2,1)}, f32[13,512]{1,0:T(8,128)}) custom-call(bf16[512,512]{1,0:T(8,128)(2,1)} %copy-done.4, s32[2,512]{1,0:T(2,128)} %bitcast.53, f32[13,512]{1,0:T(8,128)} %bitcast.43, f32[13,96]{1,0:T(8,128)} %dw_ref.3, bf16[4,8,80,640]{3,2,1,0:T(8,128)(2,1)} %bitcast.48, ...), custom_call_target="tpu_custom_call" | custom-call | tf_op jit(solution)/shard_map/model/pallas_call | solution.py:519
  156.7 4.1 %all-to-all-start.3 = ((bf16[128,96,128]{2,1,0:T(8,128)(2,1)}), bf16[128,96,128]{2,1,0:T(8,128)(2,1)S(1)}, u32[]{:S(2)}, u32[]{:S(2)}) async-start(bf16[128,96,128]{2,1,0:T(8,128)(2,1)} %bitcast.49), calls=%async_computation.3 | async-start | bytes 6291456 | tf_op jit(solution)/shard_map/all_to_all | solution.py:786
  160.7 1.0 copy-done.6
  161.8 17.0 %spread_grads.1 = bf16[4096,128]{1,0:T(8,128)(2,1)S(1)} custom-call(s32[32768]{0:T(1024)S(1)} %bitcast.41, s32[32]{0:T(128)S(1)} %get-tuple-element.38.hot_ref, bf16[512,512]{1,0:T(8,128)(2,1)S(1)} %copy-done.6), custom_call_target="tpu_custom_call" | custom-call | tf_op jit(solution)/shard_map/spread_grads/pallas_call | solution.py:606
  178.8 1.0 copy-done.2
  179.8 22.7 %all-to-all-done.3.parts_ref = bf16[128,96,128]{2,1,0:T(8,128)(2,1)S(1)} async-done(((bf16[128,96,128]{2,1,0:T(8,128)(2,1)}), bf16[128,96,128]{2,1,0:T(8,128)(2,1)S(1)}, u32[]{:S(2)}, u32[]{:S(2)}) %all-to-all-start.3) | async-done | bytes 3145760 | tf_op jit(solution)/shard_map/all_to_all | solution.py:786
  202.5 4.7 %all-to-all-start.2 = ((bf16[128,32,128]{2,1,0:T(8,128)(2,1)}), bf16[128,32,128]{2,1,0:T(8,128)(2,1)}, u32[]{:S(2)}, u32[]{:S(2)}) async-start(bf16[128,32,128]{2,1,0:T(8,128)(2,1)} %bitcast.36), calls=%async_computation.2 | async-start | bytes 2097152 | tf_op jit(solution)/shard_map/all_to_all | solution.py:786
  207.2 0.9 sum_parts.1
  208.1 0.9 copy-done.3
  209.0 17.4 %all-to-all-done.2 = bf16[128,32,128]{2,1,0:T(8,128)(2,1)} async-done(((bf16[128,32,128]{2,1,0:T(8,128)(2,1)}), bf16[128,32,128]{2,1,0:T(8,128)(2,1)}, u32[]{:S(2)}, u32[]{:S(2)}) %all-to-all-start.2) | async-done | bytes 1048608 | tf_op jit(solution)/shard_map/all_to_all | solution.py:786
  226.4 4.0 %all-to-all-start.4 = ((bf16[32,96,128]{2,1,0:T(8,128)(2,1)}), bf16[32,96,128]{2,1,0:T(8,128)(2,1)S(1)}, u32[]{:S(2)}, u32[]{:S(2)}) async-start(bf16[32,96,128]{2,1,0:T(8,128)(2,1)} %copy-done.3), calls=%async_computation.4 | async-start | bytes 1572864 | tf_op jit(solution)/shard_map/all_to_all | solution.py:786
  230.3 42.3 %scatter_add.1 = f32[26,16,4096]{2,1,0:T(8,128)} custom-call(s32[256,128]{1,0:T(8,128)} %bitcast.39, bf16[4096,128]{1,0:T(8,128)(2,1)} %bitcast.21.grads_ref), custom_call_target="tpu_custom_call" | custom-call | tf_op jit(solution)/shard_map/scatter_add/pallas_call | solution.py:674
  272.6 1.2 unpack.1
  (35 shorter events, 0.2 us)
Async XLA Ops:
  7.2 2.9 %copy-start.7 = (s32[512,26]{0,1:T(8,128)S(1)}, s32[512,26]{0,1:T(8,128)}, u32[]{:S(2)}) copy-start(s32[512,26]{0,1:T(8,128)} %param.16) | copy-start | bytes 159748
  7.2 121.3 %all-gather.3.cloned.1.call-start = ((), (), s32[]{:S(2)}) async-start(), calls=%async_computation.5 | async-start | bytes 4096000 | tf_op jit(solution)/shard_map/all_gather | solution.py:809
  21.2 21.8 %all-to-all-start = ((s32[128,2,128]{2,1,0:T(2,128)}), s32[128,2,128]{2,1,0:T(2,128)S(1)}, u32[]{:S(2)}, u32[]{:S(2)}) async-start(s32[128,2,128]{2,1,0:T(2,128)} %bitcast.3), calls=%async_computation | async-start | bytes 262144 | tf_op jit(solution)/shard_map/all_to_all | solution.py:786
  32.7 3.0 %copy-start.1 = (f32[26,4096,16]{1,2,0:T(8,128)S(1)}, f32[26,4096,16]{1,2,0:T(8,128)}, u32[]{:S(2)}) copy-start(f32[26,4096,16]{1,2,0:T(8,128)} %param.19) | copy-start | bytes 20447236
  40.1 2.8 %copy-start = (f32[13320,128]{1,0:T(8,128)}, f32[13320,128]{1,0:T(8,128)S(1)}, u32[]{:S(2)}) copy-start(f32[13320,128]{1,0:T(8,128)S(1)} %pack_tables.1.table_ref) | copy-start | bytes 20459524
  43.0 35.8 %copy-start.5 = (s32[128,2,128]{2,1,0:T(2,128)}, s32[128,2,128]{2,1,0:T(2,128)S(1)}, u32[]{:S(2)}) copy-start(s32[128,2,128]{2,1,0:T(2,128)S(1)} %all-to-all-done) | copy-start | bytes 393220
  78.8 9.9 %copy-start.12 = (f32[2,64]{1,0:T(2,128)S(1)}, f32[2,64]{1,0:T(2,128)}, u32[]{:S(2)}) copy-start(f32[2,64]{1,0:T(2,128)} %param.29) | copy-start | bytes 1540
  78.8 10.5 %copy-start.13 = (f32[2,64]{1,0:T(2,128)S(1)}, f32[2,64]{1,0:T(2,128)}, u32[]{:S(2)}) copy-start(f32[2,64]{1,0:T(2,128)} %param.30) | copy-start | bytes 1540
  78.8 10.5 %copy-start.14 = (f32[2]{0:T(128)S(1)}, f32[2]{0:T(128)}, u32[]{:S(2)}) copy-start(f32[2]{0:T(128)} %param.31) | copy-start | bytes 28
  78.8 11.2 %copy-start.10 = (f32[2,8]{1,0:T(2,128)S(1)}, f32[2,8]{1,0:T(2,128)}, u32[]{:S(2)}) copy-start(f32[2,8]{1,0:T(2,128)} %param.27) | copy-start | bytes 196
  78.8 11.9 %copy-start.11 = (f32[96]{0:T(128)S(1)}, f32[96]{0:T(128)}, u32[]{:S(2)}) copy-start(f32[96]{0:T(128)} %param.21) | copy-start | bytes 1156
  78.8 29.2 %copy-start.8 = (f32[512,13]{0,1:T(8,128)S(1)}, f32[512,13]{0,1:T(8,128)}, u32[]{:S(2)}) copy-start(f32[512,13]{0,1:T(8,128)} %param.17) | copy-start | bytes 79876
  78.8 29.2 %copy-start.9 = (f32[13,96]{1,0:T(8,128)S(1)}, f32[13,96]{1,0:T(8,128)}, u32[]{:S(2)}) copy-start(f32[13,96]{1,0:T(8,128)} %dw_ref.3) | copy-start | bytes 14980
  78.9 29.2 %all-to-all-start.1 = ((bf16[128,32,128]{2,1,0:T(8,128)(2,1)}), bf16[128,32,128]{2,1,0:T(8,128)(2,1)S(1)}, u32[]{:S(2)}, u32[]{:S(2)}) async-start(bf16[128,32,128]{2,1,0:T(8,128)(2,1)} %bitcast.7), calls=%async_computation.1 | async-start | bytes 2097152 | tf_op jit(solution)/shard_map/all_to_all | solution.py:786
  127.6 0.8 copy-start.4
  156.7 45.8 %all-to-all-start.3 = ((bf16[128,96,128]{2,1,0:T(8,128)(2,1)}), bf16[128,96,128]{2,1,0:T(8,128)(2,1)S(1)}, u32[]{:S(2)}, u32[]{:S(2)}) async-start(bf16[128,96,128]{2,1,0:T(8,128)(2,1)} %bitcast.49), calls=%async_computation.3 | async-start | bytes 6291456 | tf_op jit(solution)/shard_map/all_to_all | solution.py:786
  160.7 1.0 copy-start.6
  178.8 1.0 copy-start.2
  202.5 23.9 %all-to-all-start.2 = ((bf16[128,32,128]{2,1,0:T(8,128)(2,1)}), bf16[128,32,128]{2,1,0:T(8,128)(2,1)}, u32[]{:S(2)}, u32[]{:S(2)}) async-start(bf16[128,32,128]{2,1,0:T(8,128)(2,1)} %bitcast.36), calls=%async_computation.2 | async-start | bytes 2097152 | tf_op jit(solution)/shard_map/all_to_all | solution.py:786
  208.1 0.9 copy-start.3
  226.4 46.3 %all-to-all-start.4 = ((bf16[32,96,128]{2,1,0:T(8,128)(2,1)}), bf16[32,96,128]{2,1,0:T(8,128)(2,1)S(1)}, u32[]{:S(2)}, u32[]{:S(2)}) async-start(bf16[32,96,128]{2,1,0:T(8,128)(2,1)} %copy-done.3), calls=%async_computation.4 | async-start | bytes 1572864 | tf_op jit(solution)/shard_map/all_to_all | solution.py:786
Sparse Core Ops, SparseCore 0:
  10.3 45.5 all-gather.2

commit v3 on v2

--- a/solution.py
+++ b/solution.py
@@ -190,7 +190,47 @@
     ]
 
 
-def look_up_kernel(asked_ref, table_ref, out_ref, rows_v, groups, rows, sem, even, odd):
+def my_index():
+    return lax.axis_index("dp") * lax.axis_size("mp") + lax.axis_index("mp")
+
+
+def place_of(index):
+    return (index // 4, index % 4)
+
+
+def greet_all(me):
+    barrier = pltpu.get_barrier_semaphore()
+
+    def greet(step, carry):
+        pl.semaphore_signal(
+            barrier,
+            inc=1,
+            device_id=place_of((me + step) % OWNERS),
+            device_id_type=pl.DeviceIdType.MESH,
+        )
+        return carry
+
+    lax.fori_loop(1, OWNERS, greet, 0)
+    return barrier
+
+
+def look_up_kernel(
+    asked_ref,
+    table_ref,
+    out_ref,
+    rows_v,
+    groups,
+    rows,
+    sem,
+    even,
+    odd,
+    ready,
+    send_sem,
+    recv_sem,
+    own_sem,
+):
+    me = my_index()
+    barrier = greet_all(me)
     split_wanted(asked_ref, rows_v, groups, rows, sem)
     at_group = sublane_group()
 
@@ -204,21 +244,50 @@
             block = found[pl.ds(half * 128, 128), :].T
             block = jnp.where(at_group == groups[pl.ds(2 * source + half, 1), :], block, 0.0)
             block = jnp.sum(block.reshape(8, EMB, 128), axis=0)
-            out_ref[pl.ds(eight(source * GROUPS + EMB * half, EMB), EMB), :] = block.astype(BF16)
+            ready[pl.ds(eight(source * GROUPS + EMB * half, EMB), EMB), :] = block.astype(BF16)
+
+    def block_of(ref, index):
+        return ref.at[pl.ds(eight(index * GROUPS, GROUPS), GROUPS), :]
+
+    def send(source):
+        pltpu.make_async_remote_copy(
+            src_ref=block_of(ready, source),
+            dst_ref=block_of(out_ref, me),
+            send_sem=send_sem,
+            recv_sem=recv_sem,
+            device_id=place_of(source),
+            device_id_type=pl.DeviceIdType.MESH,
+        ).start()
 
     even[...] = jnp.zeros_like(even)
     odd[...] = jnp.zeros_like(odd)
-    gather(0, even)
+    gather(me, even)
+    gather((me + 1) % OWNERS, odd)
+    pick(me, even)
+    own = pltpu.make_async_copy(block_of(ready, me), block_of(out_ref, me), own_sem)
+    own.start()
+    pl.semaphore_wait(barrier, OWNERS - 1)
 
     def two_sources(step, carry):
-        source = 2 * step
-        gather(source + 1, odd)
-        pick(source, even)
-        gather(jnp.minimum(source + 2, OWNERS - 1), even)
-        pick(source + 1, odd)
-        return carry
-
-    lax.fori_loop(0, OWNERS // 2, two_sources, 0)
+        first = (me + 2 * step + 1) % OWNERS
+        second = (me + 2 * step + 2) % OWNERS
+        third = (me + 2 * step + 3) % OWNERS
+        gather(second, even)
+        pick(first, odd)
+        send(first)
+        gather(third, odd)
+        pick(second, even)
+        send(second)
+        return carry
+
+    lax.fori_loop(0, OWNERS // 2 - 1, two_sources, 0)
+    last = (me + OWNERS - 1) % OWNERS
+    pick(last, odd)
+    send(last)
+    own.wait()
+    every = pl.ds(0, (OWNERS - 1) * GROUPS)
+    pltpu.make_async_copy(ready.at[every, :], ready.at[every, :], send_sem).wait()
+    pltpu.make_async_copy(out_ref.at[every, :], out_ref.at[every, :], recv_sem).wait()
 
 
 def look_up(asked, table):
@@ -227,8 +296,13 @@
         in_specs=[VM, VM],
         out_specs=VM,
         out_shape=shape((OWNERS * GROUPS, 128), BF16),
-        scratch_shapes=split_scratch() + [pltpu.VMEM((SLOTS, 128), F32)] * 2,
-        compiler_params=params(48),
+        scratch_shapes=split_scratch()
+        + [pltpu.VMEM((SLOTS, 128), F32)] * 2
+        + [pltpu.VMEM((OWNERS * GROUPS, 128), BF16)]
+        + [pltpu.SemaphoreType.DMA] * 3,
+        compiler_params=pltpu.CompilerParams(
+            vmem_limit_bytes=48 * 1024 * 1024, collective_id=0, has_side_effects=True
+        ),
         name="look_up",
     )(asked, table)
 
@@ -820,7 +894,7 @@
     asked = exchange(requests, ALL)
     sources = sources.reshape(-1)
     table = pack_tables(tables.transpose(0, 2, 1))
-    answer = exchange(look_up(asked, table), ALL)
+    answer = look_up(asked, table)
     feats_t = dense_feats.T
     inputs = embed(sources, hot, ids, answer, feats_t, dense_w, dense_b.reshape(DPROJ, 1))
     task_at = lax.broadcasted_iota(jnp.int32, (TASKS, TASKS * THID), 1) // THID

time: 281 us -> 262 us (0.932)
  waiting for transfers between devices: 56.8 us -> 40.1 us
  starting transfers between devices: 34 us -> 28.1 us
  Pallas kernels: 153 us -> 156 us
    all_to_all x5 -> x4, waiting for transfers between devices: 56.8 us -> 40.1 us  [exchange(): return lax.all_to_all(value, axes, split_axis=0, concat_axis=0, tiled=True)]
    all_to_all x5 -> x4, starting transfers between devices: 34 us -> 28 us  [exchange(): return lax.all_to_all(value, axes, split_axis=0, concat_axis=0, tiled=True)]
    pallas_call x1, Pallas kernels: 35.8 us -> 39 us  [look_up(): pl.pallas_call(look_up_kernel, in_specs=[VM, VM], out_specs=VM, out_shape...]
  transfers between devices with their start and end apart: 6 -> 5, of which waited for: 3 -> 2; matrix products, arithmetic and copies ran while one was open for 4% -> 4% of each run, Pallas kernels for 44% -> 49%
where the time goes in v3:
time: 262 us; the launch traced here: 261 us
  Pallas kernels  156 us (60%)
  waiting for transfers between devices  40.1 us (15%)
  starting transfers between devices  28.1 us (11%)
  between operations  14.3 us (5%)
  local copies, waits for them, and re-layouts  12.3 us (5%)
  other arithmetic  10.1 us (4%)
    pallas_call x1, Pallas kernels, scatter_add(): pl.pallas_call(scatter_kernel, in_specs=[VM, VM], out_specs=VM, out_shape...  42.3 us
    all_to_all x4, waiting for transfers between devices, exchange(): return lax.all_to_all(value, axes, split_axis=0, concat_axis=0, tiled=True)  40.1 us
    pallas_call x1, Pallas kernels, look_up(): pl.pallas_call(look_up_kernel, in_specs=[VM, VM], out_specs=VM, out_shape...  39 us
    pallas_call x1, Pallas kernels, model(): pl.pallas_call(model_kernel, grid=(3,), in_specs=[VM] * len(operands), ou...  28.2 us
    all_to_all x4, starting transfers between devices, exchange(): return lax.all_to_all(value, axes, split_axis=0, concat_axis=0, tiled=True)  28 us
    pallas_call x1, Pallas kernels, embed(): pl.pallas_call(embed_kernel, in_specs=[SM, SM, VM, VM, VM, VM, VM], out_s...  19.6 us
    pallas_call x1, Pallas kernels, spread_grads(): pl.pallas_call(spread_kernel, in_specs=[SM, SM, VM], out_specs=VM, out_sh...  17 us
    unnamed x31, local copies, waits for them, and re-layouts  10.2 us
  transfers between devices with their start and end apart: 5, of which 2 were waited for; matrix products, arithmetic and copies ran while one was open for 4% of the time, Pallas kernels for 49%

profile of v3, /device:TPU:1, one launch (start us, length us, event | category | flops | bytes accessed | tf_op | source)
XLA Modules:
  0.0 261.2 jit_solution(5586798137284395062)
XLA Ops:
  7.2 0.0 all-gather.3.cloned.1.call-start
  7.3 0.7 copy.41
  8.0 2.1 fusion.1
  10.1 0.1 and_or_fusion
  10.2 7.4 %sort.15 = (s32[13312]{0:T(1024)S(1)}, s32[13312]{0:T(1024)S(1)}) sort(s32[13312]{0:T(1024)S(1)} %reshape.79, s32[13312]{0:T(1024)S(1)} %reshape.80), dimensions={0}, to_apply=%region_0.1 | sort | flops 186368 | bytes 212992 | tf_op jit(solution)/shard_map/sort | solution.py:892
  17.6 3.6 %route.1 = (s32[256,128]{1,0:T(8,128)}, s32[256,128]{1,0:T(8,128)S(1)}, s32[32]{0:T(128)S(1)}) custom-call(s32[104,128]{1,0:T(8,128)S(1)} %bitcast.42, s32[104,128]{1,0:T(8,128)S(1)} %bitcast.43), custom_call_target="tpu_custom_call" | custom-call | tf_op jit(solution)/shard_map/route/pallas_call | solution.py:135
  21.3 11.5 %all-to-all-start = ((s32[128,2,128]{2,1,0:T(2,128)}), s32[128,2,128]{2,1,0:T(2,128)S(1)}, u32[]{:S(2)}, u32[]{:S(2)}) async-start(s32[128,2,128]{2,1,0:T(2,128)} %bitcast.3), calls=%async_computation | async-start | bytes 262144 | tf_op jit(solution)/shard_map/all_to_all | solution.py:860
  32.8 0.6 reshape.88.b1_ref
  33.4 0.1 broadcast_in_dim.18
  33.5 0.6 copy.40.b2_ref
  34.1 0.7 reshape.95.gate_b_ref
  34.8 0.1 copy.37.db_ref
  34.9 3.0 %copy-done.1 = f32[26,4096,16]{1,2,0:T(8,128)S(1)} copy-done((f32[26,4096,16]{1,2,0:T(8,128)S(1)}, f32[26,4096,16]{1,2,0:T(8,128)}, u32[]{:S(2)}) %copy-start.1) | copy-done | bytes 6815768
  37.9 4.4 %pack_tables.1.table_ref = f32[13320,128]{1,0:T(8,128)S(1)} custom-call(f32[26,16,4096]{2,1,0:T(8,128)S(1)} %bitcast.33), custom_call_target="tpu_custom_call" | custom-call | tf_op jit(solution)/shard_map/pack_tables/pallas_call | solution.py:165
  42.3 2.8 %copy-done = f32[13320,128]{1,0:T(8,128)} copy-done((f32[13320,128]{1,0:T(8,128)}, f32[13320,128]{1,0:T(8,128)S(1)}, u32[]{:S(2)}) %copy-start) | copy-done | bytes 6819864
  45.1 0.6 compare_select_fusion.w2_ref
  45.7 39.0 %look_up.1.answer_ref = bf16[4096,128]{1,0:T(8,128)(2,1)S(1)} custom-call(s32[256,128]{1,0:T(8,128)S(1)} %bitcast.35, f32[13320,128]{1,0:T(8,128)} %copy-done), custom_call_target="tpu_custom_call" | custom-call | tf_op jit(solution)/shard_map/look_up/pallas_call | solution.py:294
  84.8 19.6 %embed.1.x_ref = bf16[512,512]{1,0:T(8,128)(2,1)S(1)} custom-call(s32[32768]{0:T(1024)S(1)} %bitcast.37, s32[32]{0:T(128)S(1)} %get-tuple-element.38.hot_ref, s32[26,512]{1,0:T(8,128)S(1)} %bitcast.39, bf16[4096,128]{1,0:T(8,128)(2,1)S(1)} %look_up.1.answer_ref, f32[13,512]{1,0:T(8,128)S(1)} %bitcast.41, f32[13,96]{1,0:T(8,128)S(1)} %copy-done.9, ...), custom_call_target="tpu_custom_call" | custom-call | tf_op jit(solution)/shard_map/embed/pallas_call | solution.py:355
  104.4 0.8 copy-done.4
  105.1 28.2 %model.1 = (bf16[32,4,96,128]{3,2,1,0:T(8,128)(2,1)}, bf16[512,512]{1,0:T(8,128)(2,1)}, f32[13,512]{1,0:T(8,128)}) custom-call(bf16[512,512]{1,0:T(8,128)(2,1)} %copy-done.4, s32[2,512]{1,0:T(2,128)} %bitcast.50, f32[13,512]{1,0:T(8,128)} %bitcast.40, f32[13,96]{1,0:T(8,128)} %dw_ref.3, bf16[4,8,80,640]{3,2,1,0:T(8,128)(2,1)} %bitcast.45, ...), custom_call_target="tpu_custom_call" | custom-call | tf_op jit(solution)/shard_map/model/pallas_call | solution.py:593
  133.4 7.9 %all-to-all-start.2 = ((bf16[128,96,128]{2,1,0:T(8,128)(2,1)}), bf16[128,96,128]{2,1,0:T(8,128)(2,1)S(1)}, u32[]{:S(2)}, u32[]{:S(2)}) async-start(bf16[128,96,128]{2,1,0:T(8,128)(2,1)} %bitcast.46), calls=%async_computation.2 | async-start | bytes 6291456 | tf_op jit(solution)/shard_map/all_to_all | solution.py:860
  141.3 1.0 copy-done.6
  142.3 17.0 %spread_grads.1 = bf16[4096,128]{1,0:T(8,128)(2,1)S(1)} custom-call(s32[32768]{0:T(1024)S(1)} %bitcast.38, s32[32]{0:T(128)S(1)} %get-tuple-element.38.hot_ref, bf16[512,512]{1,0:T(8,128)(2,1)S(1)} %copy-done.6), custom_call_target="tpu_custom_call" | custom-call | tf_op jit(solution)/shard_map/spread_grads/pallas_call | solution.py:680
  159.3 1.0 copy-done.2
  160.3 22.7 %all-to-all-done.2.parts_ref = bf16[128,96,128]{2,1,0:T(8,128)(2,1)S(1)} async-done(((bf16[128,96,128]{2,1,0:T(8,128)(2,1)}), bf16[128,96,128]{2,1,0:T(8,128)(2,1)S(1)}, u32[]{:S(2)}, u32[]{:S(2)}) %all-to-all-start.2) | async-done | bytes 3145760 | tf_op jit(solution)/shard_map/all_to_all | solution.py:860
  183.0 4.7 %all-to-all-start.1 = ((bf16[128,32,128]{2,1,0:T(8,128)(2,1)}), bf16[128,32,128]{2,1,0:T(8,128)(2,1)}, u32[]{:S(2)}, u32[]{:S(2)}) async-start(bf16[128,32,128]{2,1,0:T(8,128)(2,1)} %bitcast.34), calls=%async_computation.1 | async-start | bytes 2097152 | tf_op jit(solution)/shard_map/all_to_all | solution.py:860
  187.7 0.9 sum_parts.1
  188.6 0.9 copy-done.3
  189.5 17.4 %all-to-all-done.1 = bf16[128,32,128]{2,1,0:T(8,128)(2,1)} async-done(((bf16[128,32,128]{2,1,0:T(8,128)(2,1)}), bf16[128,32,128]{2,1,0:T(8,128)(2,1)}, u32[]{:S(2)}, u32[]{:S(2)}) %all-to-all-start.1) | async-done | bytes 1048608 | tf_op jit(solution)/shard_map/all_to_all | solution.py:860
  206.9 4.0 %all-to-all-start.3 = ((bf16[32,96,128]{2,1,0:T(8,128)(2,1)}), bf16[32,96,128]{2,1,0:T(8,128)(2,1)S(1)}, u32[]{:S(2)}, u32[]{:S(2)}) async-start(bf16[32,96,128]{2,1,0:T(8,128)(2,1)} %copy-done.3), calls=%async_computation.3 | async-start | bytes 1572864 | tf_op jit(solution)/shard_map/all_to_all | solution.py:860
  210.8 42.3 %scatter_add.1 = f32[26,16,4096]{2,1,0:T(8,128)} custom-call(s32[256,128]{1,0:T(8,128)} %bitcast.36, bf16[4096,128]{1,0:T(8,128)(2,1)} %bitcast.19.grads_ref), custom_call_target="tpu_custom_call" | custom-call | tf_op jit(solution)/shard_map/scatter_add/pallas_call | solution.py:748
  253.2 1.2 unpack.1
  (33 shorter events, 0.1 us)
Async XLA Ops:
  7.2 2.9 %copy-start.7 = (s32[512,26]{0,1:T(8,128)S(1)}, s32[512,26]{0,1:T(8,128)}, u32[]{:S(2)}) copy-start(s32[512,26]{0,1:T(8,128)} %param.16) | copy-start | bytes 159748
  7.2 25.6 %copy-start.12 = (f32[2,64]{1,0:T(2,128)S(1)}, f32[2,64]{1,0:T(2,128)}, u32[]{:S(2)}) copy-start(f32[2,64]{1,0:T(2,128)} %param.29) | copy-start | bytes 1540
  7.2 26.2 %copy-start.13 = (f32[2,64]{1,0:T(2,128)S(1)}, f32[2,64]{1,0:T(2,128)}, u32[]{:S(2)}) copy-start(f32[2,64]{1,0:T(2,128)} %param.30) | copy-start | bytes 1540
  7.2 26.2 %copy-start.14 = (f32[2]{0:T(128)S(1)}, f32[2]{0:T(128)}, u32[]{:S(2)}) copy-start(f32[2]{0:T(128)} %param.31) | copy-start | bytes 28
  7.2 26.9 %copy-start.10 = (f32[2,8]{1,0:T(2,128)S(1)}, f32[2,8]{1,0:T(2,128)}, u32[]{:S(2)}) copy-start(f32[2,8]{1,0:T(2,128)} %param.27) | copy-start | bytes 196
  7.2 27.6 %copy-start.11 = (f32[96]{0:T(128)S(1)}, f32[96]{0:T(128)}, u32[]{:S(2)}) copy-start(f32[96]{0:T(128)} %param.21) | copy-start | bytes 1156
  7.2 97.9 %all-gather.3.cloned.1.call-start = ((), (), s32[]{:S(2)}) async-start(), calls=%async_computation.4 | async-start | bytes 4096000 | tf_op jit(solution)/shard_map/all_gather | solution.py:883
  21.3 24.5 %all-to-all-start = ((s32[128,2,128]{2,1,0:T(2,128)}), s32[128,2,128]{2,1,0:T(2,128)S(1)}, u32[]{:S(2)}, u32[]{:S(2)}) async-start(s32[128,2,128]{2,1,0:T(2,128)} %bitcast.3), calls=%async_computation | async-start | bytes 262144 | tf_op jit(solution)/shard_map/all_to_all | solution.py:860
  34.9 3.0 %copy-start.1 = (f32[26,4096,16]{1,2,0:T(8,128)S(1)}, f32[26,4096,16]{1,2,0:T(8,128)}, u32[]{:S(2)}) copy-start(f32[26,4096,16]{1,2,0:T(8,128)} %param.19) | copy-start | bytes 20447236
  42.3 2.8 %copy-start = (f32[13320,128]{1,0:T(8,128)}, f32[13320,128]{1,0:T(8,128)S(1)}, u32[]{:S(2)}) copy-start(f32[13320,128]{1,0:T(8,128)S(1)} %pack_tables.1.table_ref) | copy-start | bytes 20459524
  45.7 39.0 %copy-start.5 = (s32[128,2,128]{2,1,0:T(2,128)}, s32[128,2,128]{2,1,0:T(2,128)S(1)}, u32[]{:S(2)}) copy-start(s32[128,2,128]{2,1,0:T(2,128)S(1)} %all-to-all-done) | copy-start | bytes 393220
  45.7 39.0 %copy-start.8 = (f32[512,13]{0,1:T(8,128)S(1)}, f32[512,13]{0,1:T(8,128)}, u32[]{:S(2)}) copy-start(f32[512,13]{0,1:T(8,128)} %param.17) | copy-start | bytes 79876
  45.7 39.0 %copy-start.9 = (f32[13,96]{1,0:T(8,128)S(1)}, f32[13,96]{1,0:T(8,128)}, u32[]{:S(2)}) copy-start(f32[13,96]{1,0:T(8,128)} %dw_ref.3) | copy-start | bytes 14980
  104.4 0.8 copy-start.4
  133.4 49.6 %all-to-all-start.2 = ((bf16[128,96,128]{2,1,0:T(8,128)(2,1)}), bf16[128,96,128]{2,1,0:T(8,128)(2,1)S(1)}, u32[]{:S(2)}, u32[]{:S(2)}) async-start(bf16[128,96,128]{2,1,0:T(8,128)(2,1)} %bitcast.46), calls=%async_computation.2 | async-start | bytes 6291456 | tf_op jit(solution)/shard_map/all_to_all | solution.py:860
  141.2 1.0 copy-start.6
  159.3 1.0 copy-start.2
  183.0 23.9 %all-to-all-start.1 = ((bf16[128,32,128]{2,1,0:T(8,128)(2,1)}), bf16[128,32,128]{2,1,0:T(8,128)(2,1)}, u32[]{:S(2)}, u32[]{:S(2)}) async-start(bf16[128,32,128]{2,1,0:T(8,128)(2,1)} %bitcast.34), calls=%async_computation.1 | async-start | bytes 2097152 | tf_op jit(solution)/shard_map/all_to_all | solution.py:860
  188.6 0.9 copy-start.3
  206.9 46.3 %all-to-all-start.3 = ((bf16[32,96,128]{2,1,0:T(8,128)(2,1)}), bf16[32,96,128]{2,1,0:T(8,128)(2,1)S(1)}, u32[]{:S(2)}, u32[]{:S(2)}) async-start(bf16[32,96,128]{2,1,0:T(8,128)(2,1)} %copy-done.3), calls=%async_computation.3 | async-start | bytes 1572864 | tf_op jit(solution)/shard_map/all_to_all | solution.py:860
Sparse Core Ops, SparseCore 0:
  10.3 45.4 all-gather.2

commit v4 on v3

--- a/solution.py
+++ b/solution.py
@@ -34,7 +34,7 @@
 DPROJ = 96
 CHUNK = 80
 TILES = 32
-SENT = CHUNK + 16
+CHIPS = OWNERS // 2
 PART = 64
 SUMS = 6
 
@@ -88,7 +88,71 @@
     return high, mid, low
 
 
-def route_kernel(key_ref, load_ref, req_ref, src_ref, hot_ref, both, cut, starts_v, starts, sem):
+def my_index():
+    return lax.axis_index("dp") * lax.axis_size("mp") + lax.axis_index("mp")
+
+
+def place_of(index):
+    return (index // 4, index % 4)
+
+
+def greet_all(me):
+    barrier = pltpu.get_barrier_semaphore()
+
+    def greet(step, carry):
+        pl.semaphore_signal(
+            barrier,
+            inc=1,
+            device_id=place_of((me + step) % OWNERS),
+            device_id_type=pl.DeviceIdType.MESH,
+        )
+        return carry
+
+    lax.fori_loop(1, OWNERS, greet, 0)
+    return barrier
+
+
+def block_of(ref, index):
+    return ref.at[pl.ds(eight(index * GROUPS, GROUPS), GROUPS), :]
+
+
+def send_block(ready, landing, me, dest, send_sem, recv_sem):
+    pltpu.make_async_remote_copy(
+        src_ref=block_of(ready, dest),
+        dst_ref=block_of(landing, me),
+        send_sem=send_sem,
+        recv_sem=recv_sem,
+        device_id=place_of(dest),
+        device_id_type=pl.DeviceIdType.MESH,
+    ).start()
+
+
+def wait_blocks(ready, landing, send_sem, recv_sem):
+    every = pl.ds(0, (OWNERS - 1) * GROUPS)
+    pltpu.make_async_copy(ready.at[every, :], ready.at[every, :], send_sem).wait()
+    pltpu.make_async_copy(landing.at[every, :], landing.at[every, :], recv_sem).wait()
+
+
+def remote_params(mib, identity):
+    return pltpu.CompilerParams(
+        vmem_limit_bytes=mib * 1024 * 1024, collective_id=identity, has_side_effects=True
+    )
+
+
+def route_kernel(
+    key_ref,
+    load_ref,
+    req_ref,
+    src_ref,
+    hot_src_ref,
+    hot_ref,
+    hot_at_ref,
+    both,
+    cut,
+    starts_v,
+    starts,
+    sem,
+):
     own = (key_ref[...] & 16383) << 17
     both[pl.ds(0, 104), :] = own | load_ref[...]
     both[pl.ds(104, 8), :] = jnp.zeros((8, 128), jnp.int32)
@@ -120,26 +184,30 @@
         for half in range(2):
             piece = jnp.where(lane >= off, pieces[half], pieces[half + 1])
             piece = pltpu.roll(piece, (128 - off) & 127, 1)
-            cut[pl.ds(2 * owner + half, 1), :] = jnp.where(
-                lane < end - start - 128 * half, piece, unused
-            )
+            piece = jnp.where(lane < end - start - 128 * half, piece, unused)
+            cut[pl.ds(2 * owner + half, 1), :] = piece
+            hot_src_ref[pl.ds(2 * hot_count + half, 1), :] = piece >> 17
+        is_hot = end - start > COLD
         hot_ref[hot_count] = owner
-        return jnp.minimum(hot_count + (end - start > COLD).astype(jnp.int32), 2 * HOT - 1)
+        hot_at_ref[owner] = jnp.where(is_hot & (hot_count < HOT), hot_count, HOT)
+        return jnp.minimum(hot_count + is_hot.astype(jnp.int32), 2 * HOT - 1)
 
     lax.fori_loop(0, OWNERS, per_owner, 0, unroll=8)
     src_ref[...] = cut[...] >> 17
-    req_ref[...] = cut[...] & ((1 << 17) - 1)
+    req_ref[...] = (cut[...] & ((1 << 17) - 1)).reshape(OWNERS, 2, 128)
 
 
 def route(keys, loads):
     return pl.pallas_call(
         route_kernel,
         in_specs=[VM, VM],
-        out_specs=[VM, VM, SM],
+        out_specs=[VM, VM, VM, SM, SM],
         out_shape=[
+            shape((OWNERS, 2, 128), jnp.int32),
             shape((2 * OWNERS, 128), jnp.int32),
-            shape((2 * OWNERS, 128), jnp.int32),
+            shape((4 * HOT, 128), jnp.int32),
             shape((2 * HOT,), jnp.int32),
+            shape((OWNERS,), jnp.int32),
         ],
         scratch_shapes=[
             pltpu.VMEM((112, 128), jnp.int32),
@@ -153,26 +221,6 @@
     )(keys, loads)
 
 
-def pack_kernel(table_ref, out_ref):
-    for part in range(4):
-        block = jnp.concatenate(
-            [table_ref[0, :, pl.ds(part * 1024 + k * 128, 128)] for k in range(8)], axis=0
-        )
-        out_ref[pl.ds(part * 128, 128), :] = block.T
-
-
-def pack_tables(tables_t):
-    return pl.pallas_call(
-        pack_kernel,
-        grid=(FIELDS,),
-        in_specs=[pl.BlockSpec((1, EMB, ROWS_DEV), lambda f: (f, 0, 0))],
-        out_specs=pl.BlockSpec((512, 128), lambda f: (f, 0)),
-        out_shape=shape((PACKED + 8, 128), F32),
-        compiler_params=params(32),
-        name="pack_tables",
-    )(tables_t)
-
-
 def split_wanted(asked_ref, rows_v, groups, rows, sem):
     rows_v[...] = asked_ref[...] >> 3
     copy = pltpu.make_async_copy(rows_v, rows, sem)
@@ -183,41 +231,20 @@
 
 def split_scratch():
     return [
-        pltpu.VMEM((2 * OWNERS, 128), jnp.int32),
-        pltpu.VMEM((2 * OWNERS, 128), jnp.int32),
-        pltpu.SMEM((2 * OWNERS, 128), jnp.int32),
+        pltpu.VMEM((OWNERS, 2, 128), jnp.int32),
+        pltpu.VMEM((OWNERS, 2, 128), jnp.int32),
+        pltpu.SMEM((OWNERS, 2, 128), jnp.int32),
         pltpu.SemaphoreType.DMA,
     ]
 
 
-def my_index():
-    return lax.axis_index("dp") * lax.axis_size("mp") + lax.axis_index("mp")
-
-
-def place_of(index):
-    return (index // 4, index % 4)
-
-
-def greet_all(me):
-    barrier = pltpu.get_barrier_semaphore()
-
-    def greet(step, carry):
-        pl.semaphore_signal(
-            barrier,
-            inc=1,
-            device_id=place_of((me + step) % OWNERS),
-            device_id_type=pl.DeviceIdType.MESH,
-        )
-        return carry
-
-    lax.fori_loop(1, OWNERS, greet, 0)
-    return barrier
-
-
 def look_up_kernel(
+    wanted_ref,
+    tables_ref,
+    out_ref,
     asked_ref,
-    table_ref,
-    out_ref,
+    fields,
+    table,
     rows_v,
     groups,
     rows,
@@ -225,39 +252,74 @@
     even,
     odd,
     ready,
+    field_sem,
+    ask_send,
+    ask_recv,
     send_sem,
     recv_sem,
     own_sem,
 ):
     me = my_index()
+
+    def field_copy(field):
+        return pltpu.make_async_copy(
+            tables_ref.at[field], fields.at[field], field_sem.at[field]
+        )
+
+    def start_field(field, carry):
+        field_copy(field).start()
+        return carry
+
+    lax.fori_loop(0, FIELDS, start_field, 0)
     barrier = greet_all(me)
+
+    def pack(field, carry):
+        field_copy(field).wait()
+        for part in range(4):
+            block = jnp.concatenate(
+                [fields[field, :, pl.ds(part * 1024 + k * 128, 128)] for k in range(8)], axis=0
+            )
+            table[pl.ds(eight(field * 512 + part * 128, 128), 128), :] = block.T
+        return carry
+
+    lax.fori_loop(0, 8, pack, 0)
+    table[pl.ds(PACKED, 8), :] = jnp.zeros((8, 128), F32)
+    asked_ref[me] = wanted_ref[me]
+    pl.semaphore_wait(barrier, OWNERS - 1)
+
+    def ask(step, carry):
+        owner = (me + step) % OWNERS
+        pltpu.make_async_remote_copy(
+            src_ref=wanted_ref.at[owner],
+            dst_ref=asked_ref.at[me],
+            send_sem=ask_send,
+            recv_sem=ask_recv,
+            device_id=place_of(owner),
+            device_id_type=pl.DeviceIdType.MESH,
+        ).start()
+        return carry
+
+    lax.fori_loop(1, OWNERS, ask, 0)
+    lax.fori_loop(8, FIELDS, pack, 0)
+    others = pl.ds(0, OWNERS - 1)
+    pltpu.make_async_copy(asked_ref.at[others], asked_ref.at[others], ask_recv).wait()
     split_wanted(asked_ref, rows_v, groups, rows, sem)
     at_group = sublane_group()
 
     def gather(source, found):
         for n in range(CAP):
-            at = rows[2 * source + n // 128, n % 128]
-            found[pl.ds(n, 1), :] = table_ref[pl.ds(at, 1), :]
+            at = rows[source, n // 128, n % 128]
+            found[pl.ds(n, 1), :] = table[pl.ds(at, 1), :]
 
     def pick(source, found):
         for half in range(2):
             block = found[pl.ds(half * 128, 128), :].T
-            block = jnp.where(at_group == groups[pl.ds(2 * source + half, 1), :], block, 0.0)
+            block = jnp.where(at_group == groups[source, pl.ds(half, 1), :], block, 0.0)
             block = jnp.sum(block.reshape(8, EMB, 128), axis=0)
             ready[pl.ds(eight(source * GROUPS + EMB * half, EMB), EMB), :] = block.astype(BF16)
 
-    def block_of(ref, index):
-        return ref.at[pl.ds(eight(index * GROUPS, GROUPS), GROUPS), :]
-
     def send(source):
-        pltpu.make_async_remote_copy(
-            src_ref=block_of(ready, source),
-            dst_ref=block_of(out_ref, me),
-            send_sem=send_sem,
-            recv_sem=recv_sem,
-            device_id=place_of(source),
-            device_id_type=pl.DeviceIdType.MESH,
-        ).start()
+        send_block(ready, out_ref, me, source, send_sem, recv_sem)
 
     even[...] = jnp.zeros_like(even)
     odd[...] = jnp.zeros_like(odd)
@@ -266,7 +328,6 @@
     pick(me, even)
     own = pltpu.make_async_copy(block_of(ready, me), block_of(out_ref, me), own_sem)
     own.start()
-    pl.semaphore_wait(barrier, OWNERS - 1)
 
     def two_sources(step, carry):
         first = (me + 2 * step + 1) % OWNERS
@@ -285,26 +346,31 @@
     pick(last, odd)
     send(last)
     own.wait()
-    every = pl.ds(0, (OWNERS - 1) * GROUPS)
-    pltpu.make_async_copy(ready.at[every, :], ready.at[every, :], send_sem).wait()
-    pltpu.make_async_copy(out_ref.at[every, :], out_ref.at[every, :], recv_sem).wait()
-
-
-def look_up(asked, table):
+    pltpu.make_async_copy(wanted_ref.at[others], wanted_ref.at[others], ask_send).wait()
+    wait_blocks(ready, out_ref, send_sem, recv_sem)
+
+
+def look_up(wanted, tables_t):
     return pl.pallas_call(
         look_up_kernel,
-        in_specs=[VM, VM],
-        out_specs=VM,
-        out_shape=shape((OWNERS * GROUPS, 128), BF16),
-        scratch_shapes=split_scratch()
+        in_specs=[VM, pl.BlockSpec(memory_space=pl.ANY)],
+        out_specs=[VM, VM],
+        out_shape=[
+            shape((OWNERS * GROUPS, 128), BF16),
+            shape((OWNERS, 2, 128), jnp.int32),
+        ],
+        scratch_shapes=[
+            pltpu.VMEM((FIELDS, EMB, ROWS_DEV), F32),
+            pltpu.VMEM((PACKED + 8, 128), F32),
+        ]
+        + split_scratch()
         + [pltpu.VMEM((SLOTS, 128), F32)] * 2
         + [pltpu.VMEM((OWNERS * GROUPS, 128), BF16)]
-        + [pltpu.SemaphoreType.DMA] * 3,
-        compiler_params=pltpu.CompilerParams(
-            vmem_limit_bytes=48 * 1024 * 1024, collective_id=0, has_side_effects=True
-        ),
+        + [pltpu.SemaphoreType.DMA((FIELDS,))]
+        + [pltpu.SemaphoreType.DMA] * 5,
+        compiler_params=remote_params(48, 0),
         name="look_up",
-    )(asked, table)
+    )(wanted, tables_t)
 
 
 def embed_kernel(
@@ -379,16 +445,6 @@
     return value * half, slope
 
 
-def two_parts(value):
-    high = value.astype(BF16).astype(F32)
-    return jnp.concatenate([high, value - high], axis=0).astype(BF16)
-
-
-def one_of(parts):
-    wide = parts.astype(F32)
-    return wide[0:8] + wide[8:16]
-
-
 def model_kernel(
     x_ref,
     labels_ref,
@@ -402,11 +458,15 @@
     b1_ref,
     w2_ref,
     b2_ref,
-    grads_ref,
-    d_low_ref,
+    src_ref,
+    hot_src_ref,
+    hot_at_ref,
+    rows_out_ref,
+    experts_out_ref,
+    small_out_ref,
     grad_dense_ref,
     small_ref,
-    small_b,
+    small_two,
     d_in_ref,
     hidden,
     slope,
@@ -417,9 +477,32 @@
     prod_lo,
     mix,
     stage,
+    own_grad,
+    pair_send,
+    pair_recv,
+    share_send,
+    share_recv,
+    small_recv,
+    experts_own,
+    experts_all,
+    small_own,
+    small_all,
+    rows,
+    hot_rows,
+    even,
+    odd,
+    ready,
+    landing,
+    pair_sems,
+    sems,
 ):
     x = x_ref[...]
     phase = pl.program_id(0)
+    line = lax.axis_index("dp")
+    part = lax.axis_index("mp")
+    core = line % 2
+    chip = line // 2 * 4 + part
+    me = my_index()
 
     def weights_in(k):
         return jnp.concatenate(
@@ -528,7 +611,7 @@
         lane = lax.broadcasted_iota(jnp.int32, (1, 128), 1)
         small_ref[pl.ds(218, 1), :] = jnp.where(lane < THID, grad_w2[0:1], grad_w2[1:2])
         small_ref[pl.ds(219, 1), :] = jnp.zeros((1, 128), F32)
-        small_b[...] = jnp.zeros_like(small_b)
+        small_ref[pl.ds(240, 16 + 32), :] = jnp.zeros((48, 128), F32)
         small_ref[pl.ds(220, 2), :] = jnp.broadcast_to(
             jnp.sum(d_logit, axis=1, keepdims=True), (2, 128)
         )
@@ -537,25 +620,75 @@
             jnp.sum(d_logits, axis=1, keepdims=True), (16, 128)
         )
 
-    def backward(k, carry):
+    def backward(k, store):
         d_out = d_raw[k]
-        grad_out = dot_tn(hidden[k], d_out).astype(BF16)
+        grad_out = dot_tn(hidden[k], d_out)
         d_pre = (dot_nt(d_out, weights_out(k)) * slope[k]).astype(BF16)
         bias = jnp.sum(d_pre.astype(F32), axis=0, keepdims=True)
         for p in range(4):
-            small_b[p, pl.ds(k, 1), pl.ds(0, PART)] = bias[:, PART * p : PART * p + PART]
-        grad_in = dot_tn(d_pre, x).astype(BF16)
-        for part in range(4):
-            for block in range(5):
-                for piece in range(4):
-                    at = block * 64 + piece * 16
-                    rows = slice(part * 64 + piece * 16, part * 64 + piece * 16 + 16)
-                    if block < 4:
-                        value = grad_in[rows, block * 128 : block * 128 + 128]
-                    else:
-                        value = grad_out[rows, :]
-                    grads_ref[4 * k + at // CHUNK, part, pl.ds(at % CHUNK, 16), :] = value
+            small_ref[pl.ds(8 * (TILES + p) + k, 1), pl.ds(0, PART)] = bias[
+                :, PART * p : PART * p + PART
+            ]
+        grad_in = dot_tn(d_pre, x)
+        for p in range(4):
+            at = slice(PART * p, PART * p + PART)
+            for block in range(4):
+                store(p, block, grad_in[at, block * 128 : block * 128 + 128])
+            store(p, 4, grad_out[at, :])
         d_in_ref[...] += dot_nn(d_pre, weights_in(k))
+
+    def remote(source, target, sem, place):
+        return pltpu.make_async_remote_copy(
+            src_ref=source,
+            dst_ref=target,
+            send_sem=sems.at[sem],
+            recv_sem=sems.at[sem + 1],
+            device_id=place,
+            device_id_type=pl.DeviceIdType.MESH,
+        )
+
+    def wait_all(ref, sem):
+        pltpu.make_async_copy(ref, ref, sem).wait()
+
+    def experts(step, carry):
+        q = (step + line // 2 + part) % 4
+
+        def for_pair(p, block, value):
+            pair_send[q, p, pl.ds(PART * block, PART), :] = value.astype(BF16)
+
+        def for_own(p, block, value):
+            own_grad[p, pl.ds(PART * block, PART), :] = value
+
+        backward(2 * q + 1 - core, for_pair)
+        pair = pltpu.make_async_remote_copy(
+            src_ref=pair_send.at[q],
+            dst_ref=pair_recv.at[q],
+            send_sem=sems.at[0],
+            recv_sem=pair_sems.at[q],
+            device_id=(line + 1 - 2 * core, part),
+            device_id_type=pl.DeviceIdType.MESH,
+        )
+        pair.start()
+        backward(2 * q + core, for_own)
+        pair.wait_recv()
+        for p in range(4):
+            total = own_grad[p] + pair_recv[q, p].astype(F32)
+            share_send[q, p] = total.astype(BF16).reshape(4, CHUNK, 128)
+        for r in range(4):
+            for p in range(4):
+                target = 2 * (4 * q + r) + core
+                mine = (target == line) & (part == p)
+
+                @pl.when(mine)
+                def _():
+                    share_recv[chip] = share_send[q, p, r]
+
+                @pl.when(jnp.logical_not(mine))
+                def _():
+                    remote(
+                        share_send.at[q, p, r], share_recv.at[chip], 1, (target, p)
+                    ).start()
+
         return carry
 
     def tail():
@@ -565,18 +698,152 @@
         small_ref[pl.ds(216, 1), :] = jnp.zeros((1, 128), F32)
         small_ref[pl.ds(216, 1), pl.ds(0, DPROJ)] = jnp.sum(d_last, axis=0, keepdims=True)
         grad_dense_ref[...] = dot_nt(dw_ref[...], d_last, EXACT)
-        d_low_ref[...] = d_in_ref[...].astype(BF16)
-        for tile in range(TILES - 2):
-            value = small_ref[pl.ds(8 * tile, 8), :]
-            both = two_parts(value)
+
+    def small_pair():
+        return pltpu.make_async_remote_copy(
+            src_ref=small_ref,
+            dst_ref=small_two,
+            send_sem=sems.at[9],
+            recv_sem=sems.at[10],
+            device_id=(line + 1 - 2 * core, part),
+            device_id_type=pl.DeviceIdType.MESH,
+        )
+
+    def share_small():
+        small_pair().wait()
+        small_two[...] = small_two[...] + small_ref[...]
+        for a in range(16):
             for p in range(4):
-                grads_ref[tile, p, pl.ds(CHUNK, 16), :] = both
-        for p in range(4):
-            grads_ref[TILES - 2, p, pl.ds(CHUNK, 16), :] = two_parts(small_b[p])
-            grads_ref[TILES - 1, p, pl.ds(CHUNK, 16), :] = jnp.zeros((16, 128), BF16)
+                target = 2 * a + core
+                at = 8 * target
+                if a == 15:
+                    at = 8 * (TILES + p) - core * (8 + 8 * p)
+                source = small_two.at[pl.ds(eight(at), 8), :]
+                mine = (target == line) & (part == p)
+
+                @pl.when(mine)
+                def _():
+                    small_recv[chip] = small_two[pl.ds(eight(at), 8), :]
+
+                @pl.when(jnp.logical_not(mine))
+                def _():
+                    remote(source, small_recv.at[chip], 3, (target, p)).start()
+
+    def add_up():
+        others = pl.ds(0, CHIPS - 1)
+        wait_all(share_recv.at[others], sems.at[2])
+        wait_all(small_recv.at[others], sems.at[4])
+
+        def add(at, totals):
+            total, small = totals
+            return total + share_recv[at].astype(F32), small + small_recv[at]
+
+        total, small = lax.fori_loop(
+            1, CHIPS, add, (share_recv[0].astype(F32), small_recv[0])
+        )
+        experts_own[...] = total.astype(BF16)
+        small_own[...] = small
+        experts_all[line] = total.astype(BF16)
+        small_all[line] = small
+
+        def give(step, carry):
+            place = ((line + step) % TILES, part)
+            remote(experts_own, experts_all.at[line], 5, place).start()
+            remote(small_own, small_all.at[line], 7, place).start()
+            return carry
+
+        lax.fori_loop(1, TILES, give, 0)
+
+    def drain():
+        others = pl.ds(0, CHIPS - 1)
+        wait_all(pair_send, sems.at[0])
+        wait_all(share_recv.at[others], sems.at[1])
+        wait_all(small_recv.at[others], sems.at[3])
+        others = pl.ds(0, TILES - 1)
+        for sem in (5, 6):
+            wait_all(experts_all.at[others], sems.at[sem])
+        for sem in (7, 8):
+            wait_all(small_all.at[others], sems.at[sem])
+        experts_out_ref[...] = experts_all[...]
+        small_out_ref[...] = small_all[...]
+
+    def spread():
+        lane_from = lax.broadcasted_iota(jnp.int32, (128, 128), 0)
+        lane_to = lax.broadcasted_iota(jnp.int32, (128, 128), 1)
+        for field in range(FIELDS):
+            take = lane_from == EMB * (field % 8) + lane_to % EMB
+            copies = dot_nn(d_in_ref[:, pl.ds(field // 8 * 128, 128)].astype(BF16), take.astype(F32).astype(BF16))
+            rows[pl.ds(field * ROWS_LOC, ROWS_LOC), :] = copies
+        rows[pl.ds(LOOKUPS, 8), :] = jnp.zeros((8, 128), F32)
+        group = lane_group(1)
+        wide_group = lane_group(CAP - COLD)
+
+        def hot(at, carry):
+            for n in range(COLD, CAP):
+                row = rows[pl.ds(hot_src_ref[at * SLOTS + n], 1), :]
+                hot_rows[at, pl.ds(n - COLD, 1), :] = row
+            return carry
+
+        lax.fori_loop(0, HOT, hot, 0)
+        hot_rows[HOT] = jnp.zeros((CAP - COLD, 128), F32)
+
+        def collect(step, slots):
+            source = (me // 8 + step) % 16 * (8 * SLOTS)
+            for n in range(COLD):
+                total = rows[pl.ds(src_ref[source + n], 1), :]
+                for u in range(1, 8):
+                    row = rows[pl.ds(src_ref[source + u * SLOTS + n], 1), :]
+                    total = jnp.where(group == u, row, total)
+                slots[pl.ds(n, 1), :] = total
+
+        def finish(step, slots):
+            first = (me // 8 + step) % 16 * 8
+            total = jnp.zeros((CAP - COLD, 128), F32)
+            for u in range(8):
+                total = jnp.where(wide_group == u, hot_rows[hot_at_ref[first + u]], total)
+            slots[pl.ds(COLD, CAP - COLD), :] = total
+            for half in range(2):
+                turned = slots[pl.ds(half * 128, 128), :].T.astype(BF16)
+                for u in range(8):
+                    at = eight((first + u) * GROUPS + EMB * half, EMB)
+                    ready[pl.ds(at, EMB), :] = turned[EMB * u : EMB * u + EMB]
+
+        def send(step):
+            first = (me // 8 + step) % 16 * 8
+            for u in range(8):
+                dest = first + (me + u) % 8
+
+                @pl.when(dest != me)
+                def _():
+                    send_block(ready, landing, me, dest, sems.at[11], sems.at[12])
+
+        for slots in (even, odd):
+            slots[pl.ds(CAP, SLOTS - CAP), :] = jnp.zeros((SLOTS - CAP, 128), F32)
+        collect(0, even)
+        share_small()
+
+        def two_groups(pair, carry):
+            step = 2 * pair
+            collect(step + 1, odd)
+            finish(step, even)
+            send(step)
+            collect(jnp.minimum(step + 2, 15), even)
+            finish(step + 1, odd)
+            send(step + 1)
+            return carry
+
+        lax.fori_loop(0, 6, two_groups, 0)
+        add_up()
+        lax.fori_loop(6, 8, two_groups, 0)
+        wait_blocks(ready, landing, sems.at[11], sems.at[12])
+        rows_out_ref[...] = landing[...]
+        mine = pl.ds(eight(me * GROUPS, GROUPS), GROUPS)
+        rows_out_ref[mine, :] = ready[mine, :]
+        drain()
 
     @pl.when(phase == 0)
     def _():
+        greet_all(me)
         lax.fori_loop(0, EXPERTS, forward, 0)
 
     @pl.when(phase == 1)
@@ -585,24 +852,28 @@
 
     @pl.when(phase == 2)
     def _():
-        lax.fori_loop(0, EXPERTS, backward, 0)
+        pl.semaphore_wait(pltpu.get_barrier_semaphore(), OWNERS - 1)
+        lax.fori_loop(0, 4, experts, 0)
         tail()
+        small_pair().start()
+        spread()
 
 
 def model(*operands):
     return pl.pallas_call(
         model_kernel,
         grid=(3,),
-        in_specs=[VM] * len(operands),
-        out_specs=[VM] * 3,
+        in_specs=[VM] * (len(operands) - 3) + [SM] * 3,
+        out_specs=[VM] * 4,
         out_shape=[
-            shape((TILES, 4, SENT, 128), BF16),
-            shape((ROWS_LOC, DIN), BF16),
+            shape((OWNERS * GROUPS, 128), BF16),
+            shape((TILES, CHUNK, 128), BF16),
+            shape((TILES, 8, 128), F32),
             shape((DENSE, ROWS_LOC), F32),
         ],
         scratch_shapes=[
-            pltpu.VMEM((8 * (TILES - 2), 128), F32),
-            pltpu.VMEM((4, 8, 128), F32),
+            pltpu.VMEM((8 * (TILES + 4), 128), F32),
+            pltpu.VMEM((8 * (TILES + 4), 128), F32),
             pltpu.VMEM((ROWS_LOC, DIN), F32),
             pltpu.VMEM((EXPERTS, ROWS_LOC, HID), BF16),
             pltpu.VMEM((EXPERTS, ROWS_LOC, HID), F32),
@@ -613,83 +884,28 @@
             pltpu.VMEM((ROWS_LOC, TASKS * EXPERTS * EOUT), BF16),
             pltpu.VMEM((ROWS_LOC, TASKS * EOUT), F32),
             pltpu.VMEM((48, DIN), F32),
+            pltpu.VMEM((4, 4 * CHUNK, 128), F32),
+            pltpu.VMEM((4, 4, 4 * CHUNK, 128), BF16),
+            pltpu.VMEM((4, 4, 4 * CHUNK, 128), BF16),
+            pltpu.VMEM((4, 4, 4, CHUNK, 128), BF16),
+            pltpu.VMEM((CHIPS, CHUNK, 128), BF16),
+            pltpu.VMEM((CHIPS, 8, 128), F32),
+            pltpu.VMEM((CHUNK, 128), BF16),
+            pltpu.VMEM((TILES, CHUNK, 128), BF16),
+            pltpu.VMEM((8, 128), F32),
+            pltpu.VMEM((TILES, 8, 128), F32),
+            pltpu.VMEM((LOOKUPS + 8, 128), F32),
+            pltpu.VMEM((HOT + 1, CAP - COLD, 128), F32),
+            pltpu.VMEM((SLOTS, 128), F32),
+            pltpu.VMEM((SLOTS, 128), F32),
+            pltpu.VMEM((OWNERS * GROUPS, 128), BF16),
+            pltpu.VMEM((OWNERS * GROUPS, 128), BF16),
+            pltpu.SemaphoreType.DMA((4,)),
+            pltpu.SemaphoreType.DMA((13,)),
         ],
-        compiler_params=params(56),
+        compiler_params=remote_params(58, 1),
         name="model",
     )(*operands)
-
-
-def spread_kernel(src_ref, hot_ref, d_ref, out_ref, slots, rows, hot_rows):
-    lane_from = lax.broadcasted_iota(jnp.int32, (128, 128), 0)
-    lane_to = lax.broadcasted_iota(jnp.int32, (128, 128), 1)
-    for field in range(FIELDS):
-        take = lane_from == EMB * (field % 8) + lane_to % EMB
-        copies = dot_nn(d_ref[:, pl.ds(field // 8 * 128, 128)], take.astype(F32).astype(BF16))
-        rows[pl.ds(field * ROWS_LOC, ROWS_LOC), :] = copies
-    rows[pl.ds(LOOKUPS, 8), :] = jnp.zeros((8, 128), F32)
-    group = lane_group(1)
-
-    def clear(step, carry):
-        slots[pl.ds(eight(step * SLOTS + COLD), SLOTS - COLD), :] = jnp.zeros(
-            (SLOTS - COLD, 128), F32
-        )
-        return carry
-
-    lax.fori_loop(0, OWNERS // 8, clear, 0)
-
-    def cold(step, carry):
-        base = step // 6 * SLOTS + step % 6 * 16
-        source = step // 6 * (8 * SLOTS) + step % 6 * 16
-        for n in range(16):
-            total = rows[pl.ds(src_ref[source + n], 1), :]
-            for u in range(1, 8):
-                row = rows[pl.ds(src_ref[source + u * SLOTS + n], 1), :]
-                total = jnp.where(group == u, row, total)
-            slots[pl.ds(base + n, 1), :] = total
-        return carry
-
-    def hot(at, carry):
-        owner = hot_ref[at]
-        for n in range(COLD, CAP):
-            row = rows[pl.ds(src_ref[owner * SLOTS + n], 1), :]
-            hot_rows[pl.ds(at * (CAP - COLD) + n - COLD, 1), :] = row
-        return carry
-
-    lax.fori_loop(0, OWNERS // 8 * 6, cold, 0)
-    lax.fori_loop(0, HOT, hot, 0)
-    wide_group = lane_group(CAP - COLD)
-
-    def merge(at, carry):
-        owner = hot_ref[at]
-        place = pl.ds(eight((owner >> 3) * SLOTS + COLD), CAP - COLD)
-        new = hot_rows[pl.ds(eight(at * (CAP - COLD)), CAP - COLD), :]
-        slots[place, :] = jnp.where(wide_group == (owner & 7), new, slots[place, :])
-        return carry
-
-    lax.fori_loop(0, HOT, merge, 0)
-    for block in range(32):
-        owner, half = block // 2 * 8, block % 2
-        turned = slots[pl.ds(block * 128, 128), :].T.astype(BF16)
-        for u in range(8):
-            out_ref[pl.ds((owner + u) * GROUPS + EMB * half, EMB), :] = turned[
-                EMB * u : EMB * u + EMB
-            ]
-
-
-def spread_grads(src, hot, d_inputs):
-    return pl.pallas_call(
-        spread_kernel,
-        in_specs=[SM, SM, VM],
-        out_specs=VM,
-        out_shape=shape((OWNERS * GROUPS, 128), BF16),
-        scratch_shapes=[
-            pltpu.VMEM((OWNERS * GROUPS, 128), F32),
-            pltpu.VMEM((LOOKUPS + 8, 128), F32),
-            pltpu.VMEM((HOT * (CAP - COLD), 128), F32),
-        ],
-        compiler_params=params(48),
-        name="spread_grads",
-    )(src, hot, d_inputs)
 
 
 def scatter_kernel(
@@ -709,12 +925,12 @@
         for half in range(2):
             block = grads_ref[pl.ds(eight(source * GROUPS + EMB * half, EMB), EMB), :].astype(F32)
             block = jnp.broadcast_to(block[None], (8, EMB, 128)).reshape(128, 128)
-            block = jnp.where(at_group == groups[pl.ds(2 * source + half, 1), :], block, 0.0)
+            block = jnp.where(at_group == groups[source, pl.ds(half, 1), :], block, 0.0)
             found[pl.ds(half * 128, 128), :] = block.T
 
     def add(source, found):
         for n in range(CAP):
-            at = pl.ds(rows[2 * source + n // 128, n % 128], 1)
+            at = pl.ds(rows[source, n // 128, n % 128], 1)
             total = sums[n % SUMS]
             total[at, :] = total[at, :] + found[pl.ds(n, 1), :]
 
@@ -758,31 +974,9 @@
     )(asked, grads)
 
 
-def sum_kernel(parts_ref, out_ref):
-    def add(at, total):
-        return total + parts_ref[at].astype(F32)
-
-    total = lax.fori_loop(1, OWNERS, add, parts_ref[0].astype(F32))
-    small = two_parts(total[CHUNK : CHUNK + 8] + total[CHUNK + 8 : SENT])
-    low = total[0:CHUNK].astype(BF16)
-    for at in range(TILES):
-        out_ref[at, pl.ds(0, CHUNK), :] = low
-        out_ref[at, pl.ds(CHUNK, 16), :] = small
-
-
-def sum_parts(parts):
-    return pl.pallas_call(
-        sum_kernel,
-        in_specs=[VM],
-        out_specs=VM,
-        out_shape=shape((TILES, SENT, 128), BF16),
-        compiler_params=params(32),
-        name="sum_parts",
-    )(parts)
-
-
 def unpack_kernel(
-    sums_ref,
+    experts_ref,
+    small_ref,
     w_in_ref,
     w_out_ref,
     w1_ref,
@@ -797,7 +991,7 @@
     b_in_ref,
 ):
     def expert(k, carry):
-        rows = [sums_ref[4 * k + at, pl.ds(0, CHUNK), :] for at in range(4)]
+        rows = [experts_ref[2 * (4 * (k // 2) + at) + k % 2] for at in range(4)]
         rows = jnp.concatenate(rows, axis=0).astype(F32)
         for block in range(4):
             w_in_ref[k, :, pl.ds(block * 128, 128)] = rows[PART * block : PART * block + PART]
@@ -807,7 +1001,7 @@
     lax.fori_loop(0, EXPERTS, expert, 0)
 
     def tile(at):
-        return one_of(sums_ref[at, pl.ds(CHUNK, 16), :])
+        return small_ref[at]
 
     for at in range(16):
         w1_ref[at // 8, pl.ds(at % 8 * 8, 8), :] = tile(at)
@@ -832,10 +1026,10 @@
     b_in_ref[...] = tile(30)[:, 0:PART]
 
 
-def unpack(sums):
+def unpack(experts, small):
     return pl.pallas_call(
         unpack_kernel,
-        in_specs=[VM],
+        in_specs=[VM, VM],
         out_specs=[VM] * 12,
         out_shape=[
             shape((EXPERTS, PART, DIN), F32),
@@ -853,11 +1047,7 @@
         ],
         compiler_params=params(32),
         name="unpack",
-    )(sums)
-
-
-def exchange(value, axes):
-    return lax.all_to_all(value, axes, split_axis=0, concat_axis=0, tiled=True)
+    )(experts, small)
 
 
 def body(
@@ -890,17 +1080,15 @@
     key = ((ids >> 12) << 14) | (field * ROWS_LOC + example)
     load = (packed << 3) | ((row >> 7) & 7)
     keys, loads = lax.sort((key.reshape(-1), load.reshape(-1)), num_keys=1, is_stable=False)
-    requests, sources, hot = route(keys.reshape(-1, 128), loads.reshape(-1, 128))
-    asked = exchange(requests, ALL)
+    requests, sources, hot_sources, hot, hot_at = route(keys.reshape(-1, 128), loads.reshape(-1, 128))
     sources = sources.reshape(-1)
-    table = pack_tables(tables.transpose(0, 2, 1))
-    answer = look_up(asked, table)
+    answer, asked = look_up(requests, tables.transpose(0, 2, 1))
     feats_t = dense_feats.T
     inputs = embed(sources, hot, ids, answer, feats_t, dense_w, dense_b.reshape(DPROJ, 1))
     task_at = lax.broadcasted_iota(jnp.int32, (TASKS, TASKS * THID), 1) // THID
     task_row = lax.broadcasted_iota(jnp.int32, (TASKS, TASKS * THID), 0)
     w2_bd = jnp.where(task_at == task_row, tower_w2.reshape(1, -1), 0.0)
-    grads, d_inputs, grad_dense = model(
+    incoming, experts, small, grad_dense = model(
         inputs,
         labels.T,
         feats_t,
@@ -913,10 +1101,10 @@
         tower_b1.reshape(1, TASKS * THID),
         w2_bd,
         tower_b2.reshape(TASKS, 1),
+        sources,
+        hot_sources.reshape(-1),
+        hot_at,
     )
-    grads = exchange(grads.reshape(OWNERS, SENT, 128), ALL)
-    incoming = exchange(spread_grads(sources, hot, d_inputs), ALL)
-    sums = exchange(sum_parts(grads), "dp")
     grad_tables = scatter_add(asked, incoming).transpose(0, 2, 1)
     (
         grad_w_in,
@@ -931,7 +1119,7 @@
         grad_b2,
         grad_gate_b,
         grad_b_in,
-    ) = unpack(sums)
+    ) = unpack(experts, small)
     return (
         grad_tables,
         grad_dense_w,

time: 262 us -> 222 us (0.85)
  waiting for transfers between devices: 40.1 us -> 0.02 us
  Pallas kernels: 156 us -> 190 us
  starting transfers between devices: 28.1 us -> 0.04 us
  local copies, waits for them, and re-layouts: 12.3 us -> 6.03 us
    all_to_all x4 -> x0, waiting for transfers between devices: 40.1 us -> none  [exchange(): return lax.all_to_all(value, axes, split_axis=0, concat_axis=0, tiled=True)]
    pallas_call x7 -> x4, Pallas kernels: 94.4 us -> 130 us  [the longest x1 76 us: model(): pl.pallas_call(model_kernel, grid=(3,), in_specs=[VM] * (len(operands) -...]
    all_to_all x4 -> x0, starting transfers between devices: 28 us -> none  [exchange(): return lax.all_to_all(value, axes, split_axis=0, concat_axis=0, tiled=True)]
    unnamed x31 -> x34, local copies, waits for them, and re-layouts: 10.2 us -> 3.91 us
  transfers between devices with their start and end apart: 5 -> 1, of which waited for: 2 -> 0; matrix products, arithmetic and copies ran while one was open for 4% -> 5% of each run, Pallas kernels for 49% -> 33%
where the time goes in v4:
time: 222 us; the launch traced here: 220 us
  Pallas kernels  190 us (86%)
  between operations  14.3 us (6%)
  other arithmetic  10.1 us (5%)
  local copies, waits for them, and re-layouts  6.03 us (3%)
    pallas_call x1, Pallas kernels, model(): pl.pallas_call(model_kernel, grid=(3,), in_specs=[VM] * (len(operands) -...  76 us
    pallas_call x1, Pallas kernels, look_up(): pl.pallas_call(look_up_kernel, in_specs=[VM, pl.BlockSpec(memory_space=pl...  48.9 us
    pallas_call x1, Pallas kernels, scatter_add(): pl.pallas_call(scatter_kernel, in_specs=[VM, VM], out_specs=VM, out_shape...  40.3 us
    pallas_call x1, Pallas kernels, embed(): pl.pallas_call(embed_kernel, in_specs=[SM, SM, VM, VM, VM, VM, VM], out_s...  19.6 us
    sort x1, other arithmetic, body(): lax.sort((key.reshape(-1), load.reshape(-1)), num_keys=1, is_stable=False)  7.4 us
  transfers between devices with their start and end apart: 1, of which 0 were waited for; matrix products, arithmetic and copies ran while one was open for 5% of the time, Pallas kernels for 33%

profile of v4, /device:TPU:1, one launch (start us, length us, event | category | flops | bytes accessed | tf_op | source)
XLA Modules:
  0.0 220.1 jit_solution(5073349385341503260)
XLA Ops:
  7.2 0.0 copy-start.3
  7.2 0.0 copy-start.12
  7.2 0.0 all-gather.3.cloned.1.call-start
  7.3 0.7 copy.41
  8.0 2.1 fusion.1
  10.1 0.0 all-gather.3.cloned.1.call-update
  10.1 0.1 and_or_fusion
  10.2 0.1 copy.37.db_ref
  10.3 0.7 reshape.91.gate_b_ref
  11.0 0.6 reshape.84.b1_ref
  11.6 0.1 broadcast_in_dim.18
  11.7 0.0 copy-done.15
  11.7 0.6 copy.40.b2_ref
  12.3 7.4 %sort.15 = (s32[13312]{0:T(1024)S(1)}, s32[13312]{0:T(1024)S(1)}) sort(s32[13312]{0:T(1024)S(1)} %reshape.75, s32[13312]{0:T(1024)S(1)} %reshape.76), dimensions={0}, to_apply=%region_0.1 | sort | flops 186368 | bytes 212992 | tf_op jit(solution)/shard_map/sort | solution.py:1082
  19.8 3.6 %route.1 = (s32[128,2,128]{2,1,0:T(2,128)S(1)}, s32[256,128]{1,0:T(8,128)S(1)}, s32[64,128]{1,0:T(8,128)S(1)}, s32[32]{0:T(128)S(1)}, s32[128]{0:T(128)S(1)}) custom-call(s32[104,128]{1,0:T(8,128)S(1)} %bitcast.34, s32[104,128]{1,0:T(8,128)S(1)} %bitcast.35), custom_call_target="tpu_custom_call" | custom-call | tf_op jit(solution)/shard_map/route/pallas_call | solution.py:201
  23.4 0.0 copy-start.7
  23.4 0.6 copy-done.7
  24.0 0.5 copy-done.9
  24.5 48.9 %look_up.1 = (bf16[4096,128]{1,0:T(8,128)(2,1)S(1)}, s32[128,2,128]{2,1,0:T(2,128)S(1)}) custom-call(s32[128,2,128]{2,1,0:T(2,128)S(1)} %get-tuple-element.41.wanted_ref, f32[26,16,4096]{2,1,0:T(8,128)} %bitcast.37), custom_call_target="tpu_custom_call" | custom-call | tf_op jit(solution)/shard_map/look_up/pallas_call | solution.py:354
  73.4 0.0 copy-start.4
  73.4 0.6 copy-done.4
  74.1 0.0 copy-done.5
  74.1 19.6 %embed.1.x_ref = bf16[512,512]{1,0:T(8,128)(2,1)S(1)} custom-call(s32[32768]{0:T(1024)S(1)} %bitcast.29, s32[32]{0:T(128)S(1)} %get-tuple-element.44.hot_ref, s32[26,512]{1,0:T(8,128)S(1)} %bitcast.31, bf16[4096,128]{1,0:T(8,128)(2,1)S(1)} %get-tuple-element.45.answer_ref, f32[13,512]{1,0:T(8,128)S(1)} %bitcast.33, f32[13,96]{1,0:T(8,128)S(1)} %copy-done.8, ...), custom_call_target="tpu_custom_call" | custom-call | tf_op jit(solution)/shard_map/embed/pallas_call | solution.py:421
  93.7 0.0 copy-start
  93.7 0.8 copy-done
  94.5 0.6 compare_select_fusion.w2_ref
  95.0 76.0 %model.1 = (bf16[4096,128]{1,0:T(8,128)(2,1)}, bf16[32,80,128]{2,1,0:T(8,128)(2,1)}, f32[32,8,128]{2,1,0:T(8,128)}, f32[13,512]{1,0:T(8,128)}) custom-call(bf16[512,512]{1,0:T(8,128)(2,1)} %copy-done, s32[2,512]{1,0:T(2,128)} %bitcast.44, f32[13,512]{1,0:T(8,128)} %bitcast.32, f32[13,96]{1,0:T(8,128)} %dw_ref.3, bf16[4,8,80,640]{3,2,1,0:T(8,128)(2,1)} %bitcast.39, ...), custom_call_target="tpu_custom_call" | custom-call | tf_op jit(solution)/shard_map/model/pallas_call | solution.py:863
  171.1 40.3 %scatter_add.1 = f32[26,16,4096]{2,1,0:T(8,128)} custom-call(s32[128,2,128]{2,1,0:T(2,128)} %copy-done.4, bf16[4096,128]{1,0:T(8,128)(2,1)} %get-tuple-element.48.grads_ref), custom_call_target="tpu_custom_call" | custom-call | tf_op jit(solution)/shard_map/scatter_add/pallas_call | solution.py:964
  211.4 0.0 copy-done.1
  211.4 0.0 copy-done.6
  211.4 1.3 unpack.1
  212.7 0.6 copy.43
  (25 shorter events, 0.1 us)
Async XLA Ops:
  7.2 2.9 %copy-start.3 = (s32[512,26]{0,1:T(8,128)S(1)}, s32[512,26]{0,1:T(8,128)}, u32[]{:S(2)}) copy-start(s32[512,26]{0,1:T(8,128)} %param.16) | copy-start | bytes 159748
  7.2 3.0 %copy-start.12 = (f32[96]{0:T(128)S(1)}, f32[96]{0:T(128)}, u32[]{:S(2)}) copy-start(f32[96]{0:T(128)} %param.21) | copy-start | bytes 1156
  7.2 3.1 %copy-start.11 = (f32[2,8]{1,0:T(2,128)S(1)}, f32[2,8]{1,0:T(2,128)}, u32[]{:S(2)}) copy-start(f32[2,8]{1,0:T(2,128)} %param.27) | copy-start | bytes 196
  7.2 3.8 %copy-start.13 = (f32[2,64]{1,0:T(2,128)S(1)}, f32[2,64]{1,0:T(2,128)}, u32[]{:S(2)}) copy-start(f32[2,64]{1,0:T(2,128)} %param.29) | copy-start | bytes 1540
  7.2 4.4 %copy-start.14 = (f32[2,64]{1,0:T(2,128)S(1)}, f32[2,64]{1,0:T(2,128)}, u32[]{:S(2)}) copy-start(f32[2,64]{1,0:T(2,128)} %param.30) | copy-start | bytes 1540
  7.2 4.5 %copy-start.15 = (f32[2]{0:T(128)S(1)}, f32[2]{0:T(128)}, u32[]{:S(2)}) copy-start(f32[2]{0:T(128)} %param.31) | copy-start | bytes 28
  7.2 87.8 %all-gather.3.cloned.1.call-start = ((), (), s32[]{:S(2)}) async-start(), calls=%async_computation | async-start | bytes 4096000 | tf_op jit(solution)/shard_map/all_gather | solution.py:1073
  23.4 0.6 copy-start.7
  24.0 0.5 copy-start.9
  24.5 49.6 %copy-start.2 = (s32[256,128]{1,0:T(8,128)}, s32[256,128]{1,0:T(8,128)S(1)}, u32[]{:S(2)}) copy-start(s32[256,128]{1,0:T(8,128)S(1)} %get-tuple-element.43) | copy-start | bytes 393220
  24.5 49.6 %copy-start.5 = (f32[512,13]{0,1:T(8,128)S(1)}, f32[512,13]{0,1:T(8,128)}, u32[]{:S(2)}) copy-start(f32[512,13]{0,1:T(8,128)} %param.17) | copy-start | bytes 79876
  24.5 49.6 %copy-start.8 = (f32[13,96]{1,0:T(8,128)S(1)}, f32[13,96]{1,0:T(8,128)}, u32[]{:S(2)}) copy-start(f32[13,96]{1,0:T(8,128)} %dw_ref.3) | copy-start | bytes 14980
  73.4 0.7 copy-start.4
  93.7 0.8 copy-start
  171.1 40.3 %copy-start.1 = (bf16[32,80,128]{2,1,0:T(8,128)(2,1)S(1)}, bf16[32,80,128]{2,1,0:T(8,128)(2,1)}, u32[]{:S(2)}) copy-start(bf16[32,80,128]{2,1,0:T(8,128)(2,1)} %get-tuple-element.49.experts_ref) | copy-start | bytes 1966084
  171.1 40.3 %copy-start.6 = (f32[32,8,128]{2,1,0:T(8,128)S(1)}, f32[32,8,128]{2,1,0:T(8,128)}, u32[]{:S(2)}) copy-start(f32[32,8,128]{2,1,0:T(8,128)} %get-tuple-element.50.small_ref) | copy-start | bytes 393220
  171.1 41.6 %copy-start.10 = (f32[13,512]{1,0:T(8,128)S(1)}, f32[13,512]{1,0:T(8,128)}, u32[]{:S(2)}) copy-start(f32[13,512]{1,0:T(8,128)} %get-tuple-element.63) | copy-start | bytes 79876
Sparse Core Ops, SparseCore 0:
  10.3 48.6 all-gather.2

commit v5 on v4

--- a/solution.py
+++ b/solution.py
@@ -35,6 +35,8 @@
 CHUNK = 80
 TILES = 32
 CHIPS = OWNERS // 2
+SHARE = CHUNK + 16
+MODEL_MIB = 50
 PART = 64
 SUMS = 6
 
@@ -103,12 +105,12 @@
         pl.semaphore_signal(
             barrier,
             inc=1,
-            device_id=place_of((me + step) % OWNERS),
+            device_id=place_of((me + step + 1) % OWNERS),
             device_id_type=pl.DeviceIdType.MESH,
         )
         return carry
 
-    lax.fori_loop(1, OWNERS, greet, 0)
+    lax.fori_loop(0, OWNERS - 1, greet, 0)
     return barrier
 
 
@@ -216,17 +218,14 @@
             pltpu.SMEM((8, 128), jnp.int32),
             pltpu.SemaphoreType.DMA,
         ],
-        compiler_params=params(32),
+        compiler_params=params(8),
         name="route",
     )(keys, loads)
 
 
-def split_wanted(asked_ref, rows_v, groups, rows, sem):
+def split_wanted(asked_ref, rows_v, groups):
     rows_v[...] = asked_ref[...] >> 3
-    copy = pltpu.make_async_copy(rows_v, rows, sem)
-    copy.start()
     groups[...] = asked_ref[...] & 7
-    copy.wait()
 
 
 def split_scratch():
@@ -234,15 +233,21 @@
         pltpu.VMEM((OWNERS, 2, 128), jnp.int32),
         pltpu.VMEM((OWNERS, 2, 128), jnp.int32),
         pltpu.SMEM((OWNERS, 2, 128), jnp.int32),
-        pltpu.SemaphoreType.DMA,
+        pltpu.SemaphoreType.DMA((8,)),
     ]
 
 
 def look_up_kernel(
     wanted_ref,
     tables_ref,
+    w_out_ref,
+    b_in_ref,
     out_ref,
     asked_ref,
+    w_out_all,
+    b_in_all,
+    b_low,
+    b_own,
     fields,
     table,
     rows_v,
@@ -258,8 +263,11 @@
     send_sem,
     recv_sem,
     own_sem,
+    weight_sems,
 ):
     me = my_index()
+    line = lax.axis_index("dp")
+    part = lax.axis_index("mp")
 
     def field_copy(field):
         return pltpu.make_async_copy(
@@ -270,6 +278,12 @@
         field_copy(field).start()
         return carry
 
+    own_weights = [
+        pltpu.make_async_copy(source, target, weight_sems.at[4 + at])
+        for at, (source, target) in enumerate(((w_out_ref, w_out_all.at[part]), (b_in_ref, b_low)))
+    ]
+    for copy in own_weights:
+        copy.start()
     lax.fori_loop(0, FIELDS, start_field, 0)
     barrier = greet_all(me)
 
@@ -288,7 +302,7 @@
     pl.semaphore_wait(barrier, OWNERS - 1)
 
     def ask(step, carry):
-        owner = (me + step) % OWNERS
+        owner = (me + step + 1) % OWNERS
         pltpu.make_async_remote_copy(
             src_ref=wanted_ref.at[owner],
             dst_ref=asked_ref.at[me],
@@ -299,11 +313,43 @@
         ).start()
         return carry
 
-    lax.fori_loop(1, OWNERS, ask, 0)
+    lax.fori_loop(0, OWNERS - 1, ask, 0)
+    for copy in own_weights:
+        copy.wait()
+    b_own[...] = jnp.zeros_like(b_own)
+    b_own[:, pl.ds(0, PART)] = b_low[...].astype(F32)
+    b_in_all[part] = b_own[...]
+
+    def weight_copies(step):
+        place = (line, (part + step) % 4)
+        return [
+            pltpu.make_async_remote_copy(
+                src_ref=source,
+                dst_ref=target.at[part],
+                send_sem=weight_sems.at[2 * at],
+                recv_sem=weight_sems.at[2 * at + 1],
+                device_id=place,
+                device_id_type=pl.DeviceIdType.MESH,
+            )
+            for at, (source, target) in enumerate(((w_out_ref, w_out_all), (b_own, b_in_all)))
+        ]
+
+    for step in range(1, 4):
+        for copy in weight_copies(step):
+            copy.start()
     lax.fori_loop(8, FIELDS, pack, 0)
     others = pl.ds(0, OWNERS - 1)
     pltpu.make_async_copy(asked_ref.at[others], asked_ref.at[others], ask_recv).wait()
-    split_wanted(asked_ref, rows_v, groups, rows, sem)
+    split_wanted(asked_ref, rows_v, groups)
+
+    def rows_copy(step):
+        chunk = pl.ds(eight((me // 16 + step) % 8 * 16, 16), 16)
+        return pltpu.make_async_copy(rows_v.at[chunk], rows.at[chunk], sem.at[step])
+
+    for step in range(8):
+        rows_copy(step).start()
+    for step in range(2):
+        rows_copy(step).wait()
     at_group = sublane_group()
 
     def gather(source, found):
@@ -341,25 +387,37 @@
         send(second)
         return carry
 
-    lax.fori_loop(0, OWNERS // 2 - 1, two_sources, 0)
+    lax.fori_loop(0, 6, two_sources, 0)
+    for step in range(2, 8):
+        rows_copy(step).wait()
+    lax.fori_loop(6, OWNERS // 2 - 1, two_sources, 0)
     last = (me + OWNERS - 1) % OWNERS
     pick(last, odd)
     send(last)
     own.wait()
     pltpu.make_async_copy(wanted_ref.at[others], wanted_ref.at[others], ask_send).wait()
+    three = pl.ds(0, 3)
+    for at, target in enumerate((w_out_all, b_in_all)):
+        for sem_at in (2 * at, 2 * at + 1):
+            sem = weight_sems.at[sem_at]
+            pltpu.make_async_copy(target.at[three], target.at[three], sem).wait()
     wait_blocks(ready, out_ref, send_sem, recv_sem)
 
 
-def look_up(wanted, tables_t):
+def look_up(wanted, tables_t, w_out, b_in):
     return pl.pallas_call(
         look_up_kernel,
-        in_specs=[VM, pl.BlockSpec(memory_space=pl.ANY)],
-        out_specs=[VM, VM],
+        in_specs=[VM] + [pl.BlockSpec(memory_space=pl.ANY)] * 3,
+        out_specs=[VM] * 4,
         out_shape=[
             shape((OWNERS * GROUPS, 128), BF16),
             shape((OWNERS, 2, 128), jnp.int32),
+            shape((4, EXPERTS, PART, EOUT), BF16),
+            shape((4, EXPERTS, 128), F32),
         ],
         scratch_shapes=[
+            pltpu.VMEM((EXPERTS, PART), BF16),
+            pltpu.VMEM((EXPERTS, 128), F32),
             pltpu.VMEM((FIELDS, EMB, ROWS_DEV), F32),
             pltpu.VMEM((PACKED + 8, 128), F32),
         ]
@@ -367,10 +425,11 @@
         + [pltpu.VMEM((SLOTS, 128), F32)] * 2
         + [pltpu.VMEM((OWNERS * GROUPS, 128), BF16)]
         + [pltpu.SemaphoreType.DMA((FIELDS,))]
-        + [pltpu.SemaphoreType.DMA] * 5,
+        + [pltpu.SemaphoreType.DMA] * 5
+        + [pltpu.SemaphoreType.DMA((6,))],
         compiler_params=remote_params(48, 0),
         name="look_up",
-    )(wanted, tables_t)
+    )(wanted, tables_t, w_out, b_in)
 
 
 def embed_kernel(
@@ -413,7 +472,12 @@
         return carry
 
     lax.fori_loop(0, FIELDS, field, 0)
-    x_t[pl.ds(FIELDS * EMB, DPROJ), :] = dot_tn(dw_ref[...], feats_ref[...], EXACT) + db_ref[...]
+    top = lax.broadcasted_iota(jnp.int32, (8, DPROJ), 0) == 0
+    bias = jnp.where(top, jnp.broadcast_to(db_ref[...], (8, DPROJ)), 0.0)
+    x_t[pl.ds(FIELDS * EMB, DPROJ), :] = (
+        dot_tn(dw_ref[...], feats_ref[...], EXACT)
+        + dot_tn(bias, jnp.ones((8, ROWS_LOC), F32), EXACT)
+    )
     out_ref[...] = x_t[...].T.astype(BF16)
 
 
@@ -428,7 +492,7 @@
             pltpu.VMEM((LOOKUPS + 8, 128), F32),
             pltpu.VMEM((DIN, ROWS_LOC), F32),
         ],
-        compiler_params=params(48),
+        compiler_params=params(16),
         name="embed",
     )(src, hot, ids, answer, feats_t, dense_w, dense_b)
 
@@ -445,12 +509,24 @@
     return value * half, slope
 
 
+def two_parts(value):
+    high = value.astype(BF16).astype(F32)
+    return jnp.concatenate([high, value - high], axis=0).astype(BF16)
+
+
+def one_of(parts):
+    wide = parts.astype(F32)
+    return wide[0:8] + wide[8:16]
+
+
 def model_kernel(
     x_ref,
     labels_ref,
     feats_ref,
     dw_ref,
-    weights_ref,
+    w_in_ref,
+    w_out_ref,
+    b_in_ref,
     b_out_ref,
     gate_w_ref,
     gate_b_ref,
@@ -462,8 +538,7 @@
     hot_src_ref,
     hot_at_ref,
     rows_out_ref,
-    experts_out_ref,
-    small_out_ref,
+    share_out_ref,
     grad_dense_ref,
     small_ref,
     small_two,
@@ -481,10 +556,10 @@
     pair_send,
     pair_recv,
     share_send,
+    first_recv,
+    second_send,
     share_recv,
     small_recv,
-    experts_own,
-    experts_all,
     small_own,
     small_all,
     rows,
@@ -494,6 +569,7 @@
     ready,
     landing,
     pair_sems,
+    first_sems,
     sems,
 ):
     x = x_ref[...]
@@ -503,34 +579,39 @@
     core = line % 2
     chip = line // 2 * 4 + part
     me = my_index()
+    at_y, at_x = line // 8, line // 2 % 4
 
     def weights_in(k):
         return jnp.concatenate(
-            [weights_ref[p, k, pl.ds(0, PART), pl.ds(0, DIN)] for p in range(4)], axis=0
+            [w_in_ref[p, k] for p in range(4)], axis=0
         )
 
     def weights_out(k):
         return jnp.concatenate(
-            [weights_ref[p, k, pl.ds(0, PART), pl.ds(DIN, EOUT)] for p in range(4)], axis=0
+            [w_out_ref[p, k] for p in range(4)], axis=0
         )
 
     def forward(k, carry):
-        bias = [
-            weights_ref[p, k, pl.ds(PART, 16), pl.ds(0, 128)].astype(F32)[0:1, 0:PART]
-            for p in range(4)
-        ]
+        bias = [b_in_ref[p, pl.ds(k, 1), :][:, 0:PART] for p in range(4)]
         pre = dot_nt(x, weights_in(k)) + jnp.concatenate(bias, axis=1)
         act, grad = gelu_both(pre)
         act = act.astype(BF16)
         hidden[k] = act
         slope[k] = grad
-        outs[k] = dot_nn(act, weights_out(k)) + b_out_ref[k]
+        outs[k] = dot_nn(act, weights_out(k)) + b_out_ref[pl.ds(k, 1), :]
         return carry
 
     def head():
         gate_parts = jnp.concatenate(split3(gate_w_ref[...]), axis=0)
         stage[...] = dot_nt(gate_parts, x)
-        logits = stage[0:16] + stage[16:32] + stage[32:48] + gate_b_ref[...]
+        own = lax.broadcasted_iota(jnp.int32, (EXPERTS, EXPERTS), 0) == lax.broadcasted_iota(
+            jnp.int32, (EXPERTS, EXPERTS), 1
+        )
+        gate_b = [
+            jnp.sum(jnp.where(own, gate_b_ref[pl.ds(t, 1), :], 0.0), axis=1, keepdims=True)
+            for t in range(TASKS)
+        ]
+        logits = stage[0:16] + stage[16:32] + stage[32:48] + jnp.concatenate(gate_b, axis=0)
         logits = logits.reshape(TASKS, EXPERTS, ROWS_LOC)
         gates = jnp.exp(logits - jnp.max(logits, axis=1, keepdims=True))
         gates = gates / jnp.sum(gates, axis=1, keepdims=True)
@@ -561,9 +642,18 @@
             ],
             axis=0,
         )
-        upper, upper_slope = gelu_both(dot_nt(mixture, w1_bd, EXACT) + b1_ref[...])
-        w2_bd = w2_ref[...]
-        logit = dot_nt(w2_bd, upper, EXACT) + b2_ref[...]
+        b1 = jnp.concatenate([b1_ref[pl.ds(t, 1), :] for t in range(TASKS)], axis=1)
+        upper, upper_slope = gelu_both(dot_nt(mixture, w1_bd, EXACT) + b1)
+        none = jnp.zeros((1, THID), F32)
+        w2_bd = jnp.concatenate(
+            [
+                jnp.concatenate([w2_ref[pl.ds(0, 1), :], none], axis=1),
+                jnp.concatenate([none, w2_ref[pl.ds(1, 1), :]], axis=1),
+            ],
+            axis=0,
+        )
+        task = lax.broadcasted_iota(jnp.int32, (TASKS, ROWS_LOC), 0)
+        logit = dot_nt(w2_bd, upper, EXACT) + jnp.where(task == 0, b2_ref[0], b2_ref[1])
         d_logit = jax.nn.sigmoid(logit) - labels_ref[...].astype(F32)
         d_pre1 = dot_tn(d_logit, w2_bd, EXACT) * upper_slope
         grad_w2 = dot_nn(d_logit, upper, EXACT)
@@ -650,46 +740,83 @@
     def wait_all(ref, sem):
         pltpu.make_async_copy(ref, ref, sem).wait()
 
+    def quarter(step):
+        q = (step + at_y + at_x + part) % 4
+        even = 1 - q % 2
+        return q, even, even * part + (1 - even) * at_x, even * at_x + (1 - even) * part
+
     def experts(step, carry):
-        q = (step + line // 2 + part) % 4
+        q = quarter(step)[0]
 
         def for_pair(p, block, value):
             pair_send[q, p, pl.ds(PART * block, PART), :] = value.astype(BF16)
 
         def for_own(p, block, value):
-            own_grad[p, pl.ds(PART * block, PART), :] = value
+            own_grad[step % 2, p, pl.ds(PART * block, PART), :] = value
 
         backward(2 * q + 1 - core, for_pair)
-        pair = pltpu.make_async_remote_copy(
+        pltpu.make_async_remote_copy(
             src_ref=pair_send.at[q],
             dst_ref=pair_recv.at[q],
             send_sem=sems.at[0],
             recv_sem=pair_sems.at[q],
             device_id=(line + 1 - 2 * core, part),
             device_id_type=pl.DeviceIdType.MESH,
-        )
-        pair.start()
+        ).start()
+
+        @pl.when(step > 0)
+        def _():
+            first_round(step - 1)
+
         backward(2 * q + core, for_own)
-        pair.wait_recv()
+        return carry
+
+    def first_round(step):
+        q, even, first, _ = quarter(step)
+        wait_all(pair_recv.at[0], pair_sems.at[q])
         for p in range(4):
-            total = own_grad[p] + pair_recv[q, p].astype(F32)
-            share_send[q, p] = total.astype(BF16).reshape(4, CHUNK, 128)
-        for r in range(4):
-            for p in range(4):
-                target = 2 * (4 * q + r) + core
-                mine = (target == line) & (part == p)
-
-                @pl.when(mine)
-                def _():
-                    share_recv[chip] = share_send[q, p, r]
-
-                @pl.when(jnp.logical_not(mine))
-                def _():
-                    remote(
-                        share_send.at[q, p, r], share_recv.at[chip], 1, (target, p)
-                    ).start()
-
-        return carry
+            total = (own_grad[step % 2, p] + pair_recv[q, p].astype(F32)).astype(BF16)
+            for r in range(4):
+                piece = total[CHUNK * r : CHUNK * r + CHUNK]
+                share_send[q, even * p + (1 - even) * r, even * r + (1 - even) * p] = piece
+        for hop in range(1, 4):
+            peer = (first + hop) % 4
+            pltpu.make_async_remote_copy(
+                src_ref=share_send.at[q, peer],
+                dst_ref=first_recv.at[q, first],
+                send_sem=sems.at[9],
+                recv_sem=first_sems.at[q],
+                device_id=(line + (1 - even) * 2 * (peer - at_x), even * peer + (1 - even) * part),
+                device_id_type=pl.DeviceIdType.MESH,
+            ).start()
+        first_recv[q, first] = share_send[q, first]
+
+    def second_round(step):
+        q, even, _, second = quarter(step)
+        three = first_recv.at[0, pl.ds(0, 3)]
+        wait_all(three, first_sems.at[q])
+        for at in range(4):
+            total = first_recv[q, 0, at].astype(F32)
+            for f in range(1, 4):
+                total = total + first_recv[q, f, at].astype(F32)
+            second_send[q, at] = total.astype(BF16)
+        for at in range(4):
+            target = 2 * (4 * q + even * at + (1 - even) * at_x) + core
+            target_part = even * part + (1 - even) * at
+            mine = (target == line) & (target_part == part)
+
+            @pl.when(mine)
+            def _():
+                share_recv[4 * at_y + second] = second_send[q, at]
+
+            @pl.when(jnp.logical_not(mine))
+            def _():
+                remote(
+                    second_send.at[q, at],
+                    share_recv.at[4 * at_y + second],
+                    1,
+                    (target, target_part),
+                ).start()
 
     def tail():
         d_last = d_in_ref[:, pl.ds(DIN - DPROJ, DPROJ)]
@@ -703,69 +830,93 @@
         return pltpu.make_async_remote_copy(
             src_ref=small_ref,
             dst_ref=small_two,
-            send_sem=sems.at[9],
-            recv_sem=sems.at[10],
+            send_sem=sems.at[5],
+            recv_sem=sems.at[6],
             device_id=(line + 1 - 2 * core, part),
             device_id_type=pl.DeviceIdType.MESH,
         )
 
+    adds_small = ((line < 30) & (part == line % 4)) | (line == 30)
+
     def share_small():
         small_pair().wait()
         small_two[...] = small_two[...] + small_ref[...]
-        for a in range(16):
+
+        def share_tile(at, target, p):
+            mine = (target == line) & (part == p)
+
+            @pl.when(mine)
+            def _():
+                small_recv[chip] = small_two[pl.ds(eight(at), 8), :]
+
+            @pl.when(jnp.logical_not(mine))
+            def _():
+                source = small_two.at[pl.ds(eight(at), 8), :]
+                remote(source, small_recv.at[chip], 3, (target, p)).start()
+
+        for a in range(15):
+            target = 2 * a + core
+            share_tile(8 * target, target, target % 4)
+
+        @pl.when(core == 0)
+        def _():
             for p in range(4):
-                target = 2 * a + core
-                at = 8 * target
-                if a == 15:
-                    at = 8 * (TILES + p) - core * (8 + 8 * p)
-                source = small_two.at[pl.ds(eight(at), 8), :]
-                mine = (target == line) & (part == p)
-
-                @pl.when(mine)
+                share_tile(8 * (TILES + p), 30, p)
+
+    def add_up():
+        @pl.when(line == TILES - 1)
+        def _():
+            small_all[...] = jnp.zeros_like(small_all)
+
+        @pl.when(adds_small)
+        def _():
+            wait_all(small_recv.at[pl.ds(0, CHIPS - 1)], sems.at[4])
+
+            def add_small(at, total):
+                return total + small_recv[at]
+
+            small_own[...] = lax.fori_loop(1, CHIPS, add_small, small_recv[0])
+
+            @pl.when(line < 30)
+            def _():
+                for hop in range(1, 4):
+                    remote(small_own, small_all, 10, (line, (part + hop) % 4)).start()
+
+        wait_all(share_recv.at[pl.ds(0, 15)], sems.at[2])
+        total = share_recv[0].astype(F32)
+        for at in range(1, 16):
+            total = total + share_recv[at].astype(F32)
+        low = total.astype(BF16)
+        for at in range(TILES):
+            share_out_ref[at, pl.ds(0, CHUNK), :] = low
+
+    def add_small_up():
+        @pl.when((line < 30) & jnp.logical_not(adds_small))
+        def _():
+            wait_all(small_all, sems.at[11])
+
+        @pl.when(adds_small)
+        def _():
+            small_all[...] = small_own[...]
+
+        low = two_parts(small_all[...])
+        for at in range(TILES):
+            share_out_ref[at, pl.ds(CHUNK, 16), :] = low
+
+    def drain():
+        wait_all(pair_send, sems.at[0])
+        wait_all(first_recv.at[pl.ds(0, 3)], sems.at[9])
+        wait_all(share_recv.at[pl.ds(0, 15)], sems.at[1])
+        for sends, zero_core in ((15, 1), (19, 0)):
+            for mine in (0, 1):
+
+                @pl.when((core == zero_core) & (adds_small == (mine == 1)))
                 def _():
-                    small_recv[chip] = small_two[pl.ds(eight(at), 8), :]
-
-                @pl.when(jnp.logical_not(mine))
-                def _():
-                    remote(source, small_recv.at[chip], 3, (target, p)).start()
-
-    def add_up():
-        others = pl.ds(0, CHIPS - 1)
-        wait_all(share_recv.at[others], sems.at[2])
-        wait_all(small_recv.at[others], sems.at[4])
-
-        def add(at, totals):
-            total, small = totals
-            return total + share_recv[at].astype(F32), small + small_recv[at]
-
-        total, small = lax.fori_loop(
-            1, CHIPS, add, (share_recv[0].astype(F32), small_recv[0])
-        )
-        experts_own[...] = total.astype(BF16)
-        small_own[...] = small
-        experts_all[line] = total.astype(BF16)
-        small_all[line] = small
-
-        def give(step, carry):
-            place = ((line + step) % TILES, part)
-            remote(experts_own, experts_all.at[line], 5, place).start()
-            remote(small_own, small_all.at[line], 7, place).start()
-            return carry
-
-        lax.fori_loop(1, TILES, give, 0)
-
-    def drain():
-        others = pl.ds(0, CHIPS - 1)
-        wait_all(pair_send, sems.at[0])
-        wait_all(share_recv.at[others], sems.at[1])
-        wait_all(small_recv.at[others], sems.at[3])
-        others = pl.ds(0, TILES - 1)
-        for sem in (5, 6):
-            wait_all(experts_all.at[others], sems.at[sem])
-        for sem in (7, 8):
-            wait_all(small_all.at[others], sems.at[sem])
-        experts_out_ref[...] = experts_all[...]
-        small_out_ref[...] = small_all[...]
+                    wait_all(small_recv.at[pl.ds(0, sends - mine)], sems.at[3])
+
+        @pl.when(adds_small & (line < 30))
+        def _():
+            wait_all(small_recv.at[pl.ds(0, 3)], sems.at[10])
 
     def spread():
         lane_from = lax.broadcasted_iota(jnp.int32, (128, 128), 0)
@@ -784,11 +935,16 @@
                 hot_rows[at, pl.ds(n - COLD, 1), :] = row
             return carry
 
+        second_round(0)
         lax.fori_loop(0, HOT, hot, 0)
+        second_round(1)
         hot_rows[HOT] = jnp.zeros((CAP - COLD, 128), F32)
 
+        def group_at(step):
+            return (3 * (line // 2) + part + 4 * core + step) % 16
+
         def collect(step, slots):
-            source = (me // 8 + step) % 16 * (8 * SLOTS)
+            source = group_at(step) * (8 * SLOTS)
             for n in range(COLD):
                 total = rows[pl.ds(src_ref[source + n], 1), :]
                 for u in range(1, 8):
@@ -797,7 +953,7 @@
                 slots[pl.ds(n, 1), :] = total
 
         def finish(step, slots):
-            first = (me // 8 + step) % 16 * 8
+            first = group_at(step) * 8
             total = jnp.zeros((CAP - COLD, 128), F32)
             for u in range(8):
                 total = jnp.where(wide_group == u, hot_rows[hot_at_ref[first + u]], total)
@@ -809,18 +965,20 @@
                     ready[pl.ds(at, EMB), :] = turned[EMB * u : EMB * u + EMB]
 
         def send(step):
-            first = (me // 8 + step) % 16 * 8
+            first = group_at(step) * 8
             for u in range(8):
                 dest = first + (me + u) % 8
 
                 @pl.when(dest != me)
                 def _():
-                    send_block(ready, landing, me, dest, sems.at[11], sems.at[12])
+                    send_block(ready, landing, me, dest, sems.at[7], sems.at[8])
 
         for slots in (even, odd):
             slots[pl.ds(CAP, SLOTS - CAP), :] = jnp.zeros((SLOTS - CAP, 128), F32)
+        share_small()
+        second_round(2)
         collect(0, even)
-        share_small()
+        second_round(3)
 
         def two_groups(pair, carry):
             step = 2 * pair
@@ -835,7 +993,8 @@
         lax.fori_loop(0, 6, two_groups, 0)
         add_up()
         lax.fori_loop(6, 8, two_groups, 0)
-        wait_blocks(ready, landing, sems.at[11], sems.at[12])
+        add_small_up()
+        wait_blocks(ready, landing, sems.at[7], sems.at[8])
         rows_out_ref[...] = landing[...]
         mine = pl.ds(eight(me * GROUPS, GROUPS), GROUPS)
         rows_out_ref[mine, :] = ready[mine, :]
@@ -854,6 +1013,7 @@
     def _():
         pl.semaphore_wait(pltpu.get_barrier_semaphore(), OWNERS - 1)
         lax.fori_loop(0, 4, experts, 0)
+        first_round(3)
         tail()
         small_pair().start()
         spread()
@@ -863,12 +1023,11 @@
     return pl.pallas_call(
         model_kernel,
         grid=(3,),
-        in_specs=[VM] * (len(operands) - 3) + [SM] * 3,
-        out_specs=[VM] * 4,
+        in_specs=[VM] * (len(operands) - 4) + [SM] * 4,
+        out_specs=[VM] * 3,
         out_shape=[
             shape((OWNERS * GROUPS, 128), BF16),
-            shape((TILES, CHUNK, 128), BF16),
-            shape((TILES, 8, 128), F32),
+            shape((TILES, SHARE, 128), BF16),
             shape((DENSE, ROWS_LOC), F32),
         ],
         scratch_shapes=[
@@ -884,16 +1043,16 @@
             pltpu.VMEM((ROWS_LOC, TASKS * EXPERTS * EOUT), BF16),
             pltpu.VMEM((ROWS_LOC, TASKS * EOUT), F32),
             pltpu.VMEM((48, DIN), F32),
-            pltpu.VMEM((4, 4 * CHUNK, 128), F32),
+            pltpu.VMEM((2, 4, 4 * CHUNK, 128), F32),
             pltpu.VMEM((4, 4, 4 * CHUNK, 128), BF16),
             pltpu.VMEM((4, 4, 4 * CHUNK, 128), BF16),
             pltpu.VMEM((4, 4, 4, CHUNK, 128), BF16),
-            pltpu.VMEM((CHIPS, CHUNK, 128), BF16),
+            pltpu.VMEM((4, 4, 4, CHUNK, 128), BF16),
+            pltpu.VMEM((4, 4, CHUNK, 128), BF16),
+            pltpu.VMEM((16, CHUNK, 128), BF16),
             pltpu.VMEM((CHIPS, 8, 128), F32),
-            pltpu.VMEM((CHUNK, 128), BF16),
-            pltpu.VMEM((TILES, CHUNK, 128), BF16),
             pltpu.VMEM((8, 128), F32),
-            pltpu.VMEM((TILES, 8, 128), F32),
+            pltpu.VMEM((8, 128), F32),
             pltpu.VMEM((LOOKUPS + 8, 128), F32),
             pltpu.VMEM((HOT + 1, CAP - COLD, 128), F32),
             pltpu.VMEM((SLOTS, 128), F32),
@@ -901,9 +1060,10 @@
             pltpu.VMEM((OWNERS * GROUPS, 128), BF16),
             pltpu.VMEM((OWNERS * GROUPS, 128), BF16),
             pltpu.SemaphoreType.DMA((4,)),
-            pltpu.SemaphoreType.DMA((13,)),
+            pltpu.SemaphoreType.DMA((4,)),
+            pltpu.SemaphoreType.DMA((12,)),
         ],
-        compiler_params=remote_params(58, 1),
+        compiler_params=remote_params(MODEL_MIB, 1),
         name="model",
     )(*operands)
 
@@ -911,7 +1071,9 @@
 def scatter_kernel(
     asked_ref, grads_ref, out_ref, rows_v, groups, rows, sem, even, odd, *sums
 ):
-    split_wanted(asked_ref, rows_v, groups, rows, sem)
+    split_wanted(asked_ref, rows_v, groups)
+    rows_copy = pltpu.make_async_copy(rows_v, rows, sem.at[0])
+    rows_copy.start()
     at_group = sublane_group()
 
     def clear(step, carry):
@@ -920,6 +1082,7 @@
         return carry
 
     lax.fori_loop(0, PACKED // 512, clear, 0)
+    rows_copy.wait()
 
     def place(source, found):
         for half in range(2):
@@ -975,8 +1138,7 @@
 
 
 def unpack_kernel(
-    experts_ref,
-    small_ref,
+    shares_ref,
     w_in_ref,
     w_out_ref,
     w1_ref,
@@ -991,7 +1153,8 @@
     b_in_ref,
 ):
     def expert(k, carry):
-        rows = [experts_ref[2 * (4 * (k // 2) + at) + k % 2] for at in range(4)]
+        lines = [2 * (4 * (k // 2) + at) + k % 2 for at in range(4)]
+        rows = [shares_ref[at, pl.ds(0, CHUNK), :] for at in lines]
         rows = jnp.concatenate(rows, axis=0).astype(F32)
         for block in range(4):
             w_in_ref[k, :, pl.ds(block * 128, 128)] = rows[PART * block : PART * block + PART]
@@ -1001,7 +1164,7 @@
     lax.fori_loop(0, EXPERTS, expert, 0)
 
     def tile(at):
-        return small_ref[at]
+        return one_of(shares_ref[at, pl.ds(CHUNK, 16), :])
 
     for at in range(16):
         w1_ref[at // 8, pl.ds(at % 8 * 8, 8), :] = tile(at)
@@ -1026,10 +1189,10 @@
     b_in_ref[...] = tile(30)[:, 0:PART]
 
 
-def unpack(experts, small):
+def unpack(shares):
     return pl.pallas_call(
         unpack_kernel,
-        in_specs=[VM, VM],
+        in_specs=[VM],
         out_specs=[VM] * 12,
         out_shape=[
             shape((EXPERTS, PART, DIN), F32),
@@ -1047,7 +1210,7 @@
         ],
         compiler_params=params(32),
         name="unpack",
-    )(experts, small)
+    )(shares)
 
 
 def body(
@@ -1068,10 +1231,7 @@
     tower_w2,
     tower_b2,
 ):
-    weights = jnp.concatenate([w_in.transpose(0, 2, 1), w_out], axis=2)
-    bias = jnp.pad(b_in[:, None, :], ((0, 0), (0, 15), (0, DIN + EOUT - PART)))
-    weights = lax.all_gather(jnp.concatenate([weights, bias], axis=1), "mp", axis=0)
-
+    w_in_all = lax.all_gather(w_in.transpose(0, 2, 1), "mp", axis=0)
     ids = sparse_ids.T
     field = lax.broadcasted_iota(jnp.int32, (FIELDS, ROWS_LOC), 0)
     example = lax.broadcasted_iota(jnp.int32, (FIELDS, ROWS_LOC), 1)
@@ -1082,29 +1242,31 @@
     keys, loads = lax.sort((key.reshape(-1), load.reshape(-1)), num_keys=1, is_stable=False)
     requests, sources, hot_sources, hot, hot_at = route(keys.reshape(-1, 128), loads.reshape(-1, 128))
     sources = sources.reshape(-1)
-    answer, asked = look_up(requests, tables.transpose(0, 2, 1))
+    answer, asked, w_out_all, b_in_all = look_up(
+        requests, tables.transpose(0, 2, 1), w_out, b_in
+    )
     feats_t = dense_feats.T
-    inputs = embed(sources, hot, ids, answer, feats_t, dense_w, dense_b.reshape(DPROJ, 1))
-    task_at = lax.broadcasted_iota(jnp.int32, (TASKS, TASKS * THID), 1) // THID
-    task_row = lax.broadcasted_iota(jnp.int32, (TASKS, TASKS * THID), 0)
-    w2_bd = jnp.where(task_at == task_row, tower_w2.reshape(1, -1), 0.0)
-    incoming, experts, small, grad_dense = model(
+    inputs = embed(sources, hot, ids, answer, feats_t, dense_w, dense_b.reshape(1, DPROJ))
+    incoming, share, grad_dense = model(
         inputs,
         labels.T,
         feats_t,
         dense_w,
-        weights,
-        b_out.reshape(EXPERTS, 1, EOUT),
+        w_in_all,
+        w_out_all,
+        b_in_all,
+        b_out,
         gate_w.transpose(0, 2, 1).reshape(TASKS * EXPERTS, DIN),
-        gate_b.reshape(TASKS * EXPERTS, 1),
+        gate_b,
         tower_w1.transpose(0, 2, 1),
-        tower_b1.reshape(1, TASKS * THID),
-        w2_bd,
-        tower_b2.reshape(TASKS, 1),
+        tower_b1,
+        tower_w2,
+        tower_b2,
         sources,
         hot_sources.reshape(-1),
         hot_at,
     )
+    shares = lax.all_to_all(share, "dp", split_axis=0, concat_axis=0, tiled=True)
     grad_tables = scatter_add(asked, incoming).transpose(0, 2, 1)
     (
         grad_w_in,
@@ -1119,7 +1281,7 @@
         grad_b2,
         grad_gate_b,
         grad_b_in,
-    ) = unpack(experts, small)
+    ) = unpack(shares)
     return (
         grad_tables,
         grad_dense_w,

time: 222 us -> 209 us (0.941)
  Pallas kernels: 190 us -> 175 us
  starting transfers between devices: 0.04 us -> 6.55 us
    pallas_call x1, Pallas kernels: 76 us -> 62.6 us  [model(): pl.pallas_call(model_kernel, grid=(3,), in_specs=[VM] * (len(operands) -...]
    all_to_all x0 -> x1, starting transfers between devices: none -> 6.51 us  [body(): lax.all_to_all(share, 'dp', split_axis=0, concat_axis=0, tiled=True)]
  transfers between devices with their start and end apart: 1 -> 2, of which waited for: 0 -> 0; matrix products, arithmetic and copies ran while one was open for 5% -> 4% of each run, Pallas kernels for 33% -> 53%
where the time goes in v5:
time: 209 us; the launch traced here: 208 us
  Pallas kernels  175 us (84%)
  between operations  14.3 us (7%)
  other arithmetic  8.33 us (4%)
  starting transfers between devices  6.55 us (3%)
  local copies, waits for them, and re-layouts  3.88 us (2%)
    pallas_call x1, Pallas kernels, model(): pl.pallas_call(model_kernel, grid=(3,), in_specs=[VM] * (len(operands) -...  62.6 us
    pallas_call x1, Pallas kernels, look_up(): pl.pallas_call(look_up_kernel, in_specs=[VM] + [pl.BlockSpec(memory_space...  47.7 us
    pallas_call x1, Pallas kernels, scatter_add(): pl.pallas_call(scatter_kernel, in_specs=[VM, VM], out_specs=VM, out_shape...  39.8 us
    pallas_call x1, Pallas kernels, embed(): pl.pallas_call(embed_kernel, in_specs=[SM, SM, VM, VM, VM, VM, VM], out_s...  19.6 us
    sort x1, other arithmetic, body(): lax.sort((key.reshape(-1), load.reshape(-1)), num_keys=1, is_stable=False)  7.4 us
    all_to_all x1, starting transfers between devices, body(): lax.all_to_all(share, 'dp', split_axis=0, concat_axis=0, tiled=True)  6.51 us
  transfers between devices with their start and end apart: 2, of which 0 were waited for; matrix products, arithmetic and copies ran while one was open for 4% of the time, Pallas kernels for 53%

profile of v5, /device:TPU:1, one launch (start us, length us, event | category | flops | bytes accessed | tf_op | source)
XLA Modules:
  0.0 208.4 jit_solution(8352310227017066658)
XLA Ops:
  7.2 0.0 copy-start.1
  7.2 0.0 copy-start.3
  7.2 0.0 copy-start.14
  7.2 0.0 copy-start.7
  7.2 0.0 copy-start.6
  7.2 0.0 copy-start.5
  7.2 0.0 copy-start.8
  7.3 0.0 copy-start.9
  7.3 0.0 copy-start.11
  7.3 0.0 all-gather.3.cloned.1.call-start
  7.4 0.7 all-gather.3.cloned.1.call-update
  8.1 0.9 and_or_fusion
  9.0 7.4 %sort.15 = (s32[13312]{0:T(1024)S(1)}, s32[13312]{0:T(1024)S(1)}) sort(s32[13312]{0:T(1024)S(1)} %reshape.61, s32[13312]{0:T(1024)S(1)} %reshape.62), dimensions={0}, to_apply=%region_0.0 | sort | flops 186368 | bytes 212992 | tf_op jit(solution)/shard_map/sort | solution.py:1242
  16.4 3.6 %route.1 = (s32[128,2,128]{2,1,0:T(2,128)S(1)}, s32[256,128]{1,0:T(8,128)S(1)}, s32[64,128]{1,0:T(8,128)S(1)}, s32[32]{0:T(128)S(1)}, s32[128]{0:T(128)S(1)}) custom-call(s32[104,128]{1,0:T(8,128)S(1)} %bitcast.32, s32[104,128]{1,0:T(8,128)S(1)} %bitcast.33), custom_call_target="tpu_custom_call" | custom-call | tf_op jit(solution)/shard_map/route/pallas_call | solution.py:203
  20.0 0.0 copy-start.4
  20.0 0.9 copy-done.4
  20.9 0.7 copy-done.10
  21.6 47.7 %look_up.1 = (bf16[4096,128]{1,0:T(8,128)(2,1)S(1)}, s32[128,2,128]{2,1,0:T(2,128)S(1)}, bf16[4,8,64,128]{3,2,1,0:T(8,128)(2,1)S(1)}, f32[4,8,128]{2,1,0:T(8,128)S(1)}) custom-call(s32[128,2,128]{2,1,0:T(2,128)S(1)} %get-tuple-element.42.wanted_ref, f32[26,16,4096]{2,1,0:T(8,128)} %bitcast.39, bf16[8,64,128]{2,1,0:T(8,128)(2,1)S(1)} %copy-done.4, ...), custom_call_target="tpu_custom_call" | custom-call | tf_op jit(solution)/shard_map/look_up/pallas_call | solution.py:408
  69.3 0.0 copy-start.2
  69.3 0.6 copy-done.2
  70.0 0.0 copy-done.1
  70.0 0.0 copy-done.14
  70.0 19.6 %embed.1.x_ref = bf16[512,512]{1,0:T(8,128)(2,1)S(1)} custom-call(s32[32768]{0:T(1024)S(1)} %bitcast.26, s32[32]{0:T(128)S(1)} %get-tuple-element.45.hot_ref, s32[26,512]{1,0:T(8,128)S(1)} %bitcast.28, bf16[4096,128]{1,0:T(8,128)(2,1)S(1)} %get-tuple-element.46.answer_ref, f32[13,512]{1,0:T(8,128)S(1)} %bitcast.29, f32[13,96]{1,0:T(8,128)S(1)} %copy-done.7, ...), custom_call_target="tpu_custom_call" | custom-call | tf_op jit(solution)/shard_map/embed/pallas_call | solution.py:485
  89.6 0.0 all-gather.3.cloned.1.call-done
  89.7 62.6 %model.1 = (bf16[4096,128]{1,0:T(8,128)(2,1)S(1)}, bf16[32,96,128]{2,1,0:T(8,128)(2,1)}, f32[13,512]{1,0:T(8,128)S(1)}) custom-call(bf16[512,512]{1,0:T(8,128)(2,1)S(1)} %embed.1.x_ref, s32[2,512]{1,0:T(2,128)S(1)} %bitcast.37, f32[13,512]{1,0:T(8,128)S(1)} %bitcast.30, f32[13,96]{1,0:T(8,128)S(1)} %copy-done.7, bf16[4,8,64,512]{3,2,1,0:T(8,128)(2,1)} %bitcast.41, ...), custom_call_target="tpu_custom_call" | custom-call | tf_op jit(solution)/shard_map/model/pallas_call | solution.py:1023
  152.4 0.0 copy-start
  152.4 1.0 copy-done
  153.3 6.5 %all-to-all-start = ((bf16[32,96,128]{2,1,0:T(8,128)(2,1)}), bf16[32,96,128]{2,1,0:T(8,128)(2,1)S(1)}, u32[]{:S(2)}, u32[]{:S(2)}) async-start(bf16[32,96,128]{2,1,0:T(8,128)(2,1)} %get-tuple-element.52), calls=%async_computation | async-start | bytes 1572864 | tf_op jit(solution)/shard_map/all_to_all | solution.py:1269
  159.9 39.8 %scatter_add.1 = f32[26,16,4096]{2,1,0:T(8,128)} custom-call(s32[128,2,128]{2,1,0:T(2,128)} %copy-done.2, bf16[4096,128]{1,0:T(8,128)(2,1)} %copy-done), custom_call_target="tpu_custom_call" | custom-call | tf_op jit(solution)/shard_map/scatter_add/pallas_call | solution.py:1127
  199.7 0.0 all-to-all-done.shares_ref
  199.7 1.3 unpack.1
  200.9 0.6 copy.31
  (17 shorter events, 0.0 us)
Async XLA Ops:
  7.2 62.8 %copy-start.1 = (s32[512,26]{0,1:T(8,128)S(1)}, s32[512,26]{0,1:T(8,128)}, u32[]{:S(2)}) copy-start(s32[512,26]{0,1:T(8,128)} %param.16) | copy-start | bytes 159748
  7.2 62.8 %copy-start.3 = (f32[512,13]{0,1:T(8,128)S(1)}, f32[512,13]{0,1:T(8,128)}, u32[]{:S(2)}) copy-start(f32[512,13]{0,1:T(8,128)} %param.17) | copy-start | bytes 79876
  7.2 62.8 %copy-start.14 = (f32[96]{0:T(128)S(1)}, f32[96]{0:T(128)}, u32[]{:S(2)}) copy-start(f32[96]{0:T(128)} %param.21) | copy-start | bytes 1156
  7.2 62.8 %copy-start.7 = (f32[13,96]{1,0:T(8,128)S(1)}, f32[13,96]{1,0:T(8,128)}, u32[]{:S(2)}) copy-start(f32[13,96]{1,0:T(8,128)} %dw_ref.3) | copy-start | bytes 14980
  7.2 82.4 %copy-start.6 = (f32[2,512,8]{1,2,0:T(8,128)S(1)}, f32[2,512,8]{1,2,0:T(8,128)}, u32[]{:S(2)}) copy-start(f32[2,512,8]{1,2,0:T(8,128)} %param.26) | copy-start | bytes 98308
  7.2 82.4 %copy-start.5 = (f32[2,128,64]{1,2,0:T(8,128)S(1)}, f32[2,128,64]{1,2,0:T(8,128)}, u32[]{:S(2)}) copy-start(f32[2,128,64]{1,2,0:T(8,128)} %param.28) | copy-start | bytes 196612
  7.2 82.4 %copy-start.8 = (s32[512,2]{0,1:T(2,128)S(1)}, s32[512,2]{0,1:T(2,128)}, u32[]{:S(2)}) copy-start(s32[512,2]{0,1:T(2,128)} %param.18) | copy-start | bytes 12292
  7.3 82.4 %copy-start.9 = (f32[8,128]{1,0:T(8,128)S(1)}, f32[8,128]{1,0:T(8,128)}, u32[]{:S(2)}) copy-start(f32[8,128]{1,0:T(8,128)} %b_out_ref.1) | copy-start | bytes 12292
  7.3 82.4 %copy-start.11 = (f32[2,8]{1,0:T(2,128)S(1)}, f32[2,8]{1,0:T(2,128)}, u32[]{:S(2)}) copy-start(f32[2,8]{1,0:T(2,128)} %gate_b_ref.1) | copy-start | bytes 196
  7.3 82.4 %copy-start.12 = (f32[2,64]{1,0:T(2,128)S(1)}, f32[2,64]{1,0:T(2,128)}, u32[]{:S(2)}) copy-start(f32[2,64]{1,0:T(2,128)} %b1_ref.1) | copy-start | bytes 1540
  7.3 82.4 %copy-start.13 = (f32[2,64]{1,0:T(2,128)S(1)}, f32[2,64]{1,0:T(2,128)}, u32[]{:S(2)}) copy-start(f32[2,64]{1,0:T(2,128)} %w2_ref.1) | copy-start | bytes 1540
  7.3 82.4 %copy-start.15 = (f32[2]{0:T(128)S(1)}, f32[2]{0:T(128)}, u32[]{:S(2)}) copy-start(f32[2]{0:T(128)} %b2_ref.1) | copy-start | bytes 28
  7.3 82.3 %all-gather.3.cloned.1.call-start = ((), (), s32[]{:S(2)}) async-start(), calls=%async_computation.1 | async-start | bytes 2621440 | tf_op jit(solution)/shard_map/all_gather | solution.py:1234
  20.0 0.9 copy-start.4
  20.9 0.7 copy-start.10
  69.3 0.7 copy-start.2
  152.4 1.0 copy-start
  153.3 46.3 %all-to-all-start = ((bf16[32,96,128]{2,1,0:T(8,128)(2,1)}), bf16[32,96,128]{2,1,0:T(8,128)(2,1)S(1)}, u32[]{:S(2)}, u32[]{:S(2)}) async-start(bf16[32,96,128]{2,1,0:T(8,128)(2,1)} %get-tuple-element.52), calls=%async_computation | async-start | bytes 1572864 | tf_op jit(solution)/shard_map/all_to_all | solution.py:1269
Sparse Core Ops, SparseCore 0:
  9.8 44.3 all-gather.2

commit v6 on v5

--- a/solution.py
+++ b/solution.py
@@ -548,8 +548,7 @@
     outs,
     probs,
     d_raw,
-    prod_hi,
-    prod_lo,
+    products,
     mix,
     stage,
     own_grad,
@@ -616,15 +615,21 @@
         gates = jnp.exp(logits - jnp.max(logits, axis=1, keepdims=True))
         gates = gates / jnp.sum(gates, axis=1, keepdims=True)
         gates_t = gates.reshape(TASKS * EXPERTS, ROWS_LOC)
-        gate_stack = jnp.concatenate(split3(gates_t), axis=0)
-        row_at = lax.broadcasted_iota(jnp.int32, (48, 128), 0) % 16
-
-        def spread(k, carry):
-            ones = (row_at == k).astype(F32).astype(BF16)
-            probs[k] = dot_tn(gate_stack, ones)
+        gate_parts = [part.astype(F32) for part in split3(gates_t)]
+        gate_parts.append(jnp.zeros((80, ROWS_LOC), F32))
+        gate_columns = jnp.concatenate(gate_parts, axis=0).T.astype(BF16)
+        row_at = lax.broadcasted_iota(jnp.int32, (128, 256), 0)
+        column_at = lax.broadcasted_iota(jnp.int32, (128, 256), 1) // EOUT
+        row_at = jnp.where(row_at < 48, row_at % 16, -1)
+
+        def spread_gates(pair, carry):
+            take = (row_at == 2 * pair + column_at).astype(F32).astype(BF16)
+            both = dot_nn(gate_columns, take)
+            probs[2 * pair] = both[:, 0:EOUT]
+            probs[2 * pair + 1] = both[:, EOUT : 2 * EOUT]
             return carry
 
-        lax.fori_loop(0, TASKS * EXPERTS, spread, 0)
+        lax.fori_loop(0, TASKS * EXPERTS // 2, spread_gates, 0)
 
         for t in range(TASKS):
             def add(k, total):
@@ -670,29 +675,27 @@
             d_raw[k] = grad.astype(BF16)
             value = outs[k]
             for t, d_task in enumerate((d_one, d_two)):
-                product = value * d_task
-                high = product.astype(BF16)
                 at = pl.ds(pl.multiple_of((t * EXPERTS + k) * EOUT, EOUT), EOUT)
-                prod_hi[:, at] = high
-                prod_lo[:, at] = (product - high.astype(F32)).astype(BF16)
+                products[:, at] = (value * d_task).astype(BF16)
             return carry
 
         lax.fori_loop(0, EXPERTS, back_raw, 0)
 
         wide = TASKS * EXPERTS * EOUT
-        column_gate = lax.broadcasted_iota(jnp.int32, (16, wide), 1) // EOUT
-        own_gate = lax.broadcasted_iota(jnp.int32, (16, wide), 0)
+        own_gate = lax.broadcasted_iota(jnp.int32, (wide, 128), 0) // EOUT
+        column_gate = lax.broadcasted_iota(jnp.int32, (wide, 128), 1)
         ones = (column_gate == own_gate).astype(F32).astype(BF16)
-        stage[0:16] = dot_nt(ones, prod_hi[...])
-        stage[16:32] = dot_nt(ones, prod_lo[...])
-        d_gates = stage[0:16] + stage[16:32]
+        d_gates = dot_nn(products[...], ones).T[0:16]
         d_gates = d_gates.reshape(TASKS, EXPERTS, ROWS_LOC)
         mean = jnp.sum(d_gates * gates, axis=1, keepdims=True)
         d_logits = (gates * (d_gates - mean)).reshape(16, ROWS_LOC)
         d_parts = jnp.concatenate(split3(d_logits), axis=0)
         stage[...] = dot_nn(d_parts, x)
         grad_gate = stage[0:16] + stage[16:32] + stage[32:48]
-        d_in_ref[...] = dot_tn(d_logits, gate_w_ref[...], EXACT)
+        gate_high, gate_mid, _ = split3(gate_w_ref[...])
+        left = jnp.concatenate([d_parts[0:32], d_parts[0:16]], axis=0)
+        right = jnp.concatenate([gate_high, gate_high, gate_mid], axis=0)
+        d_in_ref[...] = dot_tn(left, right)
         small_ref[pl.ds(0, THID), :] = grad_w1[0:THID, 0:EOUT]
         small_ref[pl.ds(THID, THID), :] = grad_w1[THID : 2 * THID, EOUT : 2 * EOUT]
         for tile in range(4):
@@ -990,9 +993,8 @@
             send(step + 1)
             return carry
 
-        lax.fori_loop(0, 6, two_groups, 0)
+        lax.fori_loop(0, 8, two_groups, 0)
         add_up()
-        lax.fori_loop(6, 8, two_groups, 0)
         add_small_up()
         wait_blocks(ready, landing, sems.at[7], sems.at[8])
         rows_out_ref[...] = landing[...]
@@ -1039,7 +1041,6 @@
             pltpu.VMEM((EXPERTS, ROWS_LOC, EOUT), F32),
             pltpu.VMEM((TASKS * EXPERTS, ROWS_LOC, EOUT), F32),
             pltpu.VMEM((EXPERTS, ROWS_LOC, EOUT), BF16),
-            pltpu.VMEM((ROWS_LOC, TASKS * EXPERTS * EOUT), BF16),
             pltpu.VMEM((ROWS_LOC, TASKS * EXPERTS * EOUT), BF16),
             pltpu.VMEM((ROWS_LOC, TASKS * EOUT), F32),
             pltpu.VMEM((48, DIN), F32),

time: 209 us -> 202 us (0.967)
  Pallas kernels: 175 us -> 170 us
    pallas_call x1, Pallas kernels: 62.6 us -> 58.2 us  [model(): pl.pallas_call(model_kernel, grid=(3,), in_specs=[VM] * (len(operands) -...]
  transfers between devices with their start and end apart: 2 -> 2, of which waited for: 0 -> 0; matrix products, arithmetic and copies ran while one was open for 4% -> 4% of each run, Pallas kernels for 53% -> 55%
where the time goes in v6:
time: 202 us
  Pallas kernels  170 us (84%)
  between operations  14.3 us (7%)
  other arithmetic  8.33 us (4%)
  starting transfers between devices  4.64 us (2%)
  local copies, waits for them, and re-layouts  3.88 us (2%)
    pallas_call x1, Pallas kernels, model(): pl.pallas_call(model_kernel, grid=(3,), in_specs=[VM] * (len(operands) -...  58.2 us
    pallas_call x1, Pallas kernels, look_up(): pl.pallas_call(look_up_kernel, in_specs=[VM] + [pl.BlockSpec(memory_space...  47.7 us
    pallas_call x1, Pallas kernels, scatter_add(): pl.pallas_call(scatter_kernel, in_specs=[VM, VM], out_specs=VM, out_shape...  39.8 us
    pallas_call x1, Pallas kernels, embed(): pl.pallas_call(embed_kernel, in_specs=[SM, SM, VM, VM, VM, VM, VM], out_s...  19.6 us
    sort x1, other arithmetic, body(): lax.sort((key.reshape(-1), load.reshape(-1)), num_keys=1, is_stable=False)  7.4 us
    all_to_all x1, starting transfers between devices, body(): lax.all_to_all(share, 'dp', split_axis=0, concat_axis=0, tiled=True)  4.6 us
  transfers between devices with their start and end apart: 2, of which 0 were waited for; matrix products, arithmetic and copies ran while one was open for 4% of the time, Pallas kernels for 55%

profile of v6, /device:TPU:1, one launch (start us, length us, event | category | flops | bytes accessed | tf_op | source)
XLA Modules:
  0.0 202.1 jit_solution(2239144262745062924)
XLA Ops:
  7.2 0.0 copy-start.1
  7.2 0.0 copy-start.3
  7.2 0.0 copy-start.14
  7.2 0.0 copy-start.7
  7.2 0.0 copy-start.6
  7.2 0.0 copy-start.5
  7.2 0.0 copy-start.8
  7.3 0.0 copy-start.9
  7.3 0.0 copy-start.11
  7.3 0.0 copy-start.12
  7.3 0.0 copy-start.13
  7.3 0.0 all-gather.3.cloned.1.call-start
  7.4 0.7 all-gather.3.cloned.1.call-update
  8.1 0.9 and_or_fusion
  9.0 7.4 %sort.15 = (s32[13312]{0:T(1024)S(1)}, s32[13312]{0:T(1024)S(1)}) sort(s32[13312]{0:T(1024)S(1)} %reshape.61, s32[13312]{0:T(1024)S(1)} %reshape.62), dimensions={0}, to_apply=%region_0.0 | sort | flops 186368 | bytes 212992 | tf_op jit(solution)/shard_map/sort | solution.py:1243
  16.4 3.6 %route.1 = (s32[128,2,128]{2,1,0:T(2,128)S(1)}, s32[256,128]{1,0:T(8,128)S(1)}, s32[64,128]{1,0:T(8,128)S(1)}, s32[32]{0:T(128)S(1)}, s32[128]{0:T(128)S(1)}) custom-call(s32[104,128]{1,0:T(8,128)S(1)} %bitcast.32, s32[104,128]{1,0:T(8,128)S(1)} %bitcast.33), custom_call_target="tpu_custom_call" | custom-call | tf_op jit(solution)/shard_map/route/pallas_call | solution.py:203
  20.0 0.0 copy-start.4
  20.0 0.9 copy-done.4
  20.9 0.7 copy-done.10
  21.6 47.7 %look_up.1 = (bf16[4096,128]{1,0:T(8,128)(2,1)S(1)}, s32[128,2,128]{2,1,0:T(2,128)S(1)}, bf16[4,8,64,128]{3,2,1,0:T(8,128)(2,1)S(1)}, f32[4,8,128]{2,1,0:T(8,128)S(1)}) custom-call(s32[128,2,128]{2,1,0:T(2,128)S(1)} %get-tuple-element.42.wanted_ref, f32[26,16,4096]{2,1,0:T(8,128)} %bitcast.39, bf16[8,64,128]{2,1,0:T(8,128)(2,1)S(1)} %copy-done.4, ...), custom_call_target="tpu_custom_call" | custom-call | tf_op jit(solution)/shard_map/look_up/pallas_call | solution.py:408
  69.3 0.0 copy-start.2
  69.3 0.6 copy-done.2
  70.0 19.6 %embed.1.x_ref = bf16[512,512]{1,0:T(8,128)(2,1)S(1)} custom-call(s32[32768]{0:T(1024)S(1)} %bitcast.26, s32[32]{0:T(128)S(1)} %get-tuple-element.45.hot_ref, s32[26,512]{1,0:T(8,128)S(1)} %bitcast.28, bf16[4096,128]{1,0:T(8,128)(2,1)S(1)} %get-tuple-element.46.answer_ref, f32[13,512]{1,0:T(8,128)S(1)} %bitcast.29, f32[13,96]{1,0:T(8,128)S(1)} %copy-done.7, ...), custom_call_target="tpu_custom_call" | custom-call | tf_op jit(solution)/shard_map/embed/pallas_call | solution.py:485
  89.6 0.0 all-gather.3.cloned.1.call-done
  89.7 58.2 %model.1 = (bf16[4096,128]{1,0:T(8,128)(2,1)S(1)}, bf16[32,96,128]{2,1,0:T(8,128)(2,1)}, f32[13,512]{1,0:T(8,128)S(1)}) custom-call(bf16[512,512]{1,0:T(8,128)(2,1)S(1)} %embed.1.x_ref, s32[2,512]{1,0:T(2,128)S(1)} %bitcast.37, f32[13,512]{1,0:T(8,128)S(1)} %bitcast.30, f32[13,96]{1,0:T(8,128)S(1)} %copy-done.7, bf16[4,8,64,512]{3,2,1,0:T(8,128)(2,1)} %bitcast.41, ...), custom_call_target="tpu_custom_call" | custom-call | tf_op jit(solution)/shard_map/model/pallas_call | solution.py:1025
  147.9 0.0 copy-start
  148.0 1.0 copy-done
  148.9 4.6 %all-to-all-start = ((bf16[32,96,128]{2,1,0:T(8,128)(2,1)}), bf16[32,96,128]{2,1,0:T(8,128)(2,1)S(1)}, u32[]{:S(2)}, u32[]{:S(2)}) async-start(bf16[32,96,128]{2,1,0:T(8,128)(2,1)} %get-tuple-element.52), calls=%async_computation | async-start | bytes 1572864 | tf_op jit(solution)/shard_map/all_to_all | solution.py:1270
  153.5 39.8 %scatter_add.1 = f32[26,16,4096]{2,1,0:T(8,128)} custom-call(s32[128,2,128]{2,1,0:T(2,128)} %copy-done.2, bf16[4096,128]{1,0:T(8,128)(2,1)} %copy-done), custom_call_target="tpu_custom_call" | custom-call | tf_op jit(solution)/shard_map/scatter_add/pallas_call | solution.py:1128
  193.3 0.0 all-to-all-done.shares_ref
  193.3 1.3 unpack.1
  194.6 0.6 copy.31
  (17 shorter events, 0.0 us)
Async XLA Ops:
  7.2 62.8 %copy-start.1 = (s32[512,26]{0,1:T(8,128)S(1)}, s32[512,26]{0,1:T(8,128)}, u32[]{:S(2)}) copy-start(s32[512,26]{0,1:T(8,128)} %param.16) | copy-start | bytes 159748
  7.2 62.8 %copy-start.3 = (f32[512,13]{0,1:T(8,128)S(1)}, f32[512,13]{0,1:T(8,128)}, u32[]{:S(2)}) copy-start(f32[512,13]{0,1:T(8,128)} %param.17) | copy-start | bytes 79876
  7.2 62.8 %copy-start.14 = (f32[96]{0:T(128)S(1)}, f32[96]{0:T(128)}, u32[]{:S(2)}) copy-start(f32[96]{0:T(128)} %param.21) | copy-start | bytes 1156
  7.2 62.8 %copy-start.7 = (f32[13,96]{1,0:T(8,128)S(1)}, f32[13,96]{1,0:T(8,128)}, u32[]{:S(2)}) copy-start(f32[13,96]{1,0:T(8,128)} %dw_ref.3) | copy-start | bytes 14980
  7.2 82.4 %copy-start.6 = (f32[2,512,8]{1,2,0:T(8,128)S(1)}, f32[2,512,8]{1,2,0:T(8,128)}, u32[]{:S(2)}) copy-start(f32[2,512,8]{1,2,0:T(8,128)} %param.26) | copy-start | bytes 98308
  7.2 82.4 %copy-start.5 = (f32[2,128,64]{1,2,0:T(8,128)S(1)}, f32[2,128,64]{1,2,0:T(8,128)}, u32[]{:S(2)}) copy-start(f32[2,128,64]{1,2,0:T(8,128)} %param.28) | copy-start | bytes 196612
  7.2 82.4 %copy-start.8 = (s32[512,2]{0,1:T(2,128)S(1)}, s32[512,2]{0,1:T(2,128)}, u32[]{:S(2)}) copy-start(s32[512,2]{0,1:T(2,128)} %param.18) | copy-start | bytes 12292
  7.3 82.4 %copy-start.9 = (f32[8,128]{1,0:T(8,128)S(1)}, f32[8,128]{1,0:T(8,128)}, u32[]{:S(2)}) copy-start(f32[8,128]{1,0:T(8,128)} %b_out_ref.1) | copy-start | bytes 12292
  7.3 82.4 %copy-start.11 = (f32[2,8]{1,0:T(2,128)S(1)}, f32[2,8]{1,0:T(2,128)}, u32[]{:S(2)}) copy-start(f32[2,8]{1,0:T(2,128)} %gate_b_ref.1) | copy-start | bytes 196
  7.3 82.4 %copy-start.12 = (f32[2,64]{1,0:T(2,128)S(1)}, f32[2,64]{1,0:T(2,128)}, u32[]{:S(2)}) copy-start(f32[2,64]{1,0:T(2,128)} %b1_ref.1) | copy-start | bytes 1540
  7.3 82.4 %copy-start.13 = (f32[2,64]{1,0:T(2,128)S(1)}, f32[2,64]{1,0:T(2,128)}, u32[]{:S(2)}) copy-start(f32[2,64]{1,0:T(2,128)} %w2_ref.1) | copy-start | bytes 1540
  7.3 82.4 %copy-start.15 = (f32[2]{0:T(128)S(1)}, f32[2]{0:T(128)}, u32[]{:S(2)}) copy-start(f32[2]{0:T(128)} %b2_ref.1) | copy-start | bytes 28
  7.3 82.3 %all-gather.3.cloned.1.call-start = ((), (), s32[]{:S(2)}) async-start(), calls=%async_computation.1 | async-start | bytes 2621440 | tf_op jit(solution)/shard_map/all_gather | solution.py:1235
  20.0 0.9 copy-start.4
  20.9 0.7 copy-start.10
  69.3 0.7 copy-start.2
  147.9 1.0 copy-start
  148.9 44.4 %all-to-all-start = ((bf16[32,96,128]{2,1,0:T(8,128)(2,1)}), bf16[32,96,128]{2,1,0:T(8,128)(2,1)S(1)}, u32[]{:S(2)}, u32[]{:S(2)}) async-start(bf16[32,96,128]{2,1,0:T(8,128)(2,1)} %get-tuple-element.52), calls=%async_computation | async-start | bytes 1572864 | tf_op jit(solution)/shard_map/all_to_all | solution.py:1270
Sparse Core Ops, SparseCore 0:
  9.8 44.3 all-gather.2

commit v7 on v6

--- a/solution.py
+++ b/solution.py
@@ -20,6 +20,7 @@
 LOOKUPS = ROWS_LOC * FIELDS
 PACKED = FIELDS * ROWS_DEV // 8
 CAP = 208
+NEAR = 90
 COLD = 96
 HOT = 16
 SLOTS = 256
@@ -42,6 +43,7 @@
 
 VM = pl.BlockSpec(memory_space=pltpu.VMEM)
 SM = pl.BlockSpec(memory_space=pltpu.SMEM)
+ANY = pl.BlockSpec(memory_space=pl.ANY)
 
 
 def params(mib):
@@ -433,8 +435,22 @@
 
 
 def embed_kernel(
-    src_ref, hot_ref, ids_ref, answer_ref, feats_ref, dw_ref, db_ref, out_ref, slots, rows, x_t
+    source_ref,
+    hot_ref,
+    ids_ref,
+    answer_ref,
+    feats_ref,
+    dw_ref,
+    db_ref,
+    out_ref,
+    slots,
+    rows,
+    x_t,
+    src_ref,
+    sem,
 ):
+    copy = pltpu.make_async_copy(source_ref, src_ref, sem)
+    copy.start()
     for block in range(32):
         owner, half = block // 2 * 8, block % 2
         parts = [
@@ -442,10 +458,12 @@
         ]
         slots[pl.ds(block * 128, 128), :] = jnp.concatenate(parts, axis=0).astype(F32).T
 
+    copy.wait()
+
     def cold(step, carry):
-        base = step // 6 * SLOTS + step % 6 * 16
-        source = step // 6 * (8 * SLOTS) + step % 6 * 16
-        for n in range(16):
+        base = step // 6 * SLOTS + step % 6 * (NEAR // 6)
+        source = step // 6 * (8 * SLOTS) + step % 6 * (NEAR // 6)
+        for n in range(NEAR // 6):
             row = slots[pl.ds(base + n, 1), :]
             for u in range(8):
                 rows[pl.ds(src_ref[source + u * SLOTS + n], 1), :] = row
@@ -454,7 +472,7 @@
     def hot(at, carry):
         owner = hot_ref[at]
         base = (owner >> 3) * SLOTS
-        for n in range(COLD, CAP):
+        for n in range(NEAR, CAP):
             rows[pl.ds(src_ref[owner * SLOTS + n], 1), :] = slots[pl.ds(base + n, 1), :]
         return carry
 
@@ -484,13 +502,15 @@
 def embed(src, hot, ids, answer, feats_t, dense_w, dense_b):
     return pl.pallas_call(
         embed_kernel,
-        in_specs=[SM, SM, VM, VM, VM, VM, VM],
+        in_specs=[ANY, SM, VM, VM, VM, VM, VM],
         out_specs=VM,
         out_shape=shape((ROWS_LOC, DIN), BF16),
         scratch_shapes=[
             pltpu.VMEM((OWNERS * GROUPS, 128), F32),
             pltpu.VMEM((LOOKUPS + 8, 128), F32),
             pltpu.VMEM((DIN, ROWS_LOC), F32),
+            pltpu.SMEM((OWNERS * SLOTS,), jnp.int32),
+            pltpu.SemaphoreType.DMA,
         ],
         compiler_params=params(16),
         name="embed",
@@ -524,8 +544,8 @@
     labels_ref,
     feats_ref,
     dw_ref,
-    w_in_ref,
-    w_out_ref,
+    w_in_hbm,
+    w_out_hbm,
     b_in_ref,
     b_out_ref,
     gate_w_ref,
@@ -534,9 +554,9 @@
     b1_ref,
     w2_ref,
     b2_ref,
-    src_ref,
-    hot_src_ref,
     hot_at_ref,
+    src_hbm,
+    hot_src_hbm,
     rows_out_ref,
     share_out_ref,
     grad_dense_ref,
@@ -567,6 +587,11 @@
     odd,
     ready,
     landing,
+    w_in_ref,
+    w_out_ref,
+    src_ref,
+    hot_src_ref,
+    load_sems,
     pair_sems,
     first_sems,
     sems,
@@ -580,6 +605,16 @@
     me = my_index()
     at_y, at_x = line // 8, line // 2 % 4
 
+    def load_w_in(k):
+        return pltpu.make_async_copy(w_in_hbm.at[:, k], w_in_ref.at[:, k], load_sems.at[k])
+
+    loads = [
+        pltpu.make_async_copy(source, target, load_sems.at[EXPERTS + at])
+        for at, (source, target) in enumerate(
+            ((w_out_hbm, w_out_ref), (src_hbm, src_ref), (hot_src_hbm, hot_src_ref))
+        )
+    ]
+
     def weights_in(k):
         return jnp.concatenate(
             [w_in_ref[p, k] for p in range(4)], axis=0
@@ -591,6 +626,7 @@
         )
 
     def forward(k, carry):
+        load_w_in(k).wait()
         bias = [b_in_ref[p, pl.ds(k, 1), :][:, 0:PART] for p in range(4)]
         pre = dot_nt(x, weights_in(k)) + jnp.concatenate(bias, axis=1)
         act, grad = gelu_both(pre)
@@ -1004,7 +1040,12 @@
 
     @pl.when(phase == 0)
     def _():
+        for k in range(EXPERTS):
+            load_w_in(k).start()
+        for load in loads:
+            load.start()
         greet_all(me)
+        loads[0].wait()
         lax.fori_loop(0, EXPERTS, forward, 0)
 
     @pl.when(phase == 1)
@@ -1015,6 +1056,8 @@
     def _():
         pl.semaphore_wait(pltpu.get_barrier_semaphore(), OWNERS - 1)
         lax.fori_loop(0, 4, experts, 0)
+        for load in loads[1:]:
+            load.wait()
         first_round(3)
         tail()
         small_pair().start()
@@ -1025,7 +1068,7 @@
     return pl.pallas_call(
         model_kernel,
         grid=(3,),
-        in_specs=[VM] * (len(operands) - 4) + [SM] * 4,
+        in_specs=[VM] * 4 + [ANY] * 2 + [VM] * 7 + [SM] * 2 + [ANY] * 2,
         out_specs=[VM] * 3,
         out_shape=[
             shape((OWNERS * GROUPS, 128), BF16),
@@ -1060,6 +1103,11 @@
             pltpu.VMEM((SLOTS, 128), F32),
             pltpu.VMEM((OWNERS * GROUPS, 128), BF16),
             pltpu.VMEM((OWNERS * GROUPS, 128), BF16),
+            pltpu.VMEM((4, EXPERTS, PART, DIN), BF16),
+            pltpu.VMEM((4, EXPERTS, PART, EOUT), BF16),
+            pltpu.SMEM((OWNERS * SLOTS,), jnp.int32),
+            pltpu.SMEM((2 * HOT * SLOTS,), jnp.int32),
+            pltpu.SemaphoreType.DMA((EXPERTS + 3,)),
             pltpu.SemaphoreType.DMA((4,)),
             pltpu.SemaphoreType.DMA((4,)),
             pltpu.SemaphoreType.DMA((12,)),
@@ -1070,8 +1118,26 @@
 
 
 def scatter_kernel(
-    asked_ref, grads_ref, out_ref, rows_v, groups, rows, sem, even, odd, *sums
+    asked_hbm,
+    grads_hbm,
+    out_hbm,
+    rows_v,
+    groups,
+    rows,
+    sem,
+    even,
+    odd,
+    asked_ref,
+    grads_ref,
+    out_ref,
+    out_sem,
+    *sums,
 ):
+    asked_copy = pltpu.make_async_copy(asked_hbm, asked_ref, sem.at[1])
+    asked_copy.start()
+    grads_copy = pltpu.make_async_copy(grads_hbm, grads_ref, sem.at[2])
+    grads_copy.start()
+    asked_copy.wait()
     split_wanted(asked_ref, rows_v, groups)
     rows_copy = pltpu.make_async_copy(rows_v, rows, sem.at[0])
     rows_copy.start()
@@ -1083,6 +1149,7 @@
         return carry
 
     lax.fori_loop(0, PACKED // 512, clear, 0)
+    grads_copy.wait()
     rows_copy.wait()
 
     def place(source, found):
@@ -1119,19 +1186,27 @@
             block = block.T
             for k in range(8):
                 out_ref[field, :, pl.ds(part * 1024 + k * 128, 128)] = block[16 * k : 16 * k + 16]
+        pltpu.make_async_copy(out_ref.at[field], out_hbm.at[field], out_sem).start()
         return carry
 
     lax.fori_loop(0, FIELDS, write, 0)
+    pltpu.make_async_copy(out_ref, out_hbm, out_sem).wait()
 
 
 def scatter_add(asked, grads):
     return pl.pallas_call(
         scatter_kernel,
-        in_specs=[VM, VM],
-        out_specs=VM,
+        in_specs=[ANY, ANY],
+        out_specs=ANY,
         out_shape=shape((FIELDS, EMB, ROWS_DEV), F32),
         scratch_shapes=split_scratch()
         + [pltpu.VMEM((SLOTS, 128), F32)] * 2
+        + [
+            pltpu.VMEM((OWNERS, 2, 128), jnp.int32),
+            pltpu.VMEM((OWNERS * GROUPS, 128), BF16),
+            pltpu.VMEM((FIELDS, EMB, ROWS_DEV), F32),
+            pltpu.SemaphoreType.DMA,
+        ]
         + [pltpu.VMEM((PACKED + 8, 128), F32)] * SUMS,
         compiler_params=params(58),
         name="scatter_add",
@@ -1263,9 +1338,9 @@
         tower_b1,
         tower_w2,
         tower_b2,
+        hot_at,
         sources,
         hot_sources.reshape(-1),
-        hot_at,
     )
     shares = lax.all_to_all(share, "dp", split_axis=0, concat_axis=0, tiled=True)
     grad_tables = scatter_add(asked, incoming).transpose(0, 2, 1)

time: 202 us -> 197 us (0.975)
  Pallas kernels: 170 us -> 164 us
    pallas_call x3, Pallas kernels: 118 us -> 112 us  [the longest x1 55.3 us: model(): pl.pallas_call(model_kernel, grid=(3,), in_specs=[VM] * 4 + [ANY] * 2 + [...]
where the time goes in v7:
time: 197 us; the launch traced here: 196 us
  Pallas kernels  164 us (83%)
  between operations  14.3 us (7%)
  other arithmetic  8.33 us (4%)
  starting transfers between devices  4.64 us (2%)
  local copies, waits for them, and re-layouts  3.88 us (2%)
    pallas_call x1, Pallas kernels, model(): pl.pallas_call(model_kernel, grid=(3,), in_specs=[VM] * 4 + [ANY] * 2 + [...  55.3 us
    pallas_call x1, Pallas kernels, look_up(): pl.pallas_call(look_up_kernel, in_specs=[VM] + [pl.BlockSpec(memory_space...  47.7 us
    pallas_call x1, Pallas kernels, scatter_add(): pl.pallas_call(scatter_kernel, in_specs=[ANY, ANY], out_specs=ANY, out_sh...  37.2 us
    pallas_call x1, Pallas kernels, embed(): pl.pallas_call(embed_kernel, in_specs=[ANY, SM, VM, VM, VM, VM, VM], out_...  19.3 us
    sort x1, other arithmetic, body(): lax.sort((key.reshape(-1), load.reshape(-1)), num_keys=1, is_stable=False)  7.4 us
    all_to_all x1, starting transfers between devices, body(): lax.all_to_all(share, 'dp', split_axis=0, concat_axis=0, tiled=True)  4.6 us
  transfers between devices with their start and end apart: 2, of which 0 were waited for; matrix products, arithmetic and copies ran while one was open for 4% of the time, Pallas kernels for 55%

profile of v7, /device:TPU:1, one launch (start us, length us, event | category | flops | bytes accessed | tf_op | source)
XLA Modules:
  0.0 196.2 jit_solution(17263436777653731140)
XLA Ops:
  7.2 0.0 copy-start.1
  7.2 0.0 copy-start.3
  7.2 0.0 copy-start.14
  7.2 0.0 copy-start.7
  7.2 0.0 copy-start.6
  7.2 0.0 copy-start.5
  7.2 0.0 copy-start.8
  7.3 0.0 copy-start.9
  7.3 0.0 copy-start.11
  7.3 0.0 all-gather.3.cloned.1.call-start
  7.4 0.7 all-gather.3.cloned.1.call-update
  8.1 0.9 and_or_fusion
  9.0 7.4 %sort.15 = (s32[13312]{0:T(1024)S(1)}, s32[13312]{0:T(1024)S(1)}) sort(s32[13312]{0:T(1024)S(1)} %reshape.61, s32[13312]{0:T(1024)S(1)} %reshape.62), dimensions={0}, to_apply=%region_0.0 | sort | flops 186368 | bytes 212992 | tf_op jit(solution)/shard_map/sort | solution.py:1318
  16.4 3.6 %route.1 = (s32[128,2,128]{2,1,0:T(2,128)S(1)}, s32[256,128]{1,0:T(8,128)S(1)}, s32[64,128]{1,0:T(8,128)S(1)}, s32[32]{0:T(128)S(1)}, s32[128]{0:T(128)S(1)}) custom-call(s32[104,128]{1,0:T(8,128)S(1)} %bitcast.32, s32[104,128]{1,0:T(8,128)S(1)} %bitcast.33), custom_call_target="tpu_custom_call" | custom-call | tf_op jit(solution)/shard_map/route/pallas_call | solution.py:205
  20.0 0.0 copy-start.4
  20.0 0.9 copy-done.4
  20.9 0.7 copy-done.10
  21.6 47.7 %look_up.1 = (bf16[4096,128]{1,0:T(8,128)(2,1)S(1)}, s32[128,2,128]{2,1,0:T(2,128)S(1)}, bf16[4,8,64,128]{3,2,1,0:T(8,128)(2,1)S(1)}, f32[4,8,128]{2,1,0:T(8,128)S(1)}) custom-call(s32[128,2,128]{2,1,0:T(2,128)S(1)} %get-tuple-element.42.wanted_ref, f32[26,16,4096]{2,1,0:T(8,128)} %bitcast.39, bf16[8,64,128]{2,1,0:T(8,128)(2,1)S(1)} %copy-done.4, ...), custom_call_target="tpu_custom_call" | custom-call | tf_op jit(solution)/shard_map/look_up/pallas_call | solution.py:410
  69.3 0.0 copy-start.2
  69.3 0.6 copy-done.2
  70.0 0.0 copy-done.3
  70.0 0.0 copy-done.7
  70.0 19.3 %embed.1.x_ref = bf16[512,512]{1,0:T(8,128)(2,1)S(1)} custom-call(s32[32768]{0:T(1024)S(1)} %bitcast.26, s32[32]{0:T(128)S(1)} %get-tuple-element.45.hot_ref, s32[26,512]{1,0:T(8,128)S(1)} %bitcast.28, bf16[4096,128]{1,0:T(8,128)(2,1)S(1)} %get-tuple-element.46.answer_ref, f32[13,512]{1,0:T(8,128)S(1)} %bitcast.29, f32[13,96]{1,0:T(8,128)S(1)} %copy-done.7, ...), custom_call_target="tpu_custom_call" | custom-call | tf_op jit(solution)/shard_map/embed/pallas_call | solution.py:503
  89.3 0.0 all-gather.3.cloned.1.call-done
  89.4 55.3 %model.1 = (bf16[4096,128]{1,0:T(8,128)(2,1)S(1)}, bf16[32,96,128]{2,1,0:T(8,128)(2,1)}, f32[13,512]{1,0:T(8,128)S(1)}) custom-call(bf16[512,512]{1,0:T(8,128)(2,1)S(1)} %embed.1.x_ref, s32[2,512]{1,0:T(2,128)S(1)} %bitcast.37, f32[13,512]{1,0:T(8,128)S(1)} %bitcast.30, f32[13,96]{1,0:T(8,128)S(1)} %copy-done.7, bf16[4,8,64,512]{3,2,1,0:T(8,128)(2,1)} %bitcast.41, ...), custom_call_target="tpu_custom_call" | custom-call | tf_op jit(solution)/shard_map/model/pallas_call | solution.py:1068
  144.7 0.0 copy-start
  144.7 1.0 copy-done
  145.7 4.6 %all-to-all-start = ((bf16[32,96,128]{2,1,0:T(8,128)(2,1)}), bf16[32,96,128]{2,1,0:T(8,128)(2,1)S(1)}, u32[]{:S(2)}, u32[]{:S(2)}) async-start(bf16[32,96,128]{2,1,0:T(8,128)(2,1)} %get-tuple-element.52), calls=%async_computation | async-start | bytes 1572864 | tf_op jit(solution)/shard_map/all_to_all | solution.py:1345
  150.3 37.2 %scatter_add.1 = f32[26,16,4096]{2,1,0:T(8,128)} custom-call(s32[128,2,128]{2,1,0:T(2,128)} %copy-done.2, bf16[4096,128]{1,0:T(8,128)(2,1)} %copy-done), custom_call_target="tpu_custom_call" | custom-call | tf_op jit(solution)/shard_map/scatter_add/pallas_call | solution.py:1197
  187.5 0.0 all-to-all-done.shares_ref
  187.5 1.3 unpack.1
  188.8 0.6 copy.31
  (17 shorter events, 0.0 us)
Async XLA Ops:
  7.2 62.8 %copy-start.1 = (s32[512,26]{0,1:T(8,128)S(1)}, s32[512,26]{0,1:T(8,128)}, u32[]{:S(2)}) copy-start(s32[512,26]{0,1:T(8,128)} %param.16) | copy-start | bytes 159748
  7.2 62.8 %copy-start.3 = (f32[512,13]{0,1:T(8,128)S(1)}, f32[512,13]{0,1:T(8,128)}, u32[]{:S(2)}) copy-start(f32[512,13]{0,1:T(8,128)} %param.17) | copy-start | bytes 79876
  7.2 62.8 %copy-start.14 = (f32[96]{0:T(128)S(1)}, f32[96]{0:T(128)}, u32[]{:S(2)}) copy-start(f32[96]{0:T(128)} %param.21) | copy-start | bytes 1156
  7.2 62.8 %copy-start.7 = (f32[13,96]{1,0:T(8,128)S(1)}, f32[13,96]{1,0:T(8,128)}, u32[]{:S(2)}) copy-start(f32[13,96]{1,0:T(8,128)} %dw_ref.3) | copy-start | bytes 14980
  7.2 82.1 %copy-start.6 = (f32[2,512,8]{1,2,0:T(8,128)S(1)}, f32[2,512,8]{1,2,0:T(8,128)}, u32[]{:S(2)}) copy-start(f32[2,512,8]{1,2,0:T(8,128)} %param.26) | copy-start | bytes 98308
  7.2 82.1 %copy-start.5 = (f32[2,128,64]{1,2,0:T(8,128)S(1)}, f32[2,128,64]{1,2,0:T(8,128)}, u32[]{:S(2)}) copy-start(f32[2,128,64]{1,2,0:T(8,128)} %param.28) | copy-start | bytes 196612
  7.2 82.1 %copy-start.8 = (s32[512,2]{0,1:T(2,128)S(1)}, s32[512,2]{0,1:T(2,128)}, u32[]{:S(2)}) copy-start(s32[512,2]{0,1:T(2,128)} %param.18) | copy-start | bytes 12292
  7.3 82.1 %copy-start.9 = (f32[8,128]{1,0:T(8,128)S(1)}, f32[8,128]{1,0:T(8,128)}, u32[]{:S(2)}) copy-start(f32[8,128]{1,0:T(8,128)} %b_out_ref.1) | copy-start | bytes 12292
  7.3 82.1 %copy-start.11 = (f32[2,8]{1,0:T(2,128)S(1)}, f32[2,8]{1,0:T(2,128)}, u32[]{:S(2)}) copy-start(f32[2,8]{1,0:T(2,128)} %gate_b_ref.1) | copy-start | bytes 196
  7.3 82.1 %copy-start.12 = (f32[2,64]{1,0:T(2,128)S(1)}, f32[2,64]{1,0:T(2,128)}, u32[]{:S(2)}) copy-start(f32[2,64]{1,0:T(2,128)} %b1_ref.1) | copy-start | bytes 1540
  7.3 82.1 %copy-start.13 = (f32[2,64]{1,0:T(2,128)S(1)}, f32[2,64]{1,0:T(2,128)}, u32[]{:S(2)}) copy-start(f32[2,64]{1,0:T(2,128)} %w2_ref.1) | copy-start | bytes 1540
  7.3 82.1 %copy-start.15 = (f32[2]{0:T(128)S(1)}, f32[2]{0:T(128)}, u32[]{:S(2)}) copy-start(f32[2]{0:T(128)} %b2_ref.1) | copy-start | bytes 28
  7.3 82.0 %all-gather.3.cloned.1.call-start = ((), (), s32[]{:S(2)}) async-start(), calls=%async_computation.1 | async-start | bytes 2621440 | tf_op jit(solution)/shard_map/all_gather | solution.py:1310
  20.0 0.9 copy-start.4
  20.9 0.7 copy-start.10
  69.3 0.7 copy-start.2
  144.7 1.0 copy-start
  145.7 41.8 %all-to-all-start = ((bf16[32,96,128]{2,1,0:T(8,128)(2,1)}), bf16[32,96,128]{2,1,0:T(8,128)(2,1)S(1)}, u32[]{:S(2)}, u32[]{:S(2)}) async-start(bf16[32,96,128]{2,1,0:T(8,128)(2,1)} %get-tuple-element.52), calls=%async_computation | async-start | bytes 1572864 | tf_op jit(solution)/shard_map/all_to_all | solution.py:1345
Sparse Core Ops, SparseCore 0:
  9.8 44.3 all-gather.2

commit v8 on v7

--- a/solution.py
+++ b/solution.py
@@ -962,7 +962,8 @@
         lane_to = lax.broadcasted_iota(jnp.int32, (128, 128), 1)
         for field in range(FIELDS):
             take = lane_from == EMB * (field % 8) + lane_to % EMB
-            copies = dot_nn(d_in_ref[:, pl.ds(field // 8 * 128, 128)].astype(BF16), take.astype(F32).astype(BF16))
+            block = d_in_ref[:, pl.ds(field // 8 * 128, 128)].astype(BF16)
+            copies = dot_nn(block, take.astype(F32).astype(BF16))
             rows[pl.ds(field * ROWS_LOC, ROWS_LOC), :] = copies
         rows[pl.ds(LOOKUPS, 8), :] = jnp.zeros((8, 128), F32)
         group = lane_group(1)
@@ -974,13 +975,11 @@
                 hot_rows[at, pl.ds(n - COLD, 1), :] = row
             return carry
 
-        second_round(0)
         lax.fori_loop(0, HOT, hot, 0)
-        second_round(1)
         hot_rows[HOT] = jnp.zeros((CAP - COLD, 128), F32)
 
         def group_at(step):
-            return (3 * (line // 2) + part + 4 * core + step) % 16
+            return (5 * (line // 2) + 4 * part + 8 * core + step) % 16
 
         def collect(step, slots):
             source = group_at(step) * (8 * SLOTS)
@@ -1014,10 +1013,7 @@
 
         for slots in (even, odd):
             slots[pl.ds(CAP, SLOTS - CAP), :] = jnp.zeros((SLOTS - CAP, 128), F32)
-        share_small()
-        second_round(2)
         collect(0, even)
-        second_round(3)
 
         def two_groups(pair, carry):
             step = 2 * pair
@@ -1029,7 +1025,16 @@
             send(step + 1)
             return carry
 
-        lax.fori_loop(0, 8, two_groups, 0)
+        lax.fori_loop(0, 1, two_groups, 0)
+        second_round(0)
+        second_round(1)
+        second_round(2)
+        second_round(3)
+        tail()
+        small_pair().start()
+        lax.fori_loop(1, 2, two_groups, 0)
+        share_small()
+        lax.fori_loop(2, 8, two_groups, 0)
         add_up()
         add_small_up()
         wait_blocks(ready, landing, sems.at[7], sems.at[8])
@@ -1059,8 +1064,6 @@
         for load in loads[1:]:
             load.wait()
         first_round(3)
-        tail()
-        small_pair().start()
         spread()
 
 

time: 197 us -> 195 us (0.990)
  Pallas kernels: 164 us -> 161 us
    pallas_call x1, Pallas kernels: 55.3 us -> 52.2 us  [model(): pl.pallas_call(model_kernel, grid=(3,), in_specs=[VM] * 4 + [ANY] * 2 + [...]
where the time goes in v8:
time: 195 us; the launch traced here: 194 us
  Pallas kernels  161 us (83%)
  between operations  14.3 us (7%)
  other arithmetic  8.33 us (4%)
  starting transfers between devices  5.89 us (3%)
  local copies, waits for them, and re-layouts  3.88 us (2%)
    pallas_call x1, Pallas kernels, model(): pl.pallas_call(model_kernel, grid=(3,), in_specs=[VM] * 4 + [ANY] * 2 + [...  52.2 us
    pallas_call x1, Pallas kernels, look_up(): pl.pallas_call(look_up_kernel, in_specs=[VM] + [pl.BlockSpec(memory_space...  47.7 us
    pallas_call x1, Pallas kernels, scatter_add(): pl.pallas_call(scatter_kernel, in_specs=[ANY, ANY], out_specs=ANY, out_sh...  37.1 us
    pallas_call x1, Pallas kernels, embed(): pl.pallas_call(embed_kernel, in_specs=[ANY, SM, VM, VM, VM, VM, VM], out_...  19.3 us
    sort x1, other arithmetic, body(): lax.sort((key.reshape(-1), load.reshape(-1)), num_keys=1, is_stable=False)  7.4 us
    all_to_all x1, starting transfers between devices, body(): lax.all_to_all(share, 'dp', split_axis=0, concat_axis=0, tiled=True)  5.85 us
  transfers between devices with their start and end apart: 2, of which 0 were waited for; matrix products, arithmetic and copies ran while one was open for 4% of the time, Pallas kernels for 55%

profile of v8, /device:TPU:1, one launch (start us, length us, event | category | flops | bytes accessed | tf_op | source)
XLA Modules:
  0.0 194.3 jit_solution(3674917185976867730)
XLA Ops:
  7.2 0.0 copy-start.1
  7.2 0.0 copy-start.3
  7.2 0.0 copy-start.14
  7.2 0.0 copy-start.7
  7.2 0.0 copy-start.6
  7.2 0.0 copy-start.5
  7.2 0.0 copy-start.8
  7.3 0.0 copy-start.9
  7.3 0.0 copy-start.11
  7.3 0.0 copy-start.12
  7.3 0.0 all-gather.3.cloned.1.call-start
  7.4 0.7 all-gather.3.cloned.1.call-update
  8.1 0.9 and_or_fusion
  9.0 7.4 %sort.15 = (s32[13312]{0:T(1024)S(1)}, s32[13312]{0:T(1024)S(1)}) sort(s32[13312]{0:T(1024)S(1)} %reshape.61, s32[13312]{0:T(1024)S(1)} %reshape.62), dimensions={0}, to_apply=%region_0.0 | sort | flops 186368 | bytes 212992 | tf_op jit(solution)/shard_map/sort | solution.py:1321
  16.4 3.6 %route.1 = (s32[128,2,128]{2,1,0:T(2,128)S(1)}, s32[256,128]{1,0:T(8,128)S(1)}, s32[64,128]{1,0:T(8,128)S(1)}, s32[32]{0:T(128)S(1)}, s32[128]{0:T(128)S(1)}) custom-call(s32[104,128]{1,0:T(8,128)S(1)} %bitcast.32, s32[104,128]{1,0:T(8,128)S(1)} %bitcast.33), custom_call_target="tpu_custom_call" | custom-call | tf_op jit(solution)/shard_map/route/pallas_call | solution.py:205
  20.0 0.0 copy-start.4
  20.0 0.9 copy-done.4
  20.9 0.7 copy-done.10
  21.6 47.7 %look_up.1 = (bf16[4096,128]{1,0:T(8,128)(2,1)S(1)}, s32[128,2,128]{2,1,0:T(2,128)S(1)}, bf16[4,8,64,128]{3,2,1,0:T(8,128)(2,1)S(1)}, f32[4,8,128]{2,1,0:T(8,128)S(1)}) custom-call(s32[128,2,128]{2,1,0:T(2,128)S(1)} %get-tuple-element.42.wanted_ref, f32[26,16,4096]{2,1,0:T(8,128)} %bitcast.39, bf16[8,64,128]{2,1,0:T(8,128)(2,1)S(1)} %copy-done.4, ...), custom_call_target="tpu_custom_call" | custom-call | tf_op jit(solution)/shard_map/look_up/pallas_call | solution.py:410
  69.3 0.0 copy-start.2
  69.3 0.6 copy-done.2
  70.0 0.0 copy-done.7
  70.0 19.3 %embed.1.x_ref = bf16[512,512]{1,0:T(8,128)(2,1)S(1)} custom-call(s32[32768]{0:T(1024)S(1)} %bitcast.26, s32[32]{0:T(128)S(1)} %get-tuple-element.45.hot_ref, s32[26,512]{1,0:T(8,128)S(1)} %bitcast.28, bf16[4096,128]{1,0:T(8,128)(2,1)S(1)} %get-tuple-element.46.answer_ref, f32[13,512]{1,0:T(8,128)S(1)} %bitcast.29, f32[13,96]{1,0:T(8,128)S(1)} %copy-done.7, ...), custom_call_target="tpu_custom_call" | custom-call | tf_op jit(solution)/shard_map/embed/pallas_call | solution.py:503
  89.3 0.0 all-gather.3.cloned.1.call-done
  89.4 52.2 %model.1 = (bf16[4096,128]{1,0:T(8,128)(2,1)S(1)}, bf16[32,96,128]{2,1,0:T(8,128)(2,1)}, f32[13,512]{1,0:T(8,128)S(1)}) custom-call(bf16[512,512]{1,0:T(8,128)(2,1)S(1)} %embed.1.x_ref, s32[2,512]{1,0:T(2,128)S(1)} %bitcast.37, f32[13,512]{1,0:T(8,128)S(1)} %bitcast.30, f32[13,96]{1,0:T(8,128)S(1)} %copy-done.7, bf16[4,8,64,512]{3,2,1,0:T(8,128)(2,1)} %bitcast.41, ...), custom_call_target="tpu_custom_call" | custom-call | tf_op jit(solution)/shard_map/model/pallas_call | solution.py:1071
  141.7 0.0 copy-start
  141.7 1.0 copy-done
  142.6 5.8 %all-to-all-start = ((bf16[32,96,128]{2,1,0:T(8,128)(2,1)}), bf16[32,96,128]{2,1,0:T(8,128)(2,1)S(1)}, u32[]{:S(2)}, u32[]{:S(2)}) async-start(bf16[32,96,128]{2,1,0:T(8,128)(2,1)} %get-tuple-element.52), calls=%async_computation | async-start | bytes 1572864 | tf_op jit(solution)/shard_map/all_to_all | solution.py:1348
  148.5 37.1 %scatter_add.1 = f32[26,16,4096]{2,1,0:T(8,128)} custom-call(s32[128,2,128]{2,1,0:T(2,128)} %copy-done.2, bf16[4096,128]{1,0:T(8,128)(2,1)} %copy-done), custom_call_target="tpu_custom_call" | custom-call | tf_op jit(solution)/shard_map/scatter_add/pallas_call | solution.py:1200
  185.6 0.0 all-to-all-done.shares_ref
  185.6 1.3 unpack.1
  186.9 0.6 copy.31
  (17 shorter events, 0.0 us)
Async XLA Ops:
  7.2 62.8 %copy-start.1 = (s32[512,26]{0,1:T(8,128)S(1)}, s32[512,26]{0,1:T(8,128)}, u32[]{:S(2)}) copy-start(s32[512,26]{0,1:T(8,128)} %param.16) | copy-start | bytes 159748
  7.2 62.8 %copy-start.3 = (f32[512,13]{0,1:T(8,128)S(1)}, f32[512,13]{0,1:T(8,128)}, u32[]{:S(2)}) copy-start(f32[512,13]{0,1:T(8,128)} %param.17) | copy-start | bytes 79876
  7.2 62.8 %copy-start.14 = (f32[96]{0:T(128)S(1)}, f32[96]{0:T(128)}, u32[]{:S(2)}) copy-start(f32[96]{0:T(128)} %param.21) | copy-start | bytes 1156
  7.2 62.8 %copy-start.7 = (f32[13,96]{1,0:T(8,128)S(1)}, f32[13,96]{1,0:T(8,128)}, u32[]{:S(2)}) copy-start(f32[13,96]{1,0:T(8,128)} %dw_ref.3) | copy-start | bytes 14980
  7.2 82.1 %copy-start.6 = (f32[2,512,8]{1,2,0:T(8,128)S(1)}, f32[2,512,8]{1,2,0:T(8,128)}, u32[]{:S(2)}) copy-start(f32[2,512,8]{1,2,0:T(8,128)} %param.26) | copy-start | bytes 98308
  7.2 82.1 %copy-start.5 = (f32[2,128,64]{1,2,0:T(8,128)S(1)}, f32[2,128,64]{1,2,0:T(8,128)}, u32[]{:S(2)}) copy-start(f32[2,128,64]{1,2,0:T(8,128)} %param.28) | copy-start | bytes 196612
  7.2 82.1 %copy-start.8 = (s32[512,2]{0,1:T(2,128)S(1)}, s32[512,2]{0,1:T(2,128)}, u32[]{:S(2)}) copy-start(s32[512,2]{0,1:T(2,128)} %param.18) | copy-start | bytes 12292
  7.3 82.1 %copy-start.9 = (f32[8,128]{1,0:T(8,128)S(1)}, f32[8,128]{1,0:T(8,128)}, u32[]{:S(2)}) copy-start(f32[8,128]{1,0:T(8,128)} %b_out_ref.1) | copy-start | bytes 12292
  7.3 82.1 %copy-start.11 = (f32[2,8]{1,0:T(2,128)S(1)}, f32[2,8]{1,0:T(2,128)}, u32[]{:S(2)}) copy-start(f32[2,8]{1,0:T(2,128)} %gate_b_ref.1) | copy-start | bytes 196
  7.3 82.1 %copy-start.12 = (f32[2,64]{1,0:T(2,128)S(1)}, f32[2,64]{1,0:T(2,128)}, u32[]{:S(2)}) copy-start(f32[2,64]{1,0:T(2,128)} %b1_ref.1) | copy-start | bytes 1540
  7.3 82.1 %copy-start.13 = (f32[2,64]{1,0:T(2,128)S(1)}, f32[2,64]{1,0:T(2,128)}, u32[]{:S(2)}) copy-start(f32[2,64]{1,0:T(2,128)} %w2_ref.1) | copy-start | bytes 1540
  7.3 82.1 %copy-start.15 = (f32[2]{0:T(128)S(1)}, f32[2]{0:T(128)}, u32[]{:S(2)}) copy-start(f32[2]{0:T(128)} %b2_ref.1) | copy-start | bytes 28
  7.3 82.0 %all-gather.3.cloned.1.call-start = ((), (), s32[]{:S(2)}) async-start(), calls=%async_computation.1 | async-start | bytes 2621440 | tf_op jit(solution)/shard_map/all_gather | solution.py:1313
  20.0 0.9 copy-start.4
  20.9 0.7 copy-start.10
  69.3 0.7 copy-start.2
  141.7 1.0 copy-start
  142.6 42.9 %all-to-all-start = ((bf16[32,96,128]{2,1,0:T(8,128)(2,1)}), bf16[32,96,128]{2,1,0:T(8,128)(2,1)S(1)}, u32[]{:S(2)}, u32[]{:S(2)}) async-start(bf16[32,96,128]{2,1,0:T(8,128)(2,1)} %get-tuple-element.52), calls=%async_computation | async-start | bytes 1572864 | tf_op jit(solution)/shard_map/all_to_all | solution.py:1348
Sparse Core Ops, SparseCore 0:
  9.8 44.3 all-gather.2
